TPU v7x, 256 devices: a whole 4x4x8 slice. The times are simulated.
256 devices in a mesh: dp: 128 (over z, y, x), mp: 2 (over core).
Axes of the slice: x: 4, y: 4, z: 8, core: 2. Of those that a mesh axis runs over, the one named last changes fastest.
Arguments:
- acts: bfloat16 [131072, 4096], P('dp', 'mp'), may hold values from -6 to 6
- cotangent: bfloat16 [131072, 1024], P('dp', 'mp'), may hold values from -6 to 6
- value_weight: bfloat16 [1024, 4096], P(None, 'mp'), may hold values from -0.1875 to 0.1875
- proj_in: bfloat16 [64, 4096], P(None, 'mp'), may hold values from -0.09375 to 0.09375
- proj_out: bfloat16 [64, 1024], replicated, may hold values from -0.1875 to 0.1875
- query_grads: bfloat16 [512, 4096], P('dp', 'mp'), may hold values from -0.01171875 to 0.01171875
- lengths: int32 [1024], P('dp'), may hold values from 1 to 256, as said below
- plan: int32 [16384, 2], P('dp'), may hold values from 0 to 640, as said below
- corpus: int32 [1024], P('dp'), may hold values from 0 to 1023, as said below
- segments: int32 [131072], P('dp'), may hold values from 0 to 8, as said below
Outputs:
- input_grad: bfloat16 [131072, 4096], P('dp', 'mp')
- balanced: bfloat16 [81920, 128], P('dp')
- influence: float32 [1024, 512], P('dp', 'mp')
Inputs may be any that keep to these rules, and one draw needn't show every extreme that they name: `lengths`: the documents of a device lie in number order from its first token slot; the slots after them are padding. The live tokens of each device number a multiple of 8, and every device holds one document of exactly 256 tokens. For a block of live token slots, plan[k, 0] is its balanced device and plan[k, 1] its first row there, a multiple of 8; the blocks sent to one balanced device fill its 640 rows exactly, without gaps or intersection. At most 1 block of one device go to one balanced device, and that many do. Padding blocks hold (0, 640). `corpus`: A permutation of the documents; index c is owned by device c // 8 of dp. The documents of one device all have different owners. `segments`: each slot holds the device-local number of the document that the lengths place there, or 8 on padding.
All inputs are finite; a program needn't handle non-finite values.
Results may differ from a plain program's by a relative error of at most 0.015.
Values may be sent and summed in bfloat16 or wider, within the bound.
No kernel may reach another device: no remote copies, remote signals or barrier semaphores. Data moves between devices by JAX's collectives and lax.ppermute only.
A program may use at most 64 MiB of HBM per device.

v0:
```python
import jax
import jax.numpy as jnp
from jax import lax
from jax.sharding import PartitionSpec as P

BLOCK = 8
CAP = 640


def lookup(member, table):
    return jnp.sum(jnp.where(member, table[None, :], 0), axis=1)


def pair_slots(destination):
    position = jnp.arange(destination.shape[0])
    shared = (destination[:, None] == destination[None, :]) & (
        position[:, None] > position[None, :]
    )
    return jnp.sum(shared.astype(jnp.int32), axis=1)


def spread_blocks(values):
    return jnp.broadcast_to(values[:, None], (values.shape[0], BLOCK)).reshape(-1)


def score_rows(doc_rows, query_grads):
    gathered = lax.dot_general(
        doc_rows,
        lax.all_gather(query_grads, "dp", axis=0, tiled=True),
        (((1,), (1,)), ((), ())),
        preferred_element_type=jnp.float32,
    )
    return lax.psum_scatter(gathered, "mp", scatter_dimension=1, tiled=True)


def body(
    acts, cotangent, value_weight, proj_in, proj_out, query_grads, lengths, plan, corpus, segments
):
    tok_rows = acts.shape[0]
    doc_count = lengths.shape[0]
    block_count = plan.shape[0]
    groups = lax.axis_size("dp")
    doc_pair = (doc_count + groups - 1) // groups
    block_pair = (block_count + groups - 1) // groups
    rank = proj_in.shape[0]
    contract = (((1,), (1,)), ((), ()))
    piece = lax.all_gather(cotangent, "mp", axis=1, tiled=True)
    grad_sum = jnp.dot(piece, value_weight, preferred_element_type=jnp.float32)
    out_sum = lax.dot_general(piece, proj_out, contract, preferred_element_type=jnp.float32)
    grad_sum, out_proj = (grad_sum, out_sum)
    input_grad = grad_sum.astype(jnp.bfloat16)
    in_part = lax.dot_general(acts, proj_in, contract, preferred_element_type=jnp.float32)
    in_proj = lax.psum(in_part.astype(jnp.bfloat16), "mp")
    out_low = out_proj.astype(jnp.bfloat16)
    features = jnp.concatenate([in_proj, out_low], axis=1)
    half_rank = rank // lax.axis_size("mp")
    out_half = lax.dynamic_slice_in_dim(out_low, lax.axis_index("mp") * half_rank, half_rank, 1)
    member = segments[:, None] == jnp.arange(doc_count, dtype=jnp.int32)[None, :]
    sums = jnp.einsum(
        "td,ta,tb->dab",
        member.astype(jnp.float32),
        out_half.astype(jnp.float32),
        in_proj.astype(jnp.float32),
    )
    doc_grads = sums.reshape(doc_count, half_rank * rank).astype(jnp.bfloat16)
    block_dest = plan[:, 0]
    block_first = plan[:, 1]
    block_live = block_first < CAP
    block_slot = pair_slots(jnp.where(block_live, block_dest, groups))
    starts = jnp.cumsum(lengths) - lengths
    tok_start = lookup(member, starts)
    tok_length = lookup(member, lengths)
    tok_dest = spread_blocks(block_dest)
    tok_first = spread_blocks(block_first)
    tok_slot = spread_blocks(block_slot)
    tok_live = spread_blocks(block_live)
    positions = jnp.arange(tok_rows, dtype=jnp.int32)
    within = positions % BLOCK
    offset = positions - tok_start
    present = (
        (segments < doc_count)
        & (offset >= 0)
        & (offset < tok_length)
        & tok_live
        & (tok_slot < block_pair)
    )
    total_slots = groups * block_pair * BLOCK
    slot_index = jnp.where(
        present, (tok_dest * block_pair + tok_slot) * BLOCK + within, total_slots
    )
    target_row = jnp.where(present, tok_first + within, CAP)
    out_rows = (
        jnp.zeros((total_slots, 2 * rank), jnp.bfloat16).at[slot_index].set(features, mode="drop")
    )
    out_target = (
        jnp.full((total_slots,), CAP, jnp.int32).at[slot_index].set(target_row, mode="drop")
    )
    received_rows, received_target = (
        lax.all_to_all(
            out_rows.reshape(groups, block_pair * BLOCK, 2 * rank),
            "dp",
            split_axis=0,
            concat_axis=0,
            tiled=True,
        ),
        lax.all_to_all(
            out_target.reshape(groups, block_pair * BLOCK),
            "dp",
            split_axis=0,
            concat_axis=0,
            tiled=True,
        ),
    )
    balanced = (
        jnp.zeros((CAP, 2 * rank), jnp.bfloat16)
        .at[received_target.reshape(-1)]
        .set(received_rows.reshape(-1, 2 * rank), mode="drop")
    )
    owner = corpus // doc_count
    owner_row = corpus % doc_count
    owner_slot = pair_slots(owner)
    send_index = jnp.where(owner_slot < doc_pair, owner * doc_pair + owner_slot, groups * doc_pair)
    send_target = (
        jnp.full((groups * doc_pair,), doc_count, jnp.int32)
        .at[send_index]
        .set(owner_row, mode="drop")
        .reshape(groups, doc_pair)
    )
    outgoing = (
        jnp.zeros((groups * doc_pair, doc_grads.shape[1]), jnp.bfloat16)
        .at[send_index]
        .set(doc_grads, mode="drop")
    )
    arrived, arrived_target = (
        lax.all_to_all(
            outgoing.reshape(groups, doc_pair, -1), "dp", split_axis=0, concat_axis=0, tiled=True
        ),
        lax.all_to_all(send_target, "dp", split_axis=0, concat_axis=0, tiled=True),
    )
    owned = (
        jnp.zeros((doc_count, doc_grads.shape[1]), jnp.bfloat16)
        .at[arrived_target.reshape(-1)]
        .set(arrived.reshape(groups * doc_pair, -1), mode="drop")
    )
    influence = score_rows(owned, query_grads)
    return (input_grad, balanced, influence)


def solution(mesh):
    return jax.shard_map(
        body,
        mesh=mesh,
        in_specs=(
            P("dp", "mp"),
            P("dp", "mp"),
            P(None, "mp"),
            P(None, "mp"),
            P(),
            P("dp", "mp"),
            P("dp"),
            P("dp", None),
            P("dp"),
            P("dp"),
        ),
        out_specs=(P("dp", "mp"), P("dp", None), P("dp", "mp")),
        check_vma=False,
    )
```

profile of v0, /device:TPU:1, one launch (start us, length us, event | category | flops | bytes accessed | tf_op | source)
XLA Modules:
  0.0 203.9 jit_solution(11696186400224409392)
XLA Ops:
  7.2 0.0 copy-start
  7.2 0.0 all-gather.4.cloned.1.call-start
  7.2 0.7 all-gather.4.cloned.1.call-update
  7.9 0.0 copy-start.6
  7.9 0.0 copy-start.5
  7.9 0.0 copy-start.4
  7.9 0.0 copy-start.3
  8.0 0.0 copy-start.1
  8.0 0.0 all-reduce.2.cloned.1.call-start
  8.0 0.1 copy-done
  8.1 4.2 %convolution_convert_fusion.1 = bf16[1024,64]{0,1:T(8,128)(2,1)} fusion(bf16[1024,2048]{1,0:T(8,128)(2,1)} %param.10, bf16[64,2048]{1,0:T(8,128)(2,1)S(1)} %copy-done), kind=kOutput, calls=%fused_computation.7 | convolution fusion | flops 268500992 | bytes 4587520 | tf_op jit(solution)/shard_map/dot_general | solution.py:52
  12.4 0.0 all-reduce.2.cloned.1.call-update
  12.4 0.0 all-gather.6.cloned.1.call-start
  12.4 0.7 all-gather.6.cloned.1.call-update
  13.1 0.0 copy-done.6
  13.2 0.2 convert_reduce_fusion.1
  13.3 0.6 scatter_custom_fusion.3
  13.9 0.7 copy.26
  14.7 16.3 %all-to-all-start.2 = ((s32[128,1,1]{2,1,0:T(1,128)}), s32[128,1,1]{2,1,0:T(1,128)S(1)}, u32[]{:S(2)}, u32[]{:S(2)}) async-start(s32[128,1,1]{2,1,0:T(1,128)} %copy.26), calls=%async_computation.2 | async-start | bytes 131072 | tf_op jit(solution)/shard_map/all_to_all | solution.py:138
  31.0 0.2 reduce-window.9
  31.3 0.2 convert_reduce_fusion
  31.4 0.1 broadcast_in_dim.99
  31.5 0.1 lt.91
  31.7 0.1 broadcast_in_dim.96
  31.7 0.1 reshape.145
  31.9 0.1 broadcast_in_dim.100
  31.9 0.1 mul.11
  32.0 0.1 broadcast_in_dim.103
  32.1 0.1 reshape.146
  32.2 0.1 select_reduce_fusion.1
  32.4 4.3 %scatter_custom_fusion = s32[1024]{0:T(1024)S(1)} fusion(s32[1024]{0:T(1024)S(1)} %compare_select_fusion.1, s32[1024]{0:T(1024)S(1)} %get-tuple-element.5, s32[]{:T(128)} %constant.27.clone.1), kind=kCustom, calls=%fused_computation.50 | custom fusion | bytes 4100 | tf_op jit(solution)/shard_map/scatter | solution.py:96
  36.7 0.7 all_to_all.20
  37.4 0.0 copy-done.1
  37.4 2.3 %convolution_convert_fusion.2 = bf16[1024,64]{0,1:T(8,128)(2,1)S(1)} fusion(bf16[1024,1024]{1,0:T(8,128)(2,1)} %all-gather.4.cloned.1.call-done, bf16[64,1024]{1,0:T(8,128)(2,1)S(1)} %copy-done.1), kind=kOutput, calls=%fused_computation.8 | convolution fusion | flops 134283264 | bytes 2359296 | tf_op jit(solution)/shard_map/dot_general | solution.py:49
  39.8 1.9 all-to-all-done.2
  41.7 11.3 %all-to-all-start = ((s32[128,1,8]{2,1,0:T(1,128)}), s32[128,1,8]{2,1,0:T(1,128)S(1)}, u32[]{:S(2)}, u32[]{:S(2)}) async-start(s32[128,1,8]{2,1,0:T(1,128)} %bitcast.6), calls=%async_computation | async-start | bytes 131072 | tf_op jit(solution)/shard_map/all_to_all | solution.py:106
  53.0 10.5 %all-reduce.2.cloned.1.call-done = bf16[1024,64]{0,1:T(8,128)(2,1)} async-done(((bf16[1024,64]{0,1:T(8,128)(2,1)}), bf16[1024,64]{0,1:T(8,128)(2,1)}) %all-reduce.2.cloned.1.call-update) | async-done | bytes 131088 | tf_op jit(solution)/shard_map/psum | solution.py:53
  63.5 1.2 fusion
  64.7 0.1 reshape.188
  64.8 0.9 scatter_custom_fusion.4
  65.7 0.5 broadcast.149
  66.2 1.0 reduce.5
  67.2 1.2 reshape.229
  68.4 0.0 all-to-all-done
  68.4 13.7 %all-to-all-start.3 = ((bf16[128,2,1024]{2,1,0:T(2,128)(2,1)}), bf16[128,2,1024]{2,1,0:T(2,128)(2,1)S(1)}, u32[]{:S(2)}, u32[]{:S(2)}) async-start(bf16[128,2,1024]{2,1,0:T(2,128)(2,1)} %reshape.229), calls=%async_computation.3 | async-start | bytes 1048576 | tf_op jit(solution)/shard_map/all_to_all | solution.py:135
  82.1 2.4 %reduce.1 = s32[128]{0:T(128)S(1)} reduce(s32[128,1,1]{2,1,0:T(1,128)S(1)} %all-to-all-done.2, s32[]{:T(128)} %constant.32.clone.1), dimensions={1,2}, to_apply=%all_to_all.24.reduce_sub_computation | reduce | bytes 1028 | tf_op jit(solution)/shard_map/all_to_all | solution.py:138
  84.5 0.5 broadcast.146
  85.0 0.8 reduce.4
  85.8 0.1 reshape.147
  86.0 0.2 copy.25
  86.1 3.8 %scatter_custom_fusion.1 = bf16[1024,128]{1,0:T(8,128)(2,1)} fusion(s32[1024]{0:T(1024)S(1)} %compare_select_fusion.1, bf16[1024,128]{1,0:T(8,128)(2,1)S(1)} %copy.25, bf16[]{:T(256)} %constant.26.clone.1), kind=kCustom, calls=%fused_computation.23 | custom fusion | bytes 262146 | tf_op jit(solution)/shard_map/scatter | solution.py:93
  89.9 11.2 %all-to-all-done.3 = bf16[128,2,1024]{2,1,0:T(2,128)(2,1)S(1)} async-done(((bf16[128,2,1024]{2,1,0:T(2,128)(2,1)}), bf16[128,2,1024]{2,1,0:T(2,128)(2,1)S(1)}, u32[]{:S(2)}, u32[]{:S(2)}) %all-to-all-start.3) | async-done | bytes 524320 | tf_op jit(solution)/shard_map/all_to_all | solution.py:135
  101.2 6.5 %all-to-all-start.1 = ((bf16[128,8,128]{2,1,0:T(8,128)(2,1)}), bf16[128,8,128]{2,1,0:T(8,128)(2,1)S(1)}, u32[]{:S(2)}, u32[]{:S(2)}) async-start(bf16[128,8,128]{2,1,0:T(8,128)(2,1)} %bitcast.8), calls=%async_computation.1 | async-start | bytes 524288 | tf_op jit(solution)/shard_map/all_to_all | solution.py:99
  107.7 0.0 reduce-scatter.2.cloned.1.call-start
  107.8 0.5 reshape.230
  108.2 1.6 scatter_custom_fusion.5
  109.8 68.4 %all-gather.6.cloned.1.call-done = bf16[128,4,2048]{2,1,0:T(4,128)(2,1)} async-done(((bf16[1,4,2048]{2,1,0:T(4,128)(2,1)}), bf16[128,4,2048]{2,1,0:T(4,128)(2,1)}) %all-gather.6.cloned.1.call-update) | async-done | bytes 2097168 | tf_op jit(solution)/shard_map/all_gather | solution.py:29
  178.2 2.5 %reshape.205 = bf16[512,2048]{1,0:T(8,128)(2,1)S(1)} reshape(bf16[128,4,2048]{2,1,0:T(4,128)(2,1)} %all-gather.6.cloned.1.call-done) | data formatting | bytes 4194304
  180.8 1.3 fusion.29
  182.0 0.0 reduce-scatter.2.cloned.1.call-update
  182.1 9.3 %convolution_convert_fusion = bf16[1024,2048]{1,0:T(8,128)(2,1)} fusion(bf16[1024,1024]{1,0:T(8,128)(2,1)} %all-gather.4.cloned.1.call-done, bf16[1024,2048]{1,0:T(8,128)(2,1)} %param.12), kind=kOutput, calls=%fused_computation.6 | convolution fusion | flops 4297064448 | bytes 10485760 | tf_op jit(solution)/shard_map/dot_general | solution.py:48
  191.4 0.0 all-to-all-done.1
  191.4 3.8 %scatter_custom_fusion.2 = bf16[640,128]{1,0:T(8,128)(2,1)} fusion(s32[1024]{0:T(1024)S(1)} %bitcast.53, bf16[128,8,128]{2,1,0:T(8,128)(2,1)S(1)} %all-to-all-done.1, bf16[]{:T(256)} %constant.26.clone.1), kind=kCustom, calls=%fused_computation.18 | custom fusion | bytes 425986 | tf_op jit(solution)/shard_map/scatter | solution.py:117
  195.2 2.2 %reduce-scatter.2.cloned.1.call-done = f32[8,256]{1,0:T(8,128)} async-done(((f32[8,512]{1,0:T(8,128)}), f32[8,256]{1,0:T(8,128)}) %reduce-scatter.2.cloned.1.call-update) | async-done | bytes 8208 | tf_op jit(solution)/shard_map/reduce_scatter | solution.py:33
  (22 shorter events, 0.2 us)
Async XLA Ops:
  7.2 1.0 copy-start
  7.2 30.2 %all-gather.4.cloned.1.call-start = ((), (), s32[]{:S(2)}) async-start(), calls=%async_computation.5 | async-start | bytes 3145728 | tf_op jit(solution)/shard_map/all_gather | solution.py:47
  7.9 5.2 %copy-start.6 = (s32[8]{0:T(128)S(1)}, s32[8]{0:T(128)}, u32[]{:S(2)}) copy-start(s32[8]{0:T(128)} %param.18) | copy-start | bytes 100
  7.9 23.1 %copy-start.5 = (s32[8]{0:T(128)S(1)}, s32[8]{0:T(128)}, u32[]{:S(2)}) copy-start(s32[8]{0:T(128)} %param.16) | copy-start | bytes 100
  7.9 23.3 %copy-start.4 = (s32[128,2]{0,1:T(2,128)S(1)}, s32[128,2]{0,1:T(2,128)}, u32[]{:S(2)}) copy-start(s32[128,2]{0,1:T(2,128)} %param.17) | copy-start | bytes 3076
  7.9 24.3 %copy-start.3 = (s32[1024]{0:T(1024)S(1)}, s32[1024]{0:T(1024)}, u32[]{:S(2)}) copy-start(s32[1024]{0:T(1024)} %param.19) | copy-start | bytes 12292
  8.0 29.4 %copy-start.1 = (bf16[64,1024]{1,0:T(8,128)(2,1)S(1)}, bf16[64,1024]{1,0:T(8,128)(2,1)}, u32[]{:S(2)}) copy-start(bf16[64,1024]{1,0:T(8,128)(2,1)} %param.14) | copy-start | bytes 393220
  8.0 55.5 %all-reduce.2.cloned.1.call-start = ((), (), s32[]{:S(2)}) async-start(), calls=%async_computation.6 | async-start | bytes 262144 | tf_op jit(solution)/shard_map/psum | solution.py:53
  12.4 165.9 %all-gather.6.cloned.1.call-start = ((), (), s32[]{:S(2)}) async-start(), calls=%async_computation.8 | async-start | bytes 2113536 | tf_op jit(solution)/shard_map/all_gather | solution.py:29
  14.7 27.0 %all-to-all-start.2 = ((s32[128,1,1]{2,1,0:T(1,128)}), s32[128,1,1]{2,1,0:T(1,128)S(1)}, u32[]{:S(2)}, u32[]{:S(2)}) async-start(s32[128,1,1]{2,1,0:T(1,128)} %copy.26), calls=%async_computation.2 | async-start | bytes 131072 | tf_op jit(solution)/shard_map/all_to_all | solution.py:138
  41.7 26.7 %all-to-all-start = ((s32[128,1,8]{2,1,0:T(1,128)}), s32[128,1,8]{2,1,0:T(1,128)S(1)}, u32[]{:S(2)}, u32[]{:S(2)}) async-start(s32[128,1,8]{2,1,0:T(1,128)} %bitcast.6), calls=%async_computation | async-start | bytes 131072 | tf_op jit(solution)/shard_map/all_to_all | solution.py:106
  64.7 21.3 %copy-start.2 = (bf16[1024,64]{0,1:T(8,128)(2,1)S(1)}, bf16[1024,64]{0,1:T(8,128)(2,1)}, u32[]{:S(2)}) copy-start(bf16[1024,64]{0,1:T(8,128)(2,1)} %all-reduce.2.cloned.1.call-done) | copy-start | bytes 393220
  68.4 32.8 %all-to-all-start.3 = ((bf16[128,2,1024]{2,1,0:T(2,128)(2,1)}), bf16[128,2,1024]{2,1,0:T(2,128)(2,1)S(1)}, u32[]{:S(2)}, u32[]{:S(2)}) async-start(bf16[128,2,1024]{2,1,0:T(2,128)(2,1)} %reshape.229), calls=%async_computation.3 | async-start | bytes 1048576 | tf_op jit(solution)/shard_map/all_to_all | solution.py:135
  101.2 90.2 %all-to-all-start.1 = ((bf16[128,8,128]{2,1,0:T(8,128)(2,1)}), bf16[128,8,128]{2,1,0:T(8,128)(2,1)S(1)}, u32[]{:S(2)}, u32[]{:S(2)}) async-start(bf16[128,8,128]{2,1,0:T(8,128)(2,1)} %bitcast.8), calls=%async_computation.1 | async-start | bytes 524288 | tf_op jit(solution)/shard_map/all_to_all | solution.py:99
  107.7 89.6 %reduce-scatter.2.cloned.1.call-start = ((), (), s32[]{:S(2)}) async-start(), calls=%async_computation.7 | async-start | bytes 24576 | tf_op jit(solution)/shard_map/reduce_scatter | solution.py:33
Sparse Core Ops, SparseCore 0:
  9.8 20.4 all-gather.3
  33.4 29.9 all-reduce.1
  67.1 111.1 all-gather.5
  182.2 15.1 reduce-scatter.1
where the time goes:
time: 206 us; the launch traced here: 204 us
  waiting for transfers between devices  95.6 us (46%)
  starting transfers between devices  48.1 us (23%)
  local copies, waits for them, and re-layouts  22.8 us (11%)
  matrix products  18.4 us (9%)
  between operations  14.1 us (7%)
  other arithmetic  4.9 us (2%)
    all_gather x1, waiting for transfers between devices, score_rows(): lax.all_gather(query_grads, 'dp', axis=0, tiled=True)  68.4 us
    all_to_all x1, starting transfers between devices, body(): lax.all_to_all(send_target, 'dp', split_axis=0, concat_axis=0, tiled=True)  16.3 us
    all_to_all x1, starting transfers between devices, body(): lax.all_to_all(outgoing.reshape(groups, doc_pair, -1), 'dp', split_axis=0...  13.7 us
    all_to_all x1, starting transfers between devices, body(): lax.all_to_all(out_target.reshape(groups, block_pair * BLOCK), 'dp', spli...  11.3 us
    all_to_all x1, waiting for transfers between devices, body(): lax.all_to_all(outgoing.reshape(groups, doc_pair, -1), 'dp', split_axis=0...  11.2 us
    psum x1, waiting for transfers between devices, body(): in_proj = lax.psum(in_part.astype(jnp.bfloat16), 'mp')  10.5 us
    dot_general x1, matrix products, body(): grad_sum = jnp.dot(piece, value_weight, preferred_element_type=jnp.float32)  9.33 us
    all_to_all x1, starting transfers between devices, body(): lax.all_to_all(out_rows.reshape(groups, block_pair * BLOCK, 2 * rank), 'd...  6.54 us
  transfers between devices with their start and end apart: 8, of which 5 were waited for; matrix products, arithmetic and copies ran while one was open for 22% of the time, Pallas kernels for 0%

commit v1 on v0

v1 whole, which is shorter than its diff:
```python
import jax
import jax.numpy as jnp
from jax import lax
from jax.experimental import pallas as pl
from jax.experimental.pallas import tpu as pltpu
from jax.sharding import PartitionSpec as P

BLOCK = 8
CAP = 640
NZ = 8
PLANE = 16
DP = 128
TOK = 1024
RANK = 64
DOCS = 8
SLOT = 16
SCORE_ROW = 8
PLACE_ROW = 12
OWNER_ROW = 13
GROUP = 4
LANES = 128
VMEM = pltpu.VMEM
F32 = jnp.float32
BF16 = jnp.bfloat16
NT = (((1,), (1,)), ((), ()))
TN = (((0,), (0,)), ((), ()))


def dot(a, b, dims=(((1,), (0,)), ((), ()))):
    return lax.dot_general(a, b, dims, preferred_element_type=F32)


def lane_iota(shape):
    return lax.broadcasted_iota(jnp.int32, shape, len(shape) - 1)


def params():
    return pltpu.CompilerParams(vmem_limit_bytes=48 * 1024 * 1024)


def partial_kernel(acts_ref, cot_ref, pin_ref, pout_ref, out_ref):
    half = cot_ref.shape[1]
    me = lax.axis_index("mp")
    pout = pout_ref[:, pl.ds(pl.multiple_of(me * half, half), half)]
    low = dot(acts_ref[...], pin_ref[...], NT)
    out = dot(cot_ref[...], pout, NT)
    out_ref[...] = jnp.concatenate([low, out], axis=1)


def partial_features(acts, cotangent, proj_in, proj_out):
    rows = 256
    return pl.pallas_call(
        partial_kernel,
        grid=(TOK // rows,),
        in_specs=[
            pl.BlockSpec((rows, acts.shape[1]), lambda i: (i, 0)),
            pl.BlockSpec((rows, cotangent.shape[1]), lambda i: (i, 0)),
            pl.BlockSpec(proj_in.shape, lambda i: (0, 0)),
            pl.BlockSpec(proj_out.shape, lambda i: (0, 0)),
        ],
        out_specs=pl.BlockSpec((rows, 2 * RANK), lambda i: (i, 0)),
        out_shape=jax.ShapeDtypeStruct((TOK, 2 * RANK), F32),
        compiler_params=params(),
        cost_estimate=pl.CostEstimate(flops=340_000_000, bytes_accessed=6_000_000, transcendentals=0),
    )(acts, cotangent, proj_in, proj_out)


def docs_kernel(own_ref, other_ref, lengths_ref, corpus_ref, feat_ref, docs_ref, scr):
    half = RANK // 2
    me = lax.axis_index("mp")
    feat = (own_ref[...] + other_ref[...]).astype(BF16)
    feat_ref[...] = feat
    row = lax.broadcasted_iota(jnp.int32, (LANES, 3 * LANES), 0)
    col = lane_iota((LANES, 3 * LANES))
    wide = col < 2 * LANES
    odd = jnp.where(col >= LANES, 1, 0)
    want = jnp.where(wide, RANK + me * half + 2 * (col % 16) + odd, col % RANK)
    pick = jnp.where(row == want, 1.0, 0.0).astype(BF16)
    spread = dot(feat, pick)
    doc = lane_iota((1, 2 * LANES)) % LANES // 16
    first = jnp.zeros((1, 2 * LANES), jnp.int32)
    last = jnp.zeros((1, 2 * LANES), jnp.int32)
    at = 0
    for i in range(DOCS):
        length = lengths_ref[i]
        first = jnp.where(doc == i, at, first)
        last = jnp.where(doc == i, at + length, last)
        at = at + length
    token = lax.broadcasted_iota(jnp.int32, (TOK, 2 * LANES), 0)
    live = (token >= first) & (token < last)
    out_cols = jnp.where(live, spread[:, : 2 * LANES], 0.0).astype(BF16)
    in_cols = spread[:, 2 * LANES :].astype(BF16)
    both = dot(out_cols, in_cols, TN)
    lane = lane_iota((LANES, LANES))
    scr[...] = jnp.where(lane < RANK, both[:LANES], both[LANES:])
    pairs = half // 2
    for p in range(pairs // 2):
        low = scr[pl.ds(p, DOCS, stride=pairs), :]
        high = scr[pl.ds(p + pairs // 2, DOCS, stride=pairs), :]
        docs_ref[:, p * LANES : (p + 1) * LANES] = jnp.concatenate([low, high], axis=0).astype(BF16)
    sub = lax.broadcasted_iota(jnp.int32, (2 * DOCS, LANES), 0)
    note = jnp.zeros((2 * DOCS, LANES), jnp.int32)
    for i in range(DOCS):
        note = jnp.where(sub == i, corpus_ref[i] // DOCS, note)
        note = jnp.where(sub == DOCS + i, corpus_ref[i] % DOCS + 1, note)
    docs_ref[:, pairs // 2 * LANES :] = note.astype(F32).astype(BF16)


def features_and_docs(own, other, lengths, corpus):
    smem = pl.BlockSpec(memory_space=pltpu.SMEM)
    vmem = pl.BlockSpec(memory_space=VMEM)
    return pl.pallas_call(
        docs_kernel,
        in_specs=[vmem, vmem, smem, smem],
        out_specs=[vmem, vmem],
        out_shape=[
            jax.ShapeDtypeStruct((TOK, 2 * RANK), BF16),
            jax.ShapeDtypeStruct((2 * DOCS, 9 * LANES), BF16),
        ],
        scratch_shapes=[VMEM((LANES, LANES), F32)],
        compiler_params=params(),
        cost_estimate=pl.CostEstimate(flops=200_000_000, bytes_accessed=1_500_000, transcendentals=0),
    )(own, other, lengths, corpus)


def score_kernel(d0, d1, d2, d3, queries_ref, out_ref):
    width = 8 * LANES
    left, right = queries_ref[:, :width], queries_ref[:, width:]
    for i, ref in enumerate((d0, d1, d2, d3)):
        piece = ref[:, :width]
        out_ref[i * DOCS : (i + 1) * DOCS, :] = (
            dot(piece, left, NT)[:DOCS] + dot(piece, right, NT)[DOCS:]
        )


def partial_scores(pieces, queries):
    vmem = pl.BlockSpec(memory_space=VMEM)
    return pl.pallas_call(
        score_kernel,
        in_specs=[vmem] * 5,
        out_specs=vmem,
        out_shape=jax.ShapeDtypeStruct((GROUP * DOCS, LANES), F32),
        compiler_params=params(),
        cost_estimate=pl.CostEstimate(flops=17_000_000, bytes_accessed=700_000, transcendentals=0),
    )(*pieces, queries)


def pack_kernel(feat_ref, plan_ref, own_ref, other_ref, d0, d1, d2, d3, out_ref, tokens, stage):
    tokens[...] = feat_ref[...].astype(F32)
    stage[...] = jnp.zeros_like(stage)
    lane = lane_iota((LANES, LANES))
    dest = plan_ref[:, 0:1]
    first = plan_ref[:, 1:2]
    send = jnp.where((dest == lane) & (first < CAP), 1.0, 0.0).astype(BF16)
    for r in range(BLOCK):
        rows = tokens[pl.ds(r, DP, stride=BLOCK), :].astype(BF16)
        stage[pl.ds(r, DP, stride=SLOT), :] = dot(send, rows, TN)
    place = jnp.broadcast_to(first // BLOCK + 1, (DP, LANES)).astype(F32).astype(BF16)
    stage[pl.ds(PLACE_ROW, DP, stride=SLOT), :] = dot(send, place, TN)
    scores = (own_ref[...] + other_ref[...]).astype(BF16).astype(F32)
    short = lane_iota((DOCS, LANES))
    marks = jnp.zeros((DP, LANES), F32)
    for i, ref in enumerate((d0, d1, d2, d3)):
        note = ref[:, 8 * LANES :].astype(F32)
        owner, row = note[:DOCS], note[DOCS:]
        hit = jnp.where(owner == short.astype(F32), 1.0, 0.0)
        stage[pl.ds(SCORE_ROW + i, DP, stride=SLOT), :] = dot(
            hit, scores[i * DOCS : (i + 1) * DOCS], TN
        )
        marks = marks + dot(hit, jnp.where(short // 32 == i, row, 0.0), TN)
    stage[pl.ds(OWNER_ROW, DP, stride=SLOT), :] = marks
    out_ref[...] = stage[...].astype(BF16)


def pack(features, plan, own, other, pieces):
    vmem = pl.BlockSpec(memory_space=VMEM)
    return pl.pallas_call(
        pack_kernel,
        in_specs=[vmem] * 8,
        out_specs=vmem,
        out_shape=jax.ShapeDtypeStruct((DP * SLOT, LANES), BF16),
        scratch_shapes=[VMEM((TOK, LANES), F32), VMEM((DP * SLOT, LANES), F32)],
        compiler_params=params(),
        cost_estimate=pl.CostEstimate(flops=40_000_000, bytes_accessed=900_000, transcendentals=0),
    )(features, plan, own, other, *pieces)


def unpack_kernel(got_ref, balanced_ref, influence_ref, stage, rows):
    stage[...] = got_ref[...].astype(F32)
    lane = lane_iota((DP, LANES))
    place = stage[pl.ds(PLACE_ROW, DP, stride=SLOT), :]
    put = jnp.where(place == (lane + 1).astype(F32), 1.0, 0.0).astype(BF16)
    for r in range(BLOCK):
        part = stage[pl.ds(r, DP, stride=SLOT), :].astype(BF16)
        rows[pl.ds(r, CAP // BLOCK, stride=BLOCK), :] = dot(put, part, TN)[: CAP // BLOCK]
    balanced_ref[...] = rows[...].astype(BF16)
    me = lax.axis_index("mp")
    count = 2 * PLANE
    short = lane_iota((count, LANES))
    want = jnp.where(short % 32 < DOCS, short % 32 + 1, -1).astype(F32)
    for j in range(2):
        base = pl.multiple_of((me * 2 + j) * count * SLOT, count * SLOT)
        mark = stage[pl.ds(base + OWNER_ROW, count, stride=SLOT), :]
        hit = jnp.where(mark == want, 1.0, 0.0).astype(BF16)
        total = jnp.zeros((DOCS, LANES), F32)
        for i in range(GROUP):
            part = stage[pl.ds(base + SCORE_ROW + i, count, stride=SLOT), :].astype(BF16)
            total = total + dot(hit, part, TN)[i * 32 : i * 32 + DOCS]
        influence_ref[:, j * LANES : (j + 1) * LANES] = total


def unpack(got):
    vmem = pl.BlockSpec(memory_space=VMEM)
    return pl.pallas_call(
        unpack_kernel,
        in_specs=[vmem],
        out_specs=[vmem, vmem],
        out_shape=[
            jax.ShapeDtypeStruct((CAP, 2 * RANK), BF16),
            jax.ShapeDtypeStruct((DOCS, 2 * LANES), F32),
        ],
        scratch_shapes=[VMEM((DP * SLOT, LANES), F32), VMEM((CAP, LANES), F32)],
        compiler_params=params(),
        cost_estimate=pl.CostEstimate(flops=40_000_000, bytes_accessed=700_000, transcendentals=0),
    )(got)


def grad_kernel(own_ref, other_ref, weight_ref, out_ref):
    half = own_ref.shape[1]
    me = lax.axis_index("mp")
    mine = weight_ref[pl.ds(pl.multiple_of(me * half, half), half), :]
    theirs = weight_ref[pl.ds(pl.multiple_of((1 - me) * half, half), half), :]
    total = dot(own_ref[...], mine) + dot(other_ref[...], theirs)
    out_ref[...] = total.astype(BF16)


def input_gradient(own, other, weight):
    rows = 256
    return pl.pallas_call(
        grad_kernel,
        grid=(TOK // rows,),
        in_specs=[
            pl.BlockSpec((rows, own.shape[1]), lambda i: (i, 0)),
            pl.BlockSpec((rows, own.shape[1]), lambda i: (i, 0)),
            pl.BlockSpec(weight.shape, lambda i: (0, 0)),
        ],
        out_specs=pl.BlockSpec((rows, weight.shape[1]), lambda i: (i, 0)),
        out_shape=jax.ShapeDtypeStruct((TOK, weight.shape[1]), BF16),
        compiler_params=params(),
        cost_estimate=pl.CostEstimate(flops=4_300_000_000, bytes_accessed=10_500_000, transcendentals=0),
    )(own, other, weight)


def body(
    acts, cotangent, value_weight, proj_in, proj_out, query_grads, lengths, plan, corpus, segments
):
    swap = [(0, 1), (1, 0)]
    pair_size = 2 * PLANE
    pairs = [[k * pair_size + i for i in range(pair_size)] for k in range(NZ // 2)]
    other_cot = lax.ppermute(cotangent, "mp", swap)
    queries = lax.all_to_all(
        jnp.broadcast_to(query_grads[None], (pair_size,) + query_grads.shape),
        "dp",
        0,
        0,
        tiled=True,
        axis_index_groups=pairs,
    ).reshape(LANES, -1)
    own = partial_features(acts, cotangent, proj_in, proj_out)
    features, docs = features_and_docs(own, lax.ppermute(own, "mp", swap), lengths, corpus)
    pieces = [docs]
    for i in range(1, GROUP):
        step = 2 * PLANE * i
        pieces.append(lax.ppermute(docs, "dp", [(s, (s + step) % DP) for s in range(DP)]))
    mine = partial_scores(pieces, queries)
    packed = pack(features, plan, mine, lax.ppermute(mine, "mp", swap), pieces)
    got = lax.all_to_all(packed.reshape(DP, SLOT, LANES), "dp", 0, 0, tiled=True)
    input_grad = input_gradient(cotangent, other_cot, value_weight)
    balanced, influence = unpack(got.reshape(DP * SLOT, LANES))
    return (input_grad, balanced, influence)


def solution(mesh):
    return jax.shard_map(
        body,
        mesh=mesh,
        in_specs=(
            P("dp", "mp"),
            P("dp", "mp"),
            P(None, "mp"),
            P(None, "mp"),
            P(),
            P("dp", "mp"),
            P("dp"),
            P("dp", None),
            P("dp"),
            P("dp"),
        ),
        out_specs=(P("dp", "mp"), P("dp", None), P("dp", "mp")),
        check_vma=False,
    )
```

time: 206 us -> 73.5 us (0.36)
  waiting for transfers between devices: 95.6 us -> 16 us
  matrix products: 18.4 us -> 0 us
  local copies, waits for them, and re-layouts: 22.8 us -> 6.04 us
  Pallas kernels: 0 us -> 16.5 us
  starting transfers between devices: 48.1 us -> 33.6 us
  between operations: 14.1 us -> 0.72 us
  other arithmetic: 4.9 us -> 0 us
    all_gather x2 -> x0, waiting for transfers between devices: 68.4 us -> none  [the longest x1 68.4 us: score_rows(): lax.all_gather(query_grads, 'dp', axis=0, tiled=True)]
    all_to_all x4 -> x2, starting transfers between devices: 47.9 us -> 21.9 us  [the longest x1 12.7 us: body(): lax.all_to_all(packed.reshape(DP, SLOT, LANES), 'dp', 0, 0, tiled=True)]
    dot_general x5 -> x0, matrix products: 18.4 us -> none  [the longest x1 9.33 us: body(): grad_sum = jnp.dot(piece, value_weight, preferred_element_type=jnp.float32)]
    pallas_call x0 -> x6, Pallas kernels: none -> 16.5 us  [the longest x1 8.36 us: input_gradient(): pl.pallas_call(grad_kernel, grid=(TOK // rows,), in_specs=[pl.BlockSpec((...]
    scatter x6 -> x0, local copies, waits for them, and re-layouts: 14.9 us -> none  [the longest x1 4.31 us: body(): jnp.full((total_slots,), CAP, jnp.int32).at[slot_index]]
    ppermute x0 -> x6, starting transfers between devices: none -> 11.6 us  [the longest x3 8.46 us: body(): lax.ppermute(docs, 'dp', [(s, (s + step) % DP) for s in range(DP)])]
    psum x1 -> x0, waiting for transfers between devices: 10.5 us -> none  [body(): in_proj = lax.psum(in_part.astype(jnp.bfloat16), 'mp')]
    ppermute x0 -> x6, waiting for transfers between devices: none -> 5.48 us  [the longest x3 3.32 us: body(): lax.ppermute(docs, 'dp', [(s, (s + step) % DP) for s in range(DP)])]
  transfers between devices with their start and end apart: 8 -> 8, of which waited for: 5 -> 4; matrix products, arithmetic and copies ran while one was open for 22% -> 0% of each run, Pallas kernels for 0% -> 21%
where the time goes in v1:
time: 73.5 us; the launch traced here: 72.7 us
  starting transfers between devices  33.6 us (46%)
  Pallas kernels  16.5 us (22%)
  waiting for transfers between devices  16 us (22%)
  local copies, waits for them, and re-layouts  6.04 us (8%)
    all_to_all x1, starting transfers between devices, body(): lax.all_to_all(packed.reshape(DP, SLOT, LANES), 'dp', 0, 0, tiled=True)  12.7 us
    all_to_all x1, waiting for transfers between devices, body(): lax.all_to_all(packed.reshape(DP, SLOT, LANES), 'dp', 0, 0, tiled=True)  10.5 us
    all_to_all x1, starting transfers between devices, body(): lax.all_to_all(jnp.broadcast_to(query_grads[None], (pair_size,) + query_g...  9.22 us
    ppermute x3, starting transfers between devices, body(): lax.ppermute(docs, 'dp', [(s, (s + step) % DP) for s in range(DP)])  8.46 us
    pallas_call x1, Pallas kernels, input_gradient(): pl.pallas_call(grad_kernel, grid=(TOK // rows,), in_specs=[pl.BlockSpec((...  8.36 us
    unnamed x13, local copies, waits for them, and re-layouts  4.16 us
    pallas_call x1, Pallas kernels, partial_features(): pl.pallas_call(partial_kernel, grid=(TOK // rows,), in_specs=[pl.BlockSpe...  3.62 us
    ppermute x3, waiting for transfers between devices, body(): lax.ppermute(docs, 'dp', [(s, (s + step) % DP) for s in range(DP)])  3.32 us
  transfers between devices with their start and end apart: 8, of which 4 were waited for; matrix products, arithmetic and copies ran while one was open for 0% of the time, Pallas kernels for 21%

profile of v1, /device:TPU:1, one launch (start us, length us, event | category | flops | bytes accessed | tf_op | source)
XLA Modules:
  0.0 72.7 jit_solution(17152550841851517271)
XLA Ops:
  0.6 0.0 copy-start.4
  0.6 0.0 copy-start.3
  0.7 1.8 %broadcast_in_dim.2 = bf16[32,4,2048]{2,1,0:T(4,128)(2,1)} broadcast(bf16[4,2048]{1,0:T(4,128)(2,1)} %param.15), dimensions={1,2} | broadcast | bytes 540672 | tf_op jit(solution)/shard_map/broadcast_in_dim | solution.py:262
  2.4 9.2 %all-to-all-start = ((bf16[32,4,2048]{2,1,0:T(4,128)(2,1)}), bf16[32,4,2048]{2,1,0:T(4,128)(2,1)S(1)}, u32[]{:S(2)}, u32[]{:S(2)}) async-start(bf16[32,4,2048]{2,1,0:T(4,128)(2,1)} %broadcast_in_dim.2), calls=%async_computation | async-start | bytes 1048576 | tf_op jit(solution)/shard_map/all_to_all | solution.py:261
  11.6 0.0 copy-start
  11.7 2.2 %copy-done = bf16[1024,2048]{1,0:T(8,128)(2,1)S(1)} copy-done((bf16[1024,2048]{1,0:T(8,128)(2,1)S(1)}, bf16[1024,2048]{1,0:T(8,128)(2,1)}, u32[]{:S(2)}) %copy-start) | copy-done | bytes 4194328
  13.8 0.0 copy-start.1
  13.8 0.9 %copy-done.1 = bf16[64,2048]{1,0:T(8,128)(2,1)S(1)} copy-done((bf16[64,2048]{1,0:T(8,128)(2,1)S(1)}, bf16[64,2048]{1,0:T(8,128)(2,1)}, u32[]{:S(2)}) %copy-start.1) | copy-done | bytes 262168
  14.8 0.0 copy-start.2
  14.8 0.9 %copy-done.2 = bf16[64,1024]{1,0:T(8,128)(2,1)S(1)} copy-done((bf16[64,1024]{1,0:T(8,128)(2,1)S(1)}, bf16[64,1024]{1,0:T(8,128)(2,1)}, u32[]{:S(2)}) %copy-start.2) | copy-done | bytes 131096
  15.7 0.0 copy-start.5
  15.7 3.6 %shard_map.113.own_ref = f32[1024,128]{1,0:T(8,128)S(1)} custom-call(bf16[1024,2048]{1,0:T(8,128)(2,1)S(1)} %copy-done, bf16[1024,512]{1,0:T(8,128)(2,1)} %cot_ref.1, bf16[64,2048]{1,0:T(8,128)(2,1)S(1)} %copy-done.1, bf16[64,1024]{1,0:T(8,128)(2,1)S(1)} %copy-done.2), custom_call_target="tpu_custom_call" | custom-call | flops 340000000 | bytes 6000000 | tf_op jit(solution)/shard_map/pallas_call | solution.py:52
  19.3 1.0 %collective-permute-start.1 = (f32[1024,128]{1,0:T(8,128)S(1)}, f32[1024,128]{1,0:T(8,128)S(1)}, u32[]{:S(2)}, u32[]{:S(2)}) collective-permute-start(f32[1024,128]{1,0:T(8,128)S(1)} %shard_map.113.own_ref), channel_id=1, source_target_pairs={{0,1},{1,0},{2,3},{3,2},{4,5},{5,4},{6,7},{7,6},{8,9},{9,8},{10,11... | collective-permute-start | bytes 1572872 | tf_op jit(solution)/shard_map/ppermute | solution.py:270
  20.4 0.1 collective-permute-start
  20.5 1.4 %collective-permute-done.1.other_ref = f32[1024,128]{1,0:T(8,128)S(1)} collective-permute-done((f32[1024,128]{1,0:T(8,128)S(1)}, f32[1024,128]{1,0:T(8,128)S(1)}, u32[]{:S(2)}, u32[]{:S(2)}) %collective-permute-start.1) | collective-permute-done | bytes 524320 | tf_op jit(solution)/shard_map/ppermute | solution.py:270
  21.9 0.0 copy-done.4
  21.9 0.0 copy-done.3
  21.9 1.2 %shard_map.114 = (bf16[1024,128]{1,0:T(8,128)(2,1)S(1)}, bf16[16,1152]{1,0:T(8,128)(2,1)S(1)}) custom-call(f32[1024,128]{1,0:T(8,128)S(1)} %shard_map.113.own_ref, f32[1024,128]{1,0:T(8,128)S(1)} %collective-permute-done.1.other_ref, s32[8]{0:T(128)S(1)} %copy-done.3, s32[8]{0:T(128)S(1)} %copy-done.4), custom_call_target="tpu_custom_call" | custom-call | flops 200000000 | bytes 1500000 | tf_op jit(solution)/shard_map/pallas_call | solution.py:112
  23.1 5.2 %collective-permute-start.4 = (bf16[16,1152]{1,0:T(8,128)(2,1)S(1)}, bf16[16,1152]{1,0:T(8,128)(2,1)S(1)}, u32[]{:S(2)}, u32[]{:S(2)}) collective-permute-start(bf16[16,1152]{1,0:T(8,128)(2,1)S(1)} %get-tuple-element.8.d0), channel_id=1, source_target_pairs={{0,192},{2,194},{4,196},{6,198},{8,200},{10,202},{12,204},{14,206}... | collective-permute-start | bytes 110600 | tf_op jit(solution)/shard_map/ppermute | solution.py:274
  28.3 1.2 %collective-permute-start.3 = (bf16[16,1152]{1,0:T(8,128)(2,1)S(1)}, bf16[16,1152]{1,0:T(8,128)(2,1)S(1)}, u32[]{:S(2)}, u32[]{:S(2)}) collective-permute-start(bf16[16,1152]{1,0:T(8,128)(2,1)S(1)} %get-tuple-element.8.d0), channel_id=1, source_target_pairs={{0,128},{2,130},{4,132},{6,134},{8,136},{10,138},{12,140},{14,142}... | collective-permute-start | bytes 110600 | tf_op jit(solution)/shard_map/ppermute | solution.py:274
  29.5 2.1 %collective-permute-start.2 = (bf16[16,1152]{1,0:T(8,128)(2,1)S(1)}, bf16[16,1152]{1,0:T(8,128)(2,1)S(1)}, u32[]{:S(2)}, u32[]{:S(2)}) collective-permute-start(bf16[16,1152]{1,0:T(8,128)(2,1)S(1)} %get-tuple-element.8.d0), channel_id=1, source_target_pairs={{0,64},{2,66},{4,68},{6,70},{8,72},{10,74},{12,76},{14,78},{16,80}... | collective-permute-start | bytes 110600 | tf_op jit(solution)/shard_map/ppermute | solution.py:274
  31.6 0.0 all-to-all-done
  31.6 0.1 reshape.16.queries_ref
  31.7 0.0 collective-permute-done.4.d3
  31.7 3.3 %collective-permute-done.3.d2 = bf16[16,1152]{1,0:T(8,128)(2,1)S(1)} collective-permute-done((bf16[16,1152]{1,0:T(8,128)(2,1)S(1)}, bf16[16,1152]{1,0:T(8,128)(2,1)S(1)}, u32[]{:S(2)}, u32[]{:S(2)}) %collective-permute-start.3) | collective-permute-done | bytes 36896 | tf_op jit(solution)/shard_map/ppermute | solution.py:274
  35.0 0.0 collective-permute-done.2.d1
  35.0 0.6 shard_map.115.own_ref
  35.7 2.0 %collective-permute-start.5 = (f32[32,128]{1,0:T(8,128)S(1)}, f32[32,128]{1,0:T(8,128)S(1)}, u32[]{:S(2)}, u32[]{:S(2)}) collective-permute-start(f32[32,128]{1,0:T(8,128)S(1)} %shard_map.115.own_ref), channel_id=1, source_target_pairs={{0,1},{1,0},{2,3},{3,2},{4,5},{5,4},{6,7},{7,6},{8,9},{9,8},{10,11... | collective-permute-start | bytes 49160 | tf_op jit(solution)/shard_map/ppermute | solution.py:276
  37.7 0.0 copy-done.5
  37.7 0.1 copy.12.plan_ref
  37.8 0.7 collective-permute-done.5.other_ref
  38.6 1.5 %shard_map.116 = bf16[2048,128]{1,0:T(8,128)(2,1)} custom-call(bf16[1024,128]{1,0:T(8,128)(2,1)S(1)} %get-tuple-element.7.feat_ref, s32[128,2]{1,0:T(8,128)S(1)} %copy.12.plan_ref, f32[32,128]{1,0:T(8,128)S(1)} %shard_map.115.own_ref, f32[32,128]{1,0:T(8,128)S(1)} %collective-permute-done.5.other_ref, bf16[16,1152]{1,0:T(8,128)(2,1)S(1)} %get-tuple-element.8.d0, ...), custom_call_target="tpu_custom_call" | custom-call | flops 40000000 | bytes 900000 | tf_op jit(solution)/shard_map/pallas_call | solution.py:177
  40.1 12.7 %all-to-all-start.1 = ((bf16[128,16,128]{2,1,0:T(8,128)(2,1)}), bf16[128,16,128]{2,1,0:T(8,128)(2,1)S(1)}, u32[]{:S(2)}, u32[]{:S(2)}) async-start(bf16[128,16,128]{2,1,0:T(8,128)(2,1)} %bitcast), calls=%async_computation.1 | async-start | bytes 1048576 | tf_op jit(solution)/shard_map/all_to_all | solution.py:277
  52.8 0.0 collective-permute-done.other_ref
  52.8 8.4 %shard_map.112 = bf16[1024,2048]{1,0:T(8,128)(2,1)} custom-call(bf16[1024,512]{1,0:T(8,128)(2,1)} %cot_ref.1, bf16[1024,512]{1,0:T(8,128)(2,1)S(1)} %collective-permute-done.other_ref, bf16[1024,2048]{1,0:T(8,128)(2,1)} %weight_ref.1), custom_call_target="tpu_custom_call" | custom-call | flops 4300000256 | bytes 10500000 | tf_op jit(solution)/shard_map/pallas_call | solution.py:239
  61.2 10.5 %all-to-all-done.1 = bf16[128,16,128]{2,1,0:T(8,128)(2,1)S(1)} async-done(((bf16[128,16,128]{2,1,0:T(8,128)(2,1)}), bf16[128,16,128]{2,1,0:T(8,128)(2,1)S(1)}, u32[]{:S(2)}, u32[]{:S(2)}) %all-to-all-start.1) | async-done | bytes 524320 | tf_op jit(solution)/shard_map/all_to_all | solution.py:277
  71.6 1.1 %shard_map.117 = (bf16[640,128]{1,0:T(8,128)(2,1)}, f32[8,256]{1,0:T(8,128)}) custom-call(bf16[2048,128]{1,0:T(8,128)(2,1)S(1)} %bitcast.2), custom_call_target="tpu_custom_call" | custom-call | flops 40000000 | bytes 700000 | tf_op jit(solution)/shard_map/pallas_call | solution.py:214
Async XLA Ops:
  0.6 21.3 %copy-start.4 = (s32[8]{0:T(128)S(1)}, s32[8]{0:T(128)}, u32[]{:S(2)}) copy-start(s32[8]{0:T(128)} %corpus_ref.1) | copy-start | bytes 100
  0.6 21.3 %copy-start.3 = (s32[8]{0:T(128)S(1)}, s32[8]{0:T(128)}, u32[]{:S(2)}) copy-start(s32[8]{0:T(128)} %lengths_ref.1) | copy-start | bytes 100
  2.4 29.2 %all-to-all-start = ((bf16[32,4,2048]{2,1,0:T(4,128)(2,1)}), bf16[32,4,2048]{2,1,0:T(4,128)(2,1)S(1)}, u32[]{:S(2)}, u32[]{:S(2)}) async-start(bf16[32,4,2048]{2,1,0:T(4,128)(2,1)} %broadcast_in_dim.2), calls=%async_computation | async-start | bytes 1048576 | tf_op jit(solution)/shard_map/all_to_all | solution.py:261
  11.6 2.2 %copy-start = (bf16[1024,2048]{1,0:T(8,128)(2,1)S(1)}, bf16[1024,2048]{1,0:T(8,128)(2,1)}, u32[]{:S(2)}) copy-start(bf16[1024,2048]{1,0:T(8,128)(2,1)} %acts_ref.1) | copy-start | bytes 12582916
  13.8 0.9 %copy-start.1 = (bf16[64,2048]{1,0:T(8,128)(2,1)S(1)}, bf16[64,2048]{1,0:T(8,128)(2,1)}, u32[]{:S(2)}) copy-start(bf16[64,2048]{1,0:T(8,128)(2,1)} %pin_ref.1) | copy-start | bytes 786436
  14.8 0.9 %copy-start.2 = (bf16[64,1024]{1,0:T(8,128)(2,1)S(1)}, bf16[64,1024]{1,0:T(8,128)(2,1)}, u32[]{:S(2)}) copy-start(bf16[64,1024]{1,0:T(8,128)(2,1)} %pout_ref.1) | copy-start | bytes 393220
  15.7 22.0 %copy-start.5 = (s32[128,2]{0,1:T(2,128)S(1)}, s32[128,2]{0,1:T(2,128)}, u32[]{:S(2)}) copy-start(s32[128,2]{0,1:T(2,128)} %param.17) | copy-start | bytes 3076
  19.3 2.6 %collective-permute-start.1 = (f32[1024,128]{1,0:T(8,128)S(1)}, f32[1024,128]{1,0:T(8,128)S(1)}, u32[]{:S(2)}, u32[]{:S(2)}) collective-permute-start(f32[1024,128]{1,0:T(8,128)S(1)} %shard_map.113.own_ref), channel_id=1, source_target_pairs={{0,1},{1,0},{2,3},{3,2},{4,5},{5,4},{6,7},{7,6},{8,9},{9,8},{10,11... | collective-permute-start | bytes 1572872 | tf_op jit(solution)/shard_map/ppermute | solution.py:270
  20.4 32.4 %collective-permute-start = (bf16[1024,512]{1,0:T(8,128)(2,1)}, bf16[1024,512]{1,0:T(8,128)(2,1)S(1)}, u32[]{:S(2)}, u32[]{:S(2)}) collective-permute-start(bf16[1024,512]{1,0:T(8,128)(2,1)} %cot_ref.1), channel_id=1, source_target_pairs={{0,1},{1,0},{2,3},{3,2},{4,5},{5,4},{6,7},{7,6},{8,9},{9,8},{10,11... | collective-permute-start | bytes 3145736 | tf_op jit(solution)/shard_map/ppermute | solution.py:260
  23.1 8.6 %collective-permute-start.4 = (bf16[16,1152]{1,0:T(8,128)(2,1)S(1)}, bf16[16,1152]{1,0:T(8,128)(2,1)S(1)}, u32[]{:S(2)}, u32[]{:S(2)}) collective-permute-start(bf16[16,1152]{1,0:T(8,128)(2,1)S(1)} %get-tuple-element.8.d0), channel_id=1, source_target_pairs={{0,192},{2,194},{4,196},{6,198},{8,200},{10,202},{12,204},{14,206}... | collective-permute-start | bytes 110600 | tf_op jit(solution)/shard_map/ppermute | solution.py:274
  28.3 6.7 %collective-permute-start.3 = (bf16[16,1152]{1,0:T(8,128)(2,1)S(1)}, bf16[16,1152]{1,0:T(8,128)(2,1)S(1)}, u32[]{:S(2)}, u32[]{:S(2)}) collective-permute-start(bf16[16,1152]{1,0:T(8,128)(2,1)S(1)} %get-tuple-element.8.d0), channel_id=1, source_target_pairs={{0,128},{2,130},{4,132},{6,134},{8,136},{10,138},{12,140},{14,142}... | collective-permute-start | bytes 110600 | tf_op jit(solution)/shard_map/ppermute | solution.py:274
  29.5 5.6 %collective-permute-start.2 = (bf16[16,1152]{1,0:T(8,128)(2,1)S(1)}, bf16[16,1152]{1,0:T(8,128)(2,1)S(1)}, u32[]{:S(2)}, u32[]{:S(2)}) collective-permute-start(bf16[16,1152]{1,0:T(8,128)(2,1)S(1)} %get-tuple-element.8.d0), channel_id=1, source_target_pairs={{0,64},{2,66},{4,68},{6,70},{8,72},{10,74},{12,76},{14,78},{16,80}... | collective-permute-start | bytes 110600 | tf_op jit(solution)/shard_map/ppermute | solution.py:274
  35.7 2.9 %collective-permute-start.5 = (f32[32,128]{1,0:T(8,128)S(1)}, f32[32,128]{1,0:T(8,128)S(1)}, u32[]{:S(2)}, u32[]{:S(2)}) collective-permute-start(f32[32,128]{1,0:T(8,128)S(1)} %shard_map.115.own_ref), channel_id=1, source_target_pairs={{0,1},{1,0},{2,3},{3,2},{4,5},{5,4},{6,7},{7,6},{8,9},{9,8},{10,11... | collective-permute-start | bytes 49160 | tf_op jit(solution)/shard_map/ppermute | solution.py:276
  40.1 31.5 %all-to-all-start.1 = ((bf16[128,16,128]{2,1,0:T(8,128)(2,1)}), bf16[128,16,128]{2,1,0:T(8,128)(2,1)S(1)}, u32[]{:S(2)}, u32[]{:S(2)}) async-start(bf16[128,16,128]{2,1,0:T(8,128)(2,1)} %bitcast), calls=%async_computation.1 | async-start | bytes 1048576 | tf_op jit(solution)/shard_map/all_to_all | solution.py:277

commit v2 on v1

--- a/solution.py
+++ b/solution.py
@@ -7,16 +7,15 @@
 
 BLOCK = 8
 CAP = 640
-NZ = 8
-PLANE = 16
 DP = 128
 TOK = 1024
 RANK = 64
 DOCS = 8
-SLOT = 16
-SCORE_ROW = 8
-PLACE_ROW = 12
-OWNER_ROW = 13
+SLOT = 8
+HALF_BLOCK = 4
+SCORE_ROW = 4
+PLACE_ROW = 6
+OWNER_ROW = 7
 GROUP = 4
 LANES = 128
 VMEM = pltpu.VMEM
@@ -34,8 +33,27 @@
     return lax.broadcasted_iota(jnp.int32, shape, len(shape) - 1)
 
 
-def params():
-    return pltpu.CompilerParams(vmem_limit_bytes=48 * 1024 * 1024)
+def params(mib=48):
+    return pltpu.CompilerParams(vmem_limit_bytes=mib * 1024 * 1024)
+
+
+def copies_kernel(source_ref, out_ref, sem):
+    sends = [pltpu.make_async_copy(source_ref, out_ref.at[i], sem) for i in range(out_ref.shape[0])]
+    for send in sends:
+        send.start()
+    for send in sends:
+        send.wait()
+
+
+def copies(source, count):
+    return pl.pallas_call(
+        copies_kernel,
+        in_specs=[pl.BlockSpec(memory_space=VMEM)],
+        out_specs=pl.BlockSpec(memory_space=pltpu.HBM),
+        out_shape=jax.ShapeDtypeStruct((count,) + source.shape, source.dtype),
+        scratch_shapes=[pltpu.SemaphoreType.DMA],
+        compiler_params=params(60),
+    )(source)
 
 
 def partial_kernel(acts_ref, cot_ref, pin_ref, pout_ref, out_ref):
@@ -48,7 +66,7 @@
 
 
 def partial_features(acts, cotangent, proj_in, proj_out):
-    rows = 256
+    rows = 512
     return pl.pallas_call(
         partial_kernel,
         grid=(TOK // rows,),
@@ -60,7 +78,7 @@
         ],
         out_specs=pl.BlockSpec((rows, 2 * RANK), lambda i: (i, 0)),
         out_shape=jax.ShapeDtypeStruct((TOK, 2 * RANK), F32),
-        compiler_params=params(),
+        compiler_params=params(58),
         cost_estimate=pl.CostEstimate(flops=340_000_000, bytes_accessed=6_000_000, transcendentals=0),
     )(acts, cotangent, proj_in, proj_out)
 
@@ -145,87 +163,165 @@
     )(*pieces, queries)
 
 
-def pack_kernel(feat_ref, plan_ref, own_ref, other_ref, d0, d1, d2, d3, out_ref, tokens, stage):
+def place_kernel(feat_ref, plan_ref, out_ref, tokens):
+    me = lax.axis_index("mp")
     tokens[...] = feat_ref[...].astype(F32)
-    stage[...] = jnp.zeros_like(stage)
-    lane = lane_iota((LANES, LANES))
+    lane = lane_iota((DP, LANES))
     dest = plan_ref[:, 0:1]
     first = plan_ref[:, 1:2]
     send = jnp.where((dest == lane) & (first < CAP), 1.0, 0.0).astype(BF16)
-    for r in range(BLOCK):
-        rows = tokens[pl.ds(r, DP, stride=BLOCK), :].astype(BF16)
-        stage[pl.ds(r, DP, stride=SLOT), :] = dot(send, rows, TN)
+    for r in range(HALF_BLOCK):
+        rows = tokens[pl.ds(HALF_BLOCK * me + r, DP, stride=BLOCK), :].astype(BF16)
+        out_ref[pl.ds(r, DP, stride=SLOT), :] = dot(send, rows, TN)
+    for r in (SCORE_ROW, SCORE_ROW + 1, OWNER_ROW):
+        out_ref[pl.ds(r, DP, stride=SLOT), :] = jnp.zeros((DP, LANES), F32)
     place = jnp.broadcast_to(first // BLOCK + 1, (DP, LANES)).astype(F32).astype(BF16)
-    stage[pl.ds(PLACE_ROW, DP, stride=SLOT), :] = dot(send, place, TN)
-    scores = (own_ref[...] + other_ref[...]).astype(BF16).astype(F32)
-    short = lane_iota((DOCS, LANES))
-    marks = jnp.zeros((DP, LANES), F32)
-    for i, ref in enumerate((d0, d1, d2, d3)):
-        note = ref[:, 8 * LANES :].astype(F32)
-        owner, row = note[:DOCS], note[DOCS:]
-        hit = jnp.where(owner == short.astype(F32), 1.0, 0.0)
-        stage[pl.ds(SCORE_ROW + i, DP, stride=SLOT), :] = dot(
-            hit, scores[i * DOCS : (i + 1) * DOCS], TN
-        )
-        marks = marks + dot(hit, jnp.where(short // 32 == i, row, 0.0), TN)
-    stage[pl.ds(OWNER_ROW, DP, stride=SLOT), :] = marks
+    out_ref[pl.ds(PLACE_ROW, DP, stride=SLOT), :] = dot(send, place, TN)
+
+
+def place_rows(features, plan):
+    vmem = pl.BlockSpec(memory_space=VMEM)
+    return pl.pallas_call(
+        place_kernel,
+        in_specs=[vmem] * 2,
+        out_specs=vmem,
+        out_shape=jax.ShapeDtypeStruct((DP * SLOT, LANES), F32),
+        scratch_shapes=[VMEM((TOK, LANES), F32)],
+        compiler_params=params(),
+        cost_estimate=pl.CostEstimate(flops=20_000_000, bytes_accessed=900_000, transcendentals=0),
+    )(features, plan)
+
+
+def pack_kernel(base_ref, own_ref, other_ref, d0, d1, d2, d3, out_ref, stage):
+    me = lax.axis_index("mp")
+    stage[...] = base_ref[...]
+    total = (own_ref[...] + other_ref[...]).astype(BF16).astype(F32)
+    swapped = pltpu.roll(total, 64, 1)
+    short = lane_iota(total.shape)
+    piece = lax.broadcasted_iota(jnp.int32, total.shape, 0) // DOCS
+    left = (short < 64) & (piece % 2 == 0)
+    right = (short >= 64) & (piece % 2 == 1)
+    scores = jnp.where(
+        left,
+        jnp.where(me == 0, total, swapped),
+        jnp.where(right, jnp.where(me == 0, swapped, total), 0.0),
+    ).astype(BF16)
+    notes = [ref[:, 8 * LANES :].astype(F32) for ref in (d0, d1, d2, d3)]
+    owner = jnp.concatenate([note[:DOCS] for note in notes], axis=0)
+    row = jnp.concatenate([note[DOCS:] for note in notes], axis=0)
+    hit = jnp.where(owner == short.astype(F32), 1.0, 0.0).astype(BF16)
+    marks = jnp.where(short // 32 == piece, row, 0.0).astype(BF16)
+    two = 2 * DOCS
+    stage[pl.ds(SCORE_ROW, DP, stride=SLOT), :] = dot(hit[:two], scores[:two], TN)
+    stage[pl.ds(SCORE_ROW + 1, DP, stride=SLOT), :] = dot(hit[two:], scores[two:], TN)
+    stage[pl.ds(OWNER_ROW, DP, stride=SLOT), :] = dot(hit, marks, TN)
     out_ref[...] = stage[...].astype(BF16)
 
 
-def pack(features, plan, own, other, pieces):
+def pack(base, own, other, pieces):
     vmem = pl.BlockSpec(memory_space=VMEM)
     return pl.pallas_call(
         pack_kernel,
-        in_specs=[vmem] * 8,
+        in_specs=[vmem] * 7,
         out_specs=vmem,
         out_shape=jax.ShapeDtypeStruct((DP * SLOT, LANES), BF16),
-        scratch_shapes=[VMEM((TOK, LANES), F32), VMEM((DP * SLOT, LANES), F32)],
-        compiler_params=params(),
-        cost_estimate=pl.CostEstimate(flops=40_000_000, bytes_accessed=900_000, transcendentals=0),
-    )(features, plan, own, other, *pieces)
-
-
-def unpack_kernel(got_ref, balanced_ref, influence_ref, stage, rows):
+        scratch_shapes=[VMEM((DP * SLOT, LANES), F32)],
+        compiler_params=params(),
+        cost_estimate=pl.CostEstimate(flops=4_000_000, bytes_accessed=900_000, transcendentals=0),
+    )(base, own, other, *pieces)
+
+
+def split_kernel(got_ref, after_ref, rows_ref, notes_ref, stage):
     stage[...] = got_ref[...].astype(F32)
-    lane = lane_iota((DP, LANES))
-    place = stage[pl.ds(PLACE_ROW, DP, stride=SLOT), :]
-    put = jnp.where(place == (lane + 1).astype(F32), 1.0, 0.0).astype(BF16)
-    for r in range(BLOCK):
-        part = stage[pl.ds(r, DP, stride=SLOT), :].astype(BF16)
-        rows[pl.ds(r, CAP // BLOCK, stride=BLOCK), :] = dot(put, part, TN)[: CAP // BLOCK]
-    balanced_ref[...] = rows[...].astype(BF16)
-    me = lax.axis_index("mp")
-    count = 2 * PLANE
+    for r in range(HALF_BLOCK):
+        part = stage[pl.ds(r, DP, stride=SLOT), :]
+        rows_ref[r * DP : (r + 1) * DP, :] = part.astype(BF16)
+    for r in range(HALF_BLOCK, SLOT):
+        part = stage[pl.ds(r, DP, stride=SLOT), :]
+        notes_ref[(r - HALF_BLOCK) * DP : (r - HALF_BLOCK + 1) * DP, :] = part
+
+
+def split(got, after):
+    vmem = pl.BlockSpec(memory_space=VMEM)
+    return pl.pallas_call(
+        split_kernel,
+        in_specs=[vmem, pl.BlockSpec(memory_space=pl.ANY)],
+        out_specs=[vmem, vmem],
+        out_shape=[
+            jax.ShapeDtypeStruct((HALF_BLOCK * DP, LANES), BF16),
+            jax.ShapeDtypeStruct((HALF_BLOCK * DP, LANES), F32),
+        ],
+        scratch_shapes=[VMEM((DP * SLOT, LANES), F32)],
+        compiler_params=params(),
+        cost_estimate=pl.CostEstimate(flops=0, bytes_accessed=600_000, transcendentals=0),
+    )(got, after)
+
+
+def influence_kernel(notes_ref, influence_ref):
+    count = DP // GROUP
     short = lane_iota((count, LANES))
     want = jnp.where(short % 32 < DOCS, short % 32 + 1, -1).astype(F32)
-    for j in range(2):
-        base = pl.multiple_of((me * 2 + j) * count * SLOT, count * SLOT)
-        mark = stage[pl.ds(base + OWNER_ROW, count, stride=SLOT), :]
-        hit = jnp.where(mark == want, 1.0, 0.0).astype(BF16)
-        total = jnp.zeros((DOCS, LANES), F32)
-        for i in range(GROUP):
-            part = stage[pl.ds(base + SCORE_ROW + i, count, stride=SLOT), :].astype(BF16)
-            total = total + dot(hit, part, TN)[i * 32 : i * 32 + DOCS]
-        influence_ref[:, j * LANES : (j + 1) * LANES] = total
-
-
-def unpack(got):
-    vmem = pl.BlockSpec(memory_space=VMEM)
-    return pl.pallas_call(
-        unpack_kernel,
+    low = lane_iota((DOCS, LANES)) < 64
+    parts = []
+    for x in range(GROUP):
+
+        def taken(row):
+            return notes_ref[pl.ds((row - HALF_BLOCK) * DP + x, count, stride=GROUP), :]
+
+        hit = jnp.where(taken(OWNER_ROW) == want, 1.0, 0.0).astype(BF16)
+        one = dot(hit, taken(SCORE_ROW).astype(BF16), TN)
+        two = dot(hit, taken(SCORE_ROW + 1).astype(BF16), TN)
+        parts.append(
+            jnp.where(low, one[0:8] + two[64:72], one[32:40] + two[96:104]).astype(BF16)
+        )
+    source = lax.broadcasted_iota(jnp.int32, (GROUP * LANES, 2 * LANES), 0)
+    column = lane_iota((GROUP * LANES, 2 * LANES))
+    target = source % 64 // 4 * 16 + source // LANES * 4 + source % 4
+    order = jnp.where(column == target, 1.0, 0.0).astype(BF16)
+    influence_ref[...] = dot(jnp.concatenate(parts, axis=1), order)
+
+
+def influence_rows(notes):
+    vmem = pl.BlockSpec(memory_space=VMEM)
+    return pl.pallas_call(
+        influence_kernel,
         in_specs=[vmem],
-        out_specs=[vmem, vmem],
-        out_shape=[
-            jax.ShapeDtypeStruct((CAP, 2 * RANK), BF16),
-            jax.ShapeDtypeStruct((DOCS, 2 * LANES), F32),
-        ],
-        scratch_shapes=[VMEM((DP * SLOT, LANES), F32), VMEM((CAP, LANES), F32)],
+        out_specs=vmem,
+        out_shape=jax.ShapeDtypeStruct((DOCS, 2 * LANES), F32),
+        compiler_params=params(),
+        cost_estimate=pl.CostEstimate(flops=2_000_000, bytes_accessed=270_000, transcendentals=0),
+    )(notes)
+
+
+def balance_kernel(own_ref, other_ref, notes_ref, balanced_ref, rows):
+    me = lax.axis_index("mp")
+    lane = lane_iota((DP, LANES))
+    place = notes_ref[(PLACE_ROW - HALF_BLOCK) * DP : (PLACE_ROW - HALF_BLOCK + 1) * DP, :]
+    put = jnp.where(place == (lane + 1).astype(F32), 1.0, 0.0).astype(BF16)
+    blocks = CAP // BLOCK
+    for r in range(HALF_BLOCK):
+        near = own_ref[r * DP : (r + 1) * DP, :]
+        far = other_ref[r * DP : (r + 1) * DP, :]
+        rows[pl.ds(HALF_BLOCK * me + r, blocks, stride=BLOCK), :] = dot(put, near, TN)[:blocks]
+        rows[pl.ds(HALF_BLOCK * (1 - me) + r, blocks, stride=BLOCK), :] = dot(put, far, TN)[:blocks]
+    balanced_ref[...] = rows[...].astype(BF16)
+
+
+def balance(own, other, notes):
+    vmem = pl.BlockSpec(memory_space=VMEM)
+    return pl.pallas_call(
+        balance_kernel,
+        in_specs=[vmem, vmem, vmem],
+        out_specs=vmem,
+        out_shape=jax.ShapeDtypeStruct((CAP, 2 * RANK), BF16),
+        scratch_shapes=[VMEM((CAP, LANES), F32)],
         compiler_params=params(),
         cost_estimate=pl.CostEstimate(flops=40_000_000, bytes_accessed=700_000, transcendentals=0),
-    )(got)
-
-
-def grad_kernel(own_ref, other_ref, weight_ref, out_ref):
+    )(own, other, notes)
+
+
+def grad_kernel(own_ref, other_ref, weight_ref, out_ref, token_ref):
+    token_ref[...] = jnp.zeros_like(token_ref)
     half = own_ref.shape[1]
     me = lax.axis_index("mp")
     mine = weight_ref[pl.ds(pl.multiple_of(me * half, half), half), :]
@@ -244,8 +340,14 @@
             pl.BlockSpec((rows, own.shape[1]), lambda i: (i, 0)),
             pl.BlockSpec(weight.shape, lambda i: (0, 0)),
         ],
-        out_specs=pl.BlockSpec((rows, weight.shape[1]), lambda i: (i, 0)),
-        out_shape=jax.ShapeDtypeStruct((TOK, weight.shape[1]), BF16),
+        out_specs=[
+            pl.BlockSpec((rows, weight.shape[1]), lambda i: (i, 0)),
+            pl.BlockSpec((8, LANES), lambda i: (0, 0)),
+        ],
+        out_shape=[
+            jax.ShapeDtypeStruct((TOK, weight.shape[1]), BF16),
+            jax.ShapeDtypeStruct((8, LANES), F32),
+        ],
         compiler_params=params(),
         cost_estimate=pl.CostEstimate(flops=4_300_000_000, bytes_accessed=10_500_000, transcendentals=0),
     )(own, other, weight)
@@ -255,28 +357,30 @@
     acts, cotangent, value_weight, proj_in, proj_out, query_grads, lengths, plan, corpus, segments
 ):
     swap = [(0, 1), (1, 0)]
-    pair_size = 2 * PLANE
-    pairs = [[k * pair_size + i for i in range(pair_size)] for k in range(NZ // 2)]
+    members = DP // GROUP
+    columns = [[k + GROUP * i for i in range(members)] for k in range(GROUP)]
     other_cot = lax.ppermute(cotangent, "mp", swap)
     queries = lax.all_to_all(
-        jnp.broadcast_to(query_grads[None], (pair_size,) + query_grads.shape),
+        copies(query_grads, members),
         "dp",
         0,
         0,
         tiled=True,
-        axis_index_groups=pairs,
+        axis_index_groups=columns,
     ).reshape(LANES, -1)
     own = partial_features(acts, cotangent, proj_in, proj_out)
     features, docs = features_and_docs(own, lax.ppermute(own, "mp", swap), lengths, corpus)
     pieces = [docs]
     for i in range(1, GROUP):
-        step = 2 * PLANE * i
-        pieces.append(lax.ppermute(docs, "dp", [(s, (s + step) % DP) for s in range(DP)]))
+        row = [(s, s - s % GROUP + (s + i) % GROUP) for s in range(DP)]
+        pieces.append(lax.ppermute(docs, "dp", row))
     mine = partial_scores(pieces, queries)
-    packed = pack(features, plan, mine, lax.ppermute(mine, "mp", swap), pieces)
+    packed = pack(place_rows(features, plan), mine, lax.ppermute(mine, "mp", swap), pieces)
     got = lax.all_to_all(packed.reshape(DP, SLOT, LANES), "dp", 0, 0, tiled=True)
-    input_grad = input_gradient(cotangent, other_cot, value_weight)
-    balanced, influence = unpack(got.reshape(DP * SLOT, LANES))
+    input_grad, token = input_gradient(cotangent, other_cot, value_weight)
+    rows, notes = split(got.reshape(DP * SLOT, LANES), token)
+    balanced = balance(rows, lax.ppermute(rows, "mp", swap), notes)
+    influence = influence_rows(notes)
     return (input_grad, balanced, influence)
 
 

time: 73.5 us -> 66.8 us (0.909)
  waiting for transfers between devices: 16 us -> 10.7 us
  local copies, waits for them, and re-layouts: 6.04 us -> 2.34 us
  Pallas kernels: 16.5 us -> 19.8 us
  starting transfers between devices: 33.6 us -> 32.8 us
    all_to_all x1, waiting for transfers between devices: 10.5 us -> 5.44 us  [body(): lax.all_to_all(packed.reshape(DP, SLOT, LANES), 'dp', 0, 0, tiled=True)]
    ppermute x4 -> x5, waiting for transfers between devices: 4.04 us -> 0.74 us  [the longest x3 0.43 us: body(): pieces.append(lax.ppermute(docs, 'dp', row))]
    unnamed x13 -> x11, local copies, waits for them, and re-layouts: 4.16 us -> 1.18 us
    all_to_all x1, starting transfers between devices: 9.22 us -> 12.2 us  [body(): lax.all_to_all(copies(query_grads, members), 'dp', 0, 0, tiled=True, axis...]
    all_to_all x1, waiting for transfers between devices: 0.01 us -> 2.39 us  [body(): lax.all_to_all(copies(query_grads, members), 'dp', 0, 0, tiled=True, axis...]
    pallas_call x2 -> x6, Pallas kernels: 2.63 us -> 4.97 us  [the longest x1 1.54 us: copies(): pl.pallas_call(copies_kernel, in_specs=[pl.BlockSpec(memory_space=VMEM)],...]
    ppermute x4 -> x5, starting transfers between devices: 10.5 us -> 8.17 us  [the longest x3 3.68 us: body(): pieces.append(lax.ppermute(docs, 'dp', row))]
    broadcast_in_dim x1 -> x0, local copies, waits for them, and re-layouts: 1.76 us -> none  [body(): jnp.broadcast_to(query_grads[None], (pair_size,) + query_grads.shape)]
  transfers between devices with their start and end apart: 8 -> 9, of which waited for: 4 -> 5; matrix products, arithmetic and copies ran while one was open for 0% -> 2% of each run, Pallas kernels for 21% -> 26%
where the time goes in v2:
time: 66.8 us; the launch traced here: 66.4 us
  starting transfers between devices  32.8 us (49%)
  Pallas kernels  19.8 us (30%)
  waiting for transfers between devices  10.7 us (16%)
  local copies, waits for them, and re-layouts  2.34 us (4%)
  between operations  0.75 us (1%)
    all_to_all x1, starting transfers between devices, body(): lax.all_to_all(copies(query_grads, members), 'dp', 0, 0, tiled=True, axis...  12.2 us
    all_to_all x1, starting transfers between devices, body(): lax.all_to_all(packed.reshape(DP, SLOT, LANES), 'dp', 0, 0, tiled=True)  11.4 us
    pallas_call x1, Pallas kernels, input_gradient(): pl.pallas_call(grad_kernel, grid=(TOK // rows,), in_specs=[pl.BlockSpec((...  8.26 us
    all_to_all x1, waiting for transfers between devices, body(): lax.all_to_all(packed.reshape(DP, SLOT, LANES), 'dp', 0, 0, tiled=True)  5.44 us
    pallas_call x1, Pallas kernels, partial_features(): pl.pallas_call(partial_kernel, grid=(TOK // rows,), in_specs=[pl.BlockSpe...  4.72 us
    ppermute x3, starting transfers between devices, body(): pieces.append(lax.ppermute(docs, 'dp', row))  3.68 us
    ppermute x1, starting transfers between devices, body(): balanced = balance(rows, lax.ppermute(rows, 'mp', swap), notes)  2.48 us
    all_to_all x1, waiting for transfers between devices, body(): lax.all_to_all(copies(query_grads, members), 'dp', 0, 0, tiled=True, axis...  2.39 us
  transfers between devices with their start and end apart: 9, of which 5 were waited for; matrix products, arithmetic and copies ran while one was open for 2% of the time, Pallas kernels for 26%

profile of v2, /device:TPU:1, one launch (start us, length us, event | category | flops | bytes accessed | tf_op | source)
XLA Modules:
  0.0 66.4 jit_solution(9619710593686673661)
XLA Ops:
  0.6 0.0 copy-start.3
  0.6 0.0 copy-start.2
  0.7 1.5 %shard_map.116 = bf16[32,4,2048]{2,1,0:T(4,128)(2,1)} custom-call(bf16[4,2048]{1,0:T(4,128)(2,1)} %source_ref.1), custom_call_target="tpu_custom_call" | custom-call | tf_op jit(solution)/shard_map/pallas_call | solution.py:49
  2.2 12.2 %all-to-all-start = ((bf16[32,4,2048]{2,1,0:T(4,128)(2,1)}), bf16[32,4,2048]{2,1,0:T(4,128)(2,1)}, u32[]{:S(2)}, u32[]{:S(2)}) async-start(bf16[32,4,2048]{2,1,0:T(4,128)(2,1)} %shard_map.116), calls=%async_computation | async-start | bytes 1048576 | tf_op jit(solution)/shard_map/all_to_all | solution.py:363
  14.4 0.0 copy-start.4
  14.4 0.0 copy-start.1
  14.4 1.0 %collective-permute-start = (bf16[1024,512]{1,0:T(8,128)(2,1)}, bf16[1024,512]{1,0:T(8,128)(2,1)S(1)}, u32[]{:S(2)}, u32[]{:S(2)}) collective-permute-start(bf16[1024,512]{1,0:T(8,128)(2,1)} %cot_ref.1), channel_id=1, source_target_pairs={{0,1},{1,0},{2,3},{3,2},{4,5},{5,4},{6,7},{7,6},{8,9},{9,8},{10,11... | collective-permute-start | bytes 3145736 | tf_op jit(solution)/shard_map/ppermute | solution.py:362
  15.4 4.7 %shard_map.113.own_ref = f32[1024,128]{1,0:T(8,128)} custom-call(bf16[1024,2048]{1,0:T(8,128)(2,1)} %acts_ref.1, bf16[1024,512]{1,0:T(8,128)(2,1)} %cot_ref.1, bf16[64,2048]{1,0:T(8,128)(2,1)} %pin_ref.1, bf16[64,1024]{1,0:T(8,128)(2,1)} %pout_ref.1), custom_call_target="tpu_custom_call" | custom-call | flops 340000000 | bytes 6000000 | tf_op jit(solution)/shard_map/pallas_call | solution.py:70
  20.2 0.0 collective-permute-start.1
  20.2 2.1 %collective-permute-done.1.other_ref = f32[1024,128]{1,0:T(8,128)S(1)} collective-permute-done((f32[1024,128]{1,0:T(8,128)}, f32[1024,128]{1,0:T(8,128)S(1)}, u32[]{:S(2)}, u32[]{:S(2)}) %collective-permute-start.1) | collective-permute-done | bytes 524320 | tf_op jit(solution)/shard_map/ppermute | solution.py:372
  22.3 0.0 copy-done.3
  22.3 0.0 copy-done.2
  22.3 0.0 copy-start
  22.3 1.0 %copy-done = f32[1024,128]{1,0:T(8,128)S(1)} copy-done((f32[1024,128]{1,0:T(8,128)S(1)}, f32[1024,128]{1,0:T(8,128)}, u32[]{:S(2)}) %copy-start) | copy-done | bytes 524312
  23.3 1.2 %shard_map.114 = (bf16[1024,128]{1,0:T(8,128)(2,1)S(1)}, bf16[16,1152]{1,0:T(8,128)(2,1)S(1)}) custom-call(f32[1024,128]{1,0:T(8,128)S(1)} %copy-done, f32[1024,128]{1,0:T(8,128)S(1)} %collective-permute-done.1.other_ref, s32[8]{0:T(128)S(1)} %copy-done.2, s32[8]{0:T(128)S(1)} %copy-done.3), custom_call_target="tpu_custom_call" | custom-call | flops 200000000 | bytes 1500000 | tf_op jit(solution)/shard_map/pallas_call | solution.py:130
  24.6 2.6 %collective-permute-start.4 = (bf16[16,1152]{1,0:T(8,128)(2,1)S(1)}, bf16[16,1152]{1,0:T(8,128)(2,1)S(1)}, u32[]{:S(2)}, u32[]{:S(2)}) collective-permute-start(bf16[16,1152]{1,0:T(8,128)(2,1)S(1)} %get-tuple-element.11.d0), channel_id=1, source_target_pairs={{0,6},{2,0},{4,2},{6,4},{8,14},{10,8},{12,10},{14,12},{16,22},{18,... | collective-permute-start | bytes 110600 | tf_op jit(solution)/shard_map/ppermute | solution.py:376
  27.1 0.5 collective-permute-start.3
  27.6 0.6 collective-permute-start.2
  28.2 2.4 %all-to-all-done = bf16[32,4,2048]{2,1,0:T(4,128)(2,1)} async-done(((bf16[32,4,2048]{2,1,0:T(4,128)(2,1)}), bf16[32,4,2048]{2,1,0:T(4,128)(2,1)}, u32[]{:S(2)}, u32[]{:S(2)}) %all-to-all-start) | async-done | bytes 524320 | tf_op jit(solution)/shard_map/all_to_all | solution.py:363
  30.6 1.2 %reshape.15.queries_ref = bf16[128,2048]{1,0:T(8,128)(2,1)S(1)} reshape(bf16[32,4,2048]{2,1,0:T(4,128)(2,1)} %all-to-all-done) | data formatting | bytes 1048576 | tf_op jit(solution)/shard_map/reshape | solution.py:370
  31.8 0.0 collective-permute-done.4.d3
  31.8 0.0 collective-permute-done.3.d2
  31.8 0.4 collective-permute-done.2.d1
  32.2 0.6 shard_map.117.own_ref
  32.9 2.0 %collective-permute-start.5 = (f32[32,128]{1,0:T(8,128)S(1)}, f32[32,128]{1,0:T(8,128)S(1)}, u32[]{:S(2)}, u32[]{:S(2)}) collective-permute-start(f32[32,128]{1,0:T(8,128)S(1)} %shard_map.117.own_ref), channel_id=1, source_target_pairs={{0,1},{1,0},{2,3},{3,2},{4,5},{5,4},{6,7},{7,6},{8,9},{9,8},{10,11... | collective-permute-start | bytes 49160 | tf_op jit(solution)/shard_map/ppermute | solution.py:378
  34.9 0.0 copy-done.4
  34.9 0.1 copy.12.plan_ref
  35.0 0.4 shard_map.115.base_ref
  35.4 0.3 collective-permute-done.5.other_ref
  35.7 1.0 %shard_map.118 = bf16[1024,128]{1,0:T(8,128)(2,1)} custom-call(f32[1024,128]{1,0:T(8,128)S(1)} %shard_map.115.base_ref, f32[32,128]{1,0:T(8,128)S(1)} %shard_map.117.own_ref, f32[32,128]{1,0:T(8,128)S(1)} %collective-permute-done.5.other_ref, bf16[16,1152]{1,0:T(8,128)(2,1)S(1)} %get-tuple-element.11.d0, bf16[16,1152]{1,0:T(8,128)(2,1)S(1)} %collective-permute-done.2.d1, ...), custom_call_target="tpu_custom_call" | custom-call | flops 4000000 | bytes 900000 | tf_op jit(solution)/shard_map/pallas_call | solution.py:223
  36.7 11.4 %all-to-all-start.1 = ((bf16[128,8,128]{2,1,0:T(8,128)(2,1)}), bf16[128,8,128]{2,1,0:T(8,128)(2,1)S(1)}, u32[]{:S(2)}, u32[]{:S(2)}) async-start(bf16[128,8,128]{2,1,0:T(8,128)(2,1)} %bitcast), calls=%async_computation.1 | async-start | bytes 524288 | tf_op jit(solution)/shard_map/all_to_all | solution.py:379
  48.1 0.0 collective-permute-done.other_ref
  48.1 0.0 copy-done.1
  48.1 8.3 %shard_map.112 = (bf16[1024,2048]{1,0:T(8,128)(2,1)}, f32[8,128]{1,0:T(8,128)S(1)}) custom-call(bf16[1024,512]{1,0:T(8,128)(2,1)S(1)} %copy-done.1, bf16[1024,512]{1,0:T(8,128)(2,1)S(1)} %collective-permute-done.other_ref, bf16[1024,2048]{1,0:T(8,128)(2,1)} %weight_ref.1), custom_call_target="tpu_custom_call" | custom-call | flops 4300000256 | bytes 10500000 | tf_op jit(solution)/shard_map/pallas_call | solution.py:335
  56.4 5.4 %all-to-all-done.1 = bf16[128,8,128]{2,1,0:T(8,128)(2,1)S(1)} async-done(((bf16[128,8,128]{2,1,0:T(8,128)(2,1)}), bf16[128,8,128]{2,1,0:T(8,128)(2,1)S(1)}, u32[]{:S(2)}, u32[]{:S(2)}) %all-to-all-start.1) | async-done | bytes 262176 | tf_op jit(solution)/shard_map/all_to_all | solution.py:379
  61.8 0.1 shard_map.119
  61.9 2.5 %collective-permute-start.6 = (bf16[512,128]{1,0:T(8,128)(2,1)S(1)}, bf16[512,128]{1,0:T(8,128)(2,1)S(1)}, u32[]{:S(2)}, u32[]{:S(2)}) collective-permute-start(bf16[512,128]{1,0:T(8,128)(2,1)S(1)} %get-tuple-element.13.own_ref), channel_id=1, source_target_pairs={{0,1},{1,0},{2,3},{3,2},{4,5},{5,4},{6,7},{7,6},{8,9},{9,8},{10,11... | collective-permute-start | bytes 393224 | tf_op jit(solution)/shard_map/ppermute | solution.py:382
  64.4 1.0 %shard_map.121 = f32[8,256]{1,0:T(8,128)} custom-call(f32[512,128]{1,0:T(8,128)S(1)} %get-tuple-element.14.notes_ref), custom_call_target="tpu_custom_call" | custom-call | flops 2000000 | bytes 270000 | tf_op jit(solution)/shard_map/pallas_call | solution.py:286
  65.4 0.0 collective-permute-done.6.other_ref
  65.4 1.0 %shard_map.120 = bf16[640,128]{1,0:T(8,128)(2,1)} custom-call(bf16[512,128]{1,0:T(8,128)(2,1)S(1)} %get-tuple-element.13.own_ref, bf16[512,128]{1,0:T(8,128)(2,1)S(1)} %collective-permute-done.6.other_ref, f32[512,128]{1,0:T(8,128)S(1)} %get-tuple-element.14.notes_ref), custom_call_target="tpu_custom_call" | custom-call | flops 40000000 | bytes 700000 | tf_op jit(solution)/shard_map/pallas_call | solution.py:312
Async XLA Ops:
  0.6 21.7 %copy-start.3 = (s32[8]{0:T(128)S(1)}, s32[8]{0:T(128)}, u32[]{:S(2)}) copy-start(s32[8]{0:T(128)} %corpus_ref.1) | copy-start | bytes 100
  0.6 21.7 %copy-start.2 = (s32[8]{0:T(128)S(1)}, s32[8]{0:T(128)}, u32[]{:S(2)}) copy-start(s32[8]{0:T(128)} %lengths_ref.1) | copy-start | bytes 100
  2.2 28.4 %all-to-all-start = ((bf16[32,4,2048]{2,1,0:T(4,128)(2,1)}), bf16[32,4,2048]{2,1,0:T(4,128)(2,1)}, u32[]{:S(2)}, u32[]{:S(2)}) async-start(bf16[32,4,2048]{2,1,0:T(4,128)(2,1)} %shard_map.116), calls=%async_computation | async-start | bytes 1048576 | tf_op jit(solution)/shard_map/all_to_all | solution.py:363
  14.4 20.5 %copy-start.4 = (s32[128,2]{0,1:T(2,128)S(1)}, s32[128,2]{0,1:T(2,128)}, u32[]{:S(2)}) copy-start(s32[128,2]{0,1:T(2,128)} %param.17) | copy-start | bytes 3076
  14.4 33.7 %copy-start.1 = (bf16[1024,512]{1,0:T(8,128)(2,1)S(1)}, bf16[1024,512]{1,0:T(8,128)(2,1)}, u32[]{:S(2)}) copy-start(bf16[1024,512]{1,0:T(8,128)(2,1)} %cot_ref.1) | copy-start | bytes 3145732
  14.4 33.7 %collective-permute-start = (bf16[1024,512]{1,0:T(8,128)(2,1)}, bf16[1024,512]{1,0:T(8,128)(2,1)S(1)}, u32[]{:S(2)}, u32[]{:S(2)}) collective-permute-start(bf16[1024,512]{1,0:T(8,128)(2,1)} %cot_ref.1), channel_id=1, source_target_pairs={{0,1},{1,0},{2,3},{3,2},{4,5},{5,4},{6,7},{7,6},{8,9},{9,8},{10,11... | collective-permute-start | bytes 3145736 | tf_op jit(solution)/shard_map/ppermute | solution.py:362
  20.2 2.1 %collective-permute-start.1 = (f32[1024,128]{1,0:T(8,128)}, f32[1024,128]{1,0:T(8,128)S(1)}, u32[]{:S(2)}, u32[]{:S(2)}) collective-permute-start(f32[1024,128]{1,0:T(8,128)} %shard_map.113.own_ref), channel_id=1, source_target_pairs={{0,1},{1,0},{2,3},{3,2},{4,5},{5,4},{6,7},{7,6},{8,9},{9,8},{10,11... | collective-permute-start | bytes 1572872 | tf_op jit(solution)/shard_map/ppermute | solution.py:372
  22.3 1.0 %copy-start = (f32[1024,128]{1,0:T(8,128)S(1)}, f32[1024,128]{1,0:T(8,128)}, u32[]{:S(2)}) copy-start(f32[1024,128]{1,0:T(8,128)} %shard_map.113.own_ref) | copy-start | bytes 1572868
  24.6 7.2 %collective-permute-start.4 = (bf16[16,1152]{1,0:T(8,128)(2,1)S(1)}, bf16[16,1152]{1,0:T(8,128)(2,1)S(1)}, u32[]{:S(2)}, u32[]{:S(2)}) collective-permute-start(bf16[16,1152]{1,0:T(8,128)(2,1)S(1)} %get-tuple-element.11.d0), channel_id=1, source_target_pairs={{0,6},{2,0},{4,2},{6,4},{8,14},{10,8},{12,10},{14,12},{16,22},{18,... | collective-permute-start | bytes 110600 | tf_op jit(solution)/shard_map/ppermute | solution.py:376
  27.1 4.7 %collective-permute-start.3 = (bf16[16,1152]{1,0:T(8,128)(2,1)S(1)}, bf16[16,1152]{1,0:T(8,128)(2,1)S(1)}, u32[]{:S(2)}, u32[]{:S(2)}) collective-permute-start(bf16[16,1152]{1,0:T(8,128)(2,1)S(1)} %get-tuple-element.11.d0), channel_id=1, source_target_pairs={{0,4},{2,6},{4,0},{6,2},{8,12},{10,14},{12,8},{14,10},{16,20},{18,... | collective-permute-start | bytes 110600 | tf_op jit(solution)/shard_map/ppermute | solution.py:376
  27.6 4.6 %collective-permute-start.2 = (bf16[16,1152]{1,0:T(8,128)(2,1)S(1)}, bf16[16,1152]{1,0:T(8,128)(2,1)S(1)}, u32[]{:S(2)}, u32[]{:S(2)}) collective-permute-start(bf16[16,1152]{1,0:T(8,128)(2,1)S(1)} %get-tuple-element.11.d0), channel_id=1, source_target_pairs={{0,2},{2,4},{4,6},{6,0},{8,10},{10,12},{12,14},{14,8},{16,18},{18,... | collective-permute-start | bytes 110600 | tf_op jit(solution)/shard_map/ppermute | solution.py:376
  32.9 2.8 %collective-permute-start.5 = (f32[32,128]{1,0:T(8,128)S(1)}, f32[32,128]{1,0:T(8,128)S(1)}, u32[]{:S(2)}, u32[]{:S(2)}) collective-permute-start(f32[32,128]{1,0:T(8,128)S(1)} %shard_map.117.own_ref), channel_id=1, source_target_pairs={{0,1},{1,0},{2,3},{3,2},{4,5},{5,4},{6,7},{7,6},{8,9},{9,8},{10,11... | collective-permute-start | bytes 49160 | tf_op jit(solution)/shard_map/ppermute | solution.py:378
  36.7 25.1 %all-to-all-start.1 = ((bf16[128,8,128]{2,1,0:T(8,128)(2,1)}), bf16[128,8,128]{2,1,0:T(8,128)(2,1)S(1)}, u32[]{:S(2)}, u32[]{:S(2)}) async-start(bf16[128,8,128]{2,1,0:T(8,128)(2,1)} %bitcast), calls=%async_computation.1 | async-start | bytes 524288 | tf_op jit(solution)/shard_map/all_to_all | solution.py:379
  61.9 3.5 %collective-permute-start.6 = (bf16[512,128]{1,0:T(8,128)(2,1)S(1)}, bf16[512,128]{1,0:T(8,128)(2,1)S(1)}, u32[]{:S(2)}, u32[]{:S(2)}) collective-permute-start(bf16[512,128]{1,0:T(8,128)(2,1)S(1)} %get-tuple-element.13.own_ref), channel_id=1, source_target_pairs={{0,1},{1,0},{2,3},{3,2},{4,5},{5,4},{6,7},{7,6},{8,9},{9,8},{10,11... | collective-permute-start | bytes 393224 | tf_op jit(solution)/shard_map/ppermute | solution.py:382

commit v3 on v2

--- a/solution.py
+++ b/solution.py
@@ -17,6 +17,7 @@
 PLACE_ROW = 6
 OWNER_ROW = 7
 GROUP = 4
+CHUNKS = ((0, 256), (256, 256), (512, 256), (768, 256))
 LANES = 128
 VMEM = pltpu.VMEM
 F32 = jnp.float32
@@ -37,8 +38,11 @@
     return pltpu.CompilerParams(vmem_limit_bytes=mib * 1024 * 1024)
 
 
-def copies_kernel(source_ref, out_ref, sem):
-    sends = [pltpu.make_async_copy(source_ref, out_ref.at[i], sem) for i in range(out_ref.shape[0])]
+def copies_kernel(source_ref, out_ref, held, sem, out_sem):
+    load = pltpu.make_async_copy(source_ref, held, sem)
+    load.start()
+    load.wait()
+    sends = [pltpu.make_async_copy(held, out_ref.at[i], out_sem) for i in range(out_ref.shape[0])]
     for send in sends:
         send.start()
     for send in sends:
@@ -46,47 +50,81 @@
 
 
 def copies(source, count):
+    hbm = pl.BlockSpec(memory_space=pl.ANY)
     return pl.pallas_call(
         copies_kernel,
-        in_specs=[pl.BlockSpec(memory_space=VMEM)],
-        out_specs=pl.BlockSpec(memory_space=pltpu.HBM),
-        out_shape=jax.ShapeDtypeStruct((count,) + source.shape, source.dtype),
-        scratch_shapes=[pltpu.SemaphoreType.DMA],
-        compiler_params=params(60),
-    )(source)
-
-
-def partial_kernel(acts_ref, cot_ref, pin_ref, pout_ref, out_ref):
+        in_specs=[hbm],
+        out_specs=hbm,
+        out_shape=pltpu.HBM((count,) + source.shape, source.dtype),
+        scratch_shapes=[
+            VMEM(source.shape, source.dtype),
+            pltpu.SemaphoreType.DMA,
+            pltpu.SemaphoreType.DMA,
+        ],
+        compiler_params=params(4),
+    )(pltpu.with_memory_space_constraint(source, pltpu.HBM))
+
+
+def partial_kernel(
+    acts_ref, cot_ref, pin_ref, pout_ref, out_ref, acts, cot, pin, pout, in_sems
+):
     half = cot_ref.shape[1]
     me = lax.axis_index("mp")
-    pout = pout_ref[:, pl.ds(pl.multiple_of(me * half, half), half)]
-    low = dot(acts_ref[...], pin_ref[...], NT)
-    out = dot(cot_ref[...], pout, NT)
-    out_ref[...] = jnp.concatenate([low, out], axis=1)
+    weights = [
+        pltpu.make_async_copy(pin_ref, pin, in_sems.at[0]),
+        pltpu.make_async_copy(
+            pout_ref.at[:, pl.ds(pl.multiple_of(me * half, half), half)], pout, in_sems.at[1]
+        ),
+    ]
+    loads = []
+    for i, (at, rows) in enumerate(CHUNKS):
+        span = pl.ds(at, rows)
+        loads.append(
+            [
+                pltpu.make_async_copy(acts_ref.at[span], acts.at[span], in_sems.at[2 + 2 * i]),
+                pltpu.make_async_copy(cot_ref.at[span], cot.at[span], in_sems.at[3 + 2 * i]),
+            ]
+        )
+    for copy in weights + loads[0] + loads[1]:
+        copy.start()
+    for copy in weights:
+        copy.wait()
+    for i, (at, rows) in enumerate(CHUNKS):
+        span = pl.ds(at, rows)
+        for copy in loads[i]:
+            copy.wait()
+        if i + 2 < len(CHUNKS):
+            for copy in loads[i + 2]:
+                copy.start()
+        low = dot(acts[span, :], pin[...], NT)
+        high = dot(cot[span, :], pout[...], NT)
+        out_ref[span, :] = jnp.concatenate([low, high], axis=1)
 
 
 def partial_features(acts, cotangent, proj_in, proj_out):
-    rows = 512
+    hbm = pl.BlockSpec(memory_space=pl.ANY)
+    half = cotangent.shape[1]
     return pl.pallas_call(
         partial_kernel,
-        grid=(TOK // rows,),
-        in_specs=[
-            pl.BlockSpec((rows, acts.shape[1]), lambda i: (i, 0)),
-            pl.BlockSpec((rows, cotangent.shape[1]), lambda i: (i, 0)),
-            pl.BlockSpec(proj_in.shape, lambda i: (0, 0)),
-            pl.BlockSpec(proj_out.shape, lambda i: (0, 0)),
-        ],
-        out_specs=pl.BlockSpec((rows, 2 * RANK), lambda i: (i, 0)),
-        out_shape=jax.ShapeDtypeStruct((TOK, 2 * RANK), F32),
-        compiler_params=params(58),
+        in_specs=[hbm] * 4,
+        out_specs=pl.BlockSpec(memory_space=VMEM),
+        out_shape=VMEM((TOK, 2 * RANK), F32),
+        scratch_shapes=[
+            VMEM(acts.shape, BF16),
+            VMEM(cotangent.shape, BF16),
+            VMEM(proj_in.shape, BF16),
+            VMEM((RANK, half), BF16),
+            pltpu.SemaphoreType.DMA((2 + 2 * len(CHUNKS),)),
+        ],
+        compiler_params=params(16),
         cost_estimate=pl.CostEstimate(flops=340_000_000, bytes_accessed=6_000_000, transcendentals=0),
-    )(acts, cotangent, proj_in, proj_out)
+    )(*(pltpu.with_memory_space_constraint(x, pltpu.HBM) for x in (acts, cotangent, proj_in, proj_out)))
 
 
 def docs_kernel(own_ref, other_ref, lengths_ref, corpus_ref, feat_ref, docs_ref, scr):
     half = RANK // 2
     me = lax.axis_index("mp")
-    feat = (own_ref[...] + other_ref[...]).astype(BF16)
+    feat = (own_ref[...].astype(F32) + other_ref[...].astype(F32)).astype(BF16)
     feat_ref[...] = feat
     row = lax.broadcasted_iota(jnp.int32, (LANES, 3 * LANES), 0)
     col = lane_iota((LANES, 3 * LANES))
@@ -143,7 +181,8 @@
 
 def score_kernel(d0, d1, d2, d3, queries_ref, out_ref):
     width = 8 * LANES
-    left, right = queries_ref[:, :width], queries_ref[:, width:]
+    rows = queries_ref[...].reshape(LANES, 2 * width)
+    left, right = rows[:, :width], rows[:, width:]
     for i, ref in enumerate((d0, d1, d2, d3)):
         piece = ref[:, :width]
         out_ref[i * DOCS : (i + 1) * DOCS, :] = (
@@ -169,7 +208,7 @@
     lane = lane_iota((DP, LANES))
     dest = plan_ref[:, 0:1]
     first = plan_ref[:, 1:2]
-    send = jnp.where((dest == lane) & (first < CAP), 1.0, 0.0).astype(BF16)
+    send = jnp.where((dest == DP - 1 - lane) & (first < CAP), 1.0, 0.0).astype(BF16)
     for r in range(HALF_BLOCK):
         rows = tokens[pl.ds(HALF_BLOCK * me + r, DP, stride=BLOCK), :].astype(BF16)
         out_ref[pl.ds(r, DP, stride=SLOT), :] = dot(send, rows, TN)
@@ -209,7 +248,7 @@
     notes = [ref[:, 8 * LANES :].astype(F32) for ref in (d0, d1, d2, d3)]
     owner = jnp.concatenate([note[:DOCS] for note in notes], axis=0)
     row = jnp.concatenate([note[DOCS:] for note in notes], axis=0)
-    hit = jnp.where(owner == short.astype(F32), 1.0, 0.0).astype(BF16)
+    hit = jnp.where(owner == (DP - 1 - short).astype(F32), 1.0, 0.0).astype(BF16)
     marks = jnp.where(short // 32 == piece, row, 0.0).astype(BF16)
     two = 2 * DOCS
     stage[pl.ds(SCORE_ROW, DP, stride=SLOT), :] = dot(hit[:two], scores[:two], TN)
@@ -276,7 +315,7 @@
         )
     source = lax.broadcasted_iota(jnp.int32, (GROUP * LANES, 2 * LANES), 0)
     column = lane_iota((GROUP * LANES, 2 * LANES))
-    target = source % 64 // 4 * 16 + source // LANES * 4 + source % 4
+    target = source % 64 // 4 * 16 + (GROUP - 1 - source // LANES) * 4 + source % 4
     order = jnp.where(column == target, 1.0, 0.0).astype(BF16)
     influence_ref[...] = dot(jnp.concatenate(parts, axis=1), order)
 
@@ -321,28 +360,28 @@
 
 
 def grad_kernel(own_ref, other_ref, weight_ref, out_ref, token_ref):
-    token_ref[...] = jnp.zeros_like(token_ref)
     half = own_ref.shape[1]
     me = lax.axis_index("mp")
     mine = weight_ref[pl.ds(pl.multiple_of(me * half, half), half), :]
     theirs = weight_ref[pl.ds(pl.multiple_of((1 - me) * half, half), half), :]
     total = dot(own_ref[...], mine) + dot(other_ref[...], theirs)
     out_ref[...] = total.astype(BF16)
+    token_ref[...] = jnp.zeros_like(token_ref)
 
 
 def input_gradient(own, other, weight):
-    rows = 256
+    columns = 512
     return pl.pallas_call(
         grad_kernel,
-        grid=(TOK // rows,),
+        grid=(weight.shape[1] // columns,),
         in_specs=[
-            pl.BlockSpec((rows, own.shape[1]), lambda i: (i, 0)),
-            pl.BlockSpec((rows, own.shape[1]), lambda i: (i, 0)),
-            pl.BlockSpec(weight.shape, lambda i: (0, 0)),
+            pl.BlockSpec(own.shape, lambda j: (0, 0)),
+            pl.BlockSpec(other.shape, lambda j: (0, 0)),
+            pl.BlockSpec((weight.shape[0], columns), lambda j: (0, j)),
         ],
         out_specs=[
-            pl.BlockSpec((rows, weight.shape[1]), lambda i: (i, 0)),
-            pl.BlockSpec((8, LANES), lambda i: (0, 0)),
+            pl.BlockSpec((TOK, columns), lambda j: (0, j)),
+            pl.BlockSpec((8, LANES), lambda j: (0, 0)),
         ],
         out_shape=[
             jax.ShapeDtypeStruct((TOK, weight.shape[1]), BF16),
@@ -367,16 +406,22 @@
         0,
         tiled=True,
         axis_index_groups=columns,
-    ).reshape(LANES, -1)
+    )
     own = partial_features(acts, cotangent, proj_in, proj_out)
     features, docs = features_and_docs(own, lax.ppermute(own, "mp", swap), lengths, corpus)
     pieces = [docs]
     for i in range(1, GROUP):
-        row = [(s, s - s % GROUP + (s + i) % GROUP) for s in range(DP)]
-        pieces.append(lax.ppermute(docs, "dp", row))
+        pieces.append(lax.ppermute(docs, "dp", [(s, s ^ i) for s in range(DP)]))
     mine = partial_scores(pieces, queries)
     packed = pack(place_rows(features, plan), mine, lax.ppermute(mine, "mp", swap), pieces)
-    got = lax.all_to_all(packed.reshape(DP, SLOT, LANES), "dp", 0, 0, tiled=True)
+    got = lax.all_to_all(
+        packed.reshape(DP, SLOT, LANES),
+        "dp",
+        0,
+        0,
+        tiled=True,
+        axis_index_groups=[list(range(DP - 1, -1, -1))],
+    )
     input_grad, token = input_gradient(cotangent, other_cot, value_weight)
     rows, notes = split(got.reshape(DP * SLOT, LANES), token)
     balanced = balance(rows, lax.ppermute(rows, "mp", swap), notes)

time: 66.8 us -> 60.8 us (0.910)
  waiting for transfers between devices: 10.7 us -> 6.83 us
  local copies, waits for them, and re-layouts: 2.34 us -> 0.13 us
  Pallas kernels: 19.8 us -> 18.8 us
  starting transfers between devices: 32.8 us -> 33.8 us
    all_to_all x1, waiting for transfers between devices: 5.44 us -> 0.41 us  [body(): lax.all_to_all(packed.reshape(DP, SLOT, LANES), 'dp', 0, 0, tiled=True, a...]
    ppermute x3, waiting for transfers between devices: 0.43 us -> 3.83 us  [body(): pieces.append(lax.ppermute(docs, 'dp', [(s, s ^ i) for s in range(DP)]))]
    all_to_all x1, waiting for transfers between devices: 2.39 us -> 0.39 us  [body(): lax.all_to_all(copies(query_grads, members), 'dp', 0, 0, tiled=True, axis...]
    all_to_all x1, starting transfers between devices: 11.4 us -> 12.6 us  [body(): lax.all_to_all(packed.reshape(DP, SLOT, LANES), 'dp', 0, 0, tiled=True, a...]
    reshape x1 -> x0, local copies, waits for them, and re-layouts: 1.16 us -> none  [body(): queries = lax.all_to_all(copies(query_grads, members), 'dp', 0, 0, tiled=...]
    unnamed x11 -> x9, local copies, waits for them, and re-layouts: 1.18 us -> 0.13 us
    pallas_call x3, Pallas kernels: 14.5 us -> 13.6 us  [the longest x1 7.65 us: input_gradient(): pl.pallas_call(grad_kernel, grid=(weight.shape[1] // columns,), in_specs=...]
  transfers between devices with their start and end apart: 9 -> 9, of which waited for: 5 -> 6; matrix products, arithmetic and copies ran while one was open for 2% -> 0% of each run, Pallas kernels for 26% -> 27%
where the time goes in v3:
time: 60.8 us; the launch traced here: 60.4 us
  starting transfers between devices  33.8 us (56%)
  Pallas kernels  18.8 us (31%)
  waiting for transfers between devices  6.83 us (11%)
  between operations  0.74 us (1%)
    all_to_all x1, starting transfers between devices, body(): lax.all_to_all(packed.reshape(DP, SLOT, LANES), 'dp', 0, 0, tiled=True, a...  12.6 us
    all_to_all x1, starting transfers between devices, body(): lax.all_to_all(copies(query_grads, members), 'dp', 0, 0, tiled=True, axis...  12 us
    pallas_call x1, Pallas kernels, input_gradient(): pl.pallas_call(grad_kernel, grid=(weight.shape[1] // columns,), in_specs=...  7.65 us
    pallas_call x1, Pallas kernels, partial_features(): pl.pallas_call(partial_kernel, in_specs=[hbm] * 4, out_specs=pl.BlockSpec...  4.4 us
    ppermute x3, waiting for transfers between devices, body(): pieces.append(lax.ppermute(docs, 'dp', [(s, s ^ i) for s in range(DP)]))  3.83 us
    ppermute x3, starting transfers between devices, body(): pieces.append(lax.ppermute(docs, 'dp', [(s, s ^ i) for s in range(DP)]))  3.34 us
    ppermute x1, starting transfers between devices, body(): lax.ppermute(mine, 'mp', swap)  2.41 us
    ppermute x1, starting transfers between devices, body(): balanced = balance(rows, lax.ppermute(rows, 'mp', swap), notes)  2.24 us
  transfers between devices with their start and end apart: 9, of which 6 were waited for; matrix products, arithmetic and copies ran while one was open for 0% of the time, Pallas kernels for 27%

profile of v3, /device:TPU:1, one launch (start us, length us, event | category | flops | bytes accessed | tf_op | source)
XLA Modules:
  0.0 60.4 jit_solution(6659031901123569602)
XLA Ops:
  0.6 0.0 copy-start.2
  0.6 0.0 copy-start.1
  0.7 1.5 %shard_map.116 = bf16[32,4,2048]{2,1,0:T(4,128)(2,1)} custom-call(bf16[4,2048]{1,0:T(4,128)(2,1)} %source_ref.1), custom_call_target="tpu_custom_call" | custom-call | tf_op jit(solution)/shard_map/pallas_call | solution.py:54
  2.2 12.0 %all-to-all-start = ((bf16[32,4,2048]{2,1,0:T(4,128)(2,1)}), bf16[32,4,2048]{2,1,0:T(4,128)(2,1)S(1)}, u32[]{:S(2)}, u32[]{:S(2)}) async-start(bf16[32,4,2048]{2,1,0:T(4,128)(2,1)} %shard_map.116), calls=%async_computation | async-start | bytes 1048576 | tf_op jit(solution)/shard_map/all_to_all | solution.py:402
  14.2 0.0 copy-start.3
  14.2 0.0 copy-start
  14.3 1.0 %collective-permute-start = (bf16[1024,512]{1,0:T(8,128)(2,1)}, bf16[1024,512]{1,0:T(8,128)(2,1)S(1)}, u32[]{:S(2)}, u32[]{:S(2)}) collective-permute-start(bf16[1024,512]{1,0:T(8,128)(2,1)} %cot_ref.1), channel_id=1, source_target_pairs={{0,1},{1,0},{2,3},{3,2},{4,5},{5,4},{6,7},{7,6},{8,9},{9,8},{10,11... | collective-permute-start | bytes 3145736 | tf_op jit(solution)/shard_map/ppermute | solution.py:401
  15.3 4.4 %shard_map.113.own_ref = f32[1024,128]{1,0:T(8,128)S(1)} custom-call(bf16[1024,2048]{1,0:T(8,128)(2,1)} %acts_ref.1, bf16[1024,512]{1,0:T(8,128)(2,1)} %cot_ref.1, bf16[64,2048]{1,0:T(8,128)(2,1)} %pin_ref.1, bf16[64,1024]{1,0:T(8,128)(2,1)} %pout_ref.1), custom_call_target="tpu_custom_call" | custom-call | flops 340000000 | bytes 6000000 | tf_op jit(solution)/shard_map/pallas_call | solution.py:107
  19.7 0.1 collective-permute-start.1
  19.8 1.9 %collective-permute-done.1.other_ref = f32[1024,128]{1,0:T(8,128)S(1)} collective-permute-done((f32[1024,128]{1,0:T(8,128)S(1)}, f32[1024,128]{1,0:T(8,128)S(1)}, u32[]{:S(2)}, u32[]{:S(2)}) %collective-permute-start.1) | collective-permute-done | bytes 524320 | tf_op jit(solution)/shard_map/ppermute | solution.py:411
  21.7 0.0 copy-done.2
  21.7 0.0 copy-done.1
  21.7 1.2 %shard_map.114 = (bf16[1024,128]{1,0:T(8,128)(2,1)S(1)}, bf16[16,1152]{1,0:T(8,128)(2,1)S(1)}) custom-call(f32[1024,128]{1,0:T(8,128)S(1)} %shard_map.113.own_ref, f32[1024,128]{1,0:T(8,128)S(1)} %collective-permute-done.1.other_ref, s32[8]{0:T(128)S(1)} %copy-done.1, s32[8]{0:T(128)S(1)} %copy-done.2), custom_call_target="tpu_custom_call" | custom-call | flops 200000000 | bytes 1500000 | tf_op jit(solution)/shard_map/pallas_call | solution.py:168
  22.9 2.6 %collective-permute-start.4 = (bf16[16,1152]{1,0:T(8,128)(2,1)S(1)}, bf16[16,1152]{1,0:T(8,128)(2,1)S(1)}, u32[]{:S(2)}, u32[]{:S(2)}) collective-permute-start(bf16[16,1152]{1,0:T(8,128)(2,1)S(1)} %get-tuple-element.11.d0), channel_id=1, source_target_pairs={{0,6},{2,4},{4,2},{6,0},{8,14},{10,12},{12,10},{14,8},{16,22},{18,... | collective-permute-start | bytes 110600 | tf_op jit(solution)/shard_map/ppermute | solution.py:414
  25.5 0.5 collective-permute-start.3
  26.0 0.3 collective-permute-start.2
  26.3 1.1 %collective-permute-done.4.d3 = bf16[16,1152]{1,0:T(8,128)(2,1)S(1)} collective-permute-done((bf16[16,1152]{1,0:T(8,128)(2,1)S(1)}, bf16[16,1152]{1,0:T(8,128)(2,1)S(1)}, u32[]{:S(2)}, u32[]{:S(2)}) %collective-permute-start.4) | collective-permute-done | bytes 36896 | tf_op jit(solution)/shard_map/ppermute | solution.py:414
  27.3 2.8 %collective-permute-done.3.d2 = bf16[16,1152]{1,0:T(8,128)(2,1)S(1)} collective-permute-done((bf16[16,1152]{1,0:T(8,128)(2,1)S(1)}, bf16[16,1152]{1,0:T(8,128)(2,1)S(1)}, u32[]{:S(2)}, u32[]{:S(2)}) %collective-permute-start.3) | collective-permute-done | bytes 36896 | tf_op jit(solution)/shard_map/ppermute | solution.py:414
  30.1 0.0 collective-permute-done.2.d1
  30.1 0.4 all-to-all-done.queries_ref
  30.5 0.6 %shard_map.117.own_ref = f32[32,128]{1,0:T(8,128)S(1)} custom-call(bf16[16,1152]{1,0:T(8,128)(2,1)S(1)} %get-tuple-element.11.d0, bf16[16,1152]{1,0:T(8,128)(2,1)S(1)} %collective-permute-done.2.d1, bf16[16,1152]{1,0:T(8,128)(2,1)S(1)} %collective-permute-done.3.d2, bf16[16,1152]{1,0:T(8,128)(2,1)S(1)} %collective-permute-done.4.d3, ...), custom_call_target="tpu_custom_call" | custom-call | flops 17000000 | bytes 700000 | tf_op jit(solution)/shard_map/pallas_call | solution.py:195
  31.1 2.4 %collective-permute-start.5 = (f32[32,128]{1,0:T(8,128)S(1)}, f32[32,128]{1,0:T(8,128)S(1)}, u32[]{:S(2)}, u32[]{:S(2)}) collective-permute-start(f32[32,128]{1,0:T(8,128)S(1)} %shard_map.117.own_ref), channel_id=1, source_target_pairs={{0,1},{1,0},{2,3},{3,2},{4,5},{5,4},{6,7},{7,6},{8,9},{9,8},{10,11... | collective-permute-start | bytes 49160 | tf_op jit(solution)/shard_map/ppermute | solution.py:416
  33.6 0.0 copy-done.3
  33.6 0.1 copy.12.plan_ref
  33.7 0.4 shard_map.115.base_ref
  34.1 0.3 collective-permute-done.5.other_ref
  34.4 0.9 %shard_map.118 = bf16[1024,128]{1,0:T(8,128)(2,1)} custom-call(f32[1024,128]{1,0:T(8,128)S(1)} %shard_map.115.base_ref, f32[32,128]{1,0:T(8,128)S(1)} %shard_map.117.own_ref, f32[32,128]{1,0:T(8,128)S(1)} %collective-permute-done.5.other_ref, bf16[16,1152]{1,0:T(8,128)(2,1)S(1)} %get-tuple-element.11.d0, bf16[16,1152]{1,0:T(8,128)(2,1)S(1)} %collective-permute-done.2.d1, ...), custom_call_target="tpu_custom_call" | custom-call | flops 4000000 | bytes 900000 | tf_op jit(solution)/shard_map/pallas_call | solution.py:262
  35.3 12.6 %all-to-all-start.1 = ((bf16[128,8,128]{2,1,0:T(8,128)(2,1)}), bf16[128,8,128]{2,1,0:T(8,128)(2,1)S(1)}, u32[]{:S(2)}, u32[]{:S(2)}) async-start(bf16[128,8,128]{2,1,0:T(8,128)(2,1)} %bitcast), calls=%async_computation.1 | async-start | bytes 524288 | tf_op jit(solution)/shard_map/all_to_all | solution.py:417
  48.0 0.0 collective-permute-done.other_ref
  48.0 0.0 copy-done
  48.0 7.7 %shard_map.112 = (bf16[1024,2048]{1,0:T(8,128)(2,1)}, f32[8,128]{1,0:T(8,128)S(1)}) custom-call(bf16[1024,512]{1,0:T(8,128)(2,1)S(1)} %copy-done, bf16[1024,512]{1,0:T(8,128)(2,1)S(1)} %collective-permute-done.other_ref, bf16[1024,2048]{1,0:T(8,128)(2,1)} %weight_ref.1), custom_call_target="tpu_custom_call" | custom-call | flops 4300000256 | bytes 10500000 | tf_op jit(solution)/shard_map/pallas_call | solution.py:374
  55.6 0.4 all-to-all-done.1
  56.0 0.1 shard_map.119
  56.2 2.2 %collective-permute-start.6 = (bf16[512,128]{1,0:T(8,128)(2,1)S(1)}, bf16[512,128]{1,0:T(8,128)(2,1)S(1)}, u32[]{:S(2)}, u32[]{:S(2)}) collective-permute-start(bf16[512,128]{1,0:T(8,128)(2,1)S(1)} %get-tuple-element.13.own_ref), channel_id=1, source_target_pairs={{0,1},{1,0},{2,3},{3,2},{4,5},{5,4},{6,7},{7,6},{8,9},{9,8},{10,11... | collective-permute-start | bytes 393224 | tf_op jit(solution)/shard_map/ppermute | solution.py:427
  58.4 1.0 %shard_map.121 = f32[8,256]{1,0:T(8,128)} custom-call(f32[512,128]{1,0:T(8,128)S(1)} %get-tuple-element.14.notes_ref), custom_call_target="tpu_custom_call" | custom-call | flops 2000000 | bytes 270000 | tf_op jit(solution)/shard_map/pallas_call | solution.py:325
  59.4 0.0 collective-permute-done.6.other_ref
  59.4 1.0 %shard_map.120 = bf16[640,128]{1,0:T(8,128)(2,1)} custom-call(bf16[512,128]{1,0:T(8,128)(2,1)S(1)} %get-tuple-element.13.own_ref, bf16[512,128]{1,0:T(8,128)(2,1)S(1)} %collective-permute-done.6.other_ref, f32[512,128]{1,0:T(8,128)S(1)} %get-tuple-element.14.notes_ref), custom_call_target="tpu_custom_call" | custom-call | flops 40000000 | bytes 700000 | tf_op jit(solution)/shard_map/pallas_call | solution.py:351
Async XLA Ops:
  0.6 21.1 %copy-start.2 = (s32[8]{0:T(128)S(1)}, s32[8]{0:T(128)}, u32[]{:S(2)}) copy-start(s32[8]{0:T(128)} %corpus_ref.1) | copy-start | bytes 100
  0.6 21.1 %copy-start.1 = (s32[8]{0:T(128)S(1)}, s32[8]{0:T(128)}, u32[]{:S(2)}) copy-start(s32[8]{0:T(128)} %lengths_ref.1) | copy-start | bytes 100
  2.2 28.3 %all-to-all-start = ((bf16[32,4,2048]{2,1,0:T(4,128)(2,1)}), bf16[32,4,2048]{2,1,0:T(4,128)(2,1)S(1)}, u32[]{:S(2)}, u32[]{:S(2)}) async-start(bf16[32,4,2048]{2,1,0:T(4,128)(2,1)} %shard_map.116), calls=%async_computation | async-start | bytes 1048576 | tf_op jit(solution)/shard_map/all_to_all | solution.py:402
  14.2 19.3 %copy-start.3 = (s32[128,2]{0,1:T(2,128)S(1)}, s32[128,2]{0,1:T(2,128)}, u32[]{:S(2)}) copy-start(s32[128,2]{0,1:T(2,128)} %param.17) | copy-start | bytes 3076
  14.2 33.7 %copy-start = (bf16[1024,512]{1,0:T(8,128)(2,1)S(1)}, bf16[1024,512]{1,0:T(8,128)(2,1)}, u32[]{:S(2)}) copy-start(bf16[1024,512]{1,0:T(8,128)(2,1)} %cot_ref.1) | copy-start | bytes 3145732
  14.3 33.7 %collective-permute-start = (bf16[1024,512]{1,0:T(8,128)(2,1)}, bf16[1024,512]{1,0:T(8,128)(2,1)S(1)}, u32[]{:S(2)}, u32[]{:S(2)}) collective-permute-start(bf16[1024,512]{1,0:T(8,128)(2,1)} %cot_ref.1), channel_id=1, source_target_pairs={{0,1},{1,0},{2,3},{3,2},{4,5},{5,4},{6,7},{7,6},{8,9},{9,8},{10,11... | collective-permute-start | bytes 3145736 | tf_op jit(solution)/shard_map/ppermute | solution.py:401
  19.7 2.0 %collective-permute-start.1 = (f32[1024,128]{1,0:T(8,128)S(1)}, f32[1024,128]{1,0:T(8,128)S(1)}, u32[]{:S(2)}, u32[]{:S(2)}) collective-permute-start(f32[1024,128]{1,0:T(8,128)S(1)} %shard_map.113.own_ref), channel_id=1, source_target_pairs={{0,1},{1,0},{2,3},{3,2},{4,5},{5,4},{6,7},{7,6},{8,9},{9,8},{10,11... | collective-permute-start | bytes 1572872 | tf_op jit(solution)/shard_map/ppermute | solution.py:411
  22.9 4.4 %collective-permute-start.4 = (bf16[16,1152]{1,0:T(8,128)(2,1)S(1)}, bf16[16,1152]{1,0:T(8,128)(2,1)S(1)}, u32[]{:S(2)}, u32[]{:S(2)}) collective-permute-start(bf16[16,1152]{1,0:T(8,128)(2,1)S(1)} %get-tuple-element.11.d0), channel_id=1, source_target_pairs={{0,6},{2,4},{4,2},{6,0},{8,14},{10,12},{12,10},{14,8},{16,22},{18,... | collective-permute-start | bytes 110600 | tf_op jit(solution)/shard_map/ppermute | solution.py:414
  25.5 4.6 %collective-permute-start.3 = (bf16[16,1152]{1,0:T(8,128)(2,1)S(1)}, bf16[16,1152]{1,0:T(8,128)(2,1)S(1)}, u32[]{:S(2)}, u32[]{:S(2)}) collective-permute-start(bf16[16,1152]{1,0:T(8,128)(2,1)S(1)} %get-tuple-element.11.d0), channel_id=1, source_target_pairs={{0,4},{2,6},{4,0},{6,2},{8,12},{10,14},{12,8},{14,10},{16,20},{18,... | collective-permute-start | bytes 110600 | tf_op jit(solution)/shard_map/ppermute | solution.py:414
  26.0 4.1 %collective-permute-start.2 = (bf16[16,1152]{1,0:T(8,128)(2,1)S(1)}, bf16[16,1152]{1,0:T(8,128)(2,1)S(1)}, u32[]{:S(2)}, u32[]{:S(2)}) collective-permute-start(bf16[16,1152]{1,0:T(8,128)(2,1)S(1)} %get-tuple-element.11.d0), channel_id=1, source_target_pairs={{0,2},{2,0},{4,6},{6,4},{8,10},{10,8},{12,14},{14,12},{16,18},{18,... | collective-permute-start | bytes 110600 | tf_op jit(solution)/shard_map/ppermute | solution.py:414
  31.1 3.3 %collective-permute-start.5 = (f32[32,128]{1,0:T(8,128)S(1)}, f32[32,128]{1,0:T(8,128)S(1)}, u32[]{:S(2)}, u32[]{:S(2)}) collective-permute-start(f32[32,128]{1,0:T(8,128)S(1)} %shard_map.117.own_ref), channel_id=1, source_target_pairs={{0,1},{1,0},{2,3},{3,2},{4,5},{5,4},{6,7},{7,6},{8,9},{9,8},{10,11... | collective-permute-start | bytes 49160 | tf_op jit(solution)/shard_map/ppermute | solution.py:416
  35.3 20.7 %all-to-all-start.1 = ((bf16[128,8,128]{2,1,0:T(8,128)(2,1)}), bf16[128,8,128]{2,1,0:T(8,128)(2,1)S(1)}, u32[]{:S(2)}, u32[]{:S(2)}) async-start(bf16[128,8,128]{2,1,0:T(8,128)(2,1)} %bitcast), calls=%async_computation.1 | async-start | bytes 524288 | tf_op jit(solution)/shard_map/all_to_all | solution.py:417
  56.2 3.2 %collective-permute-start.6 = (bf16[512,128]{1,0:T(8,128)(2,1)S(1)}, bf16[512,128]{1,0:T(8,128)(2,1)S(1)}, u32[]{:S(2)}, u32[]{:S(2)}) collective-permute-start(bf16[512,128]{1,0:T(8,128)(2,1)S(1)} %get-tuple-element.13.own_ref), channel_id=1, source_target_pairs={{0,1},{1,0},{2,3},{3,2},{4,5},{5,4},{6,7},{7,6},{8,9},{9,8},{10,11... | collective-permute-start | bytes 393224 | tf_op jit(solution)/shard_map/ppermute | solution.py:427

commit v4 on v3

--- a/solution.py
+++ b/solution.py
@@ -17,6 +17,7 @@
 PLACE_ROW = 6
 OWNER_ROW = 7
 GROUP = 4
+PAD = 8
 CHUNKS = ((0, 256), (256, 256), (512, 256), (768, 256))
 LANES = 128
 VMEM = pltpu.VMEM
@@ -28,6 +29,11 @@
 
 def dot(a, b, dims=(((1,), (0,)), ((), ()))):
     return lax.dot_general(a, b, dims, preferred_element_type=F32)
+
+
+def slot_of(device):
+    z, y, x = device // 16, device // GROUP % GROUP, device % GROUP
+    return DP - 1 - (x * 32 + y * 8 + z)
 
 
 def lane_iota(shape):
@@ -126,29 +132,25 @@
     me = lax.axis_index("mp")
     feat = (own_ref[...].astype(F32) + other_ref[...].astype(F32)).astype(BF16)
     feat_ref[...] = feat
-    row = lax.broadcasted_iota(jnp.int32, (LANES, 3 * LANES), 0)
-    col = lane_iota((LANES, 3 * LANES))
-    wide = col < 2 * LANES
-    odd = jnp.where(col >= LANES, 1, 0)
-    want = jnp.where(wide, RANK + me * half + 2 * (col % 16) + odd, col % RANK)
-    pick = jnp.where(row == want, 1.0, 0.0).astype(BF16)
-    spread = dot(feat, pick)
-    doc = lane_iota((1, 2 * LANES)) % LANES // 16
-    first = jnp.zeros((1, 2 * LANES), jnp.int32)
-    last = jnp.zeros((1, 2 * LANES), jnp.int32)
+    wide = 2 * LANES
+    row = lax.broadcasted_iota(jnp.int32, (wide, LANES), 0)
+    want = RANK + me * half + 2 * (row % 16) + row // LANES
+    pick = jnp.where(lane_iota((wide, LANES)) == want, 1.0, 0.0).astype(BF16)
+    spread = dot(pick, feat, NT)
+    doc = lax.broadcasted_iota(jnp.int32, (wide, 1), 0) % LANES // 16
+    first = jnp.zeros((wide, 1), jnp.int32)
+    last = jnp.zeros((wide, 1), jnp.int32)
     at = 0
     for i in range(DOCS):
         length = lengths_ref[i]
         first = jnp.where(doc == i, at, first)
         last = jnp.where(doc == i, at + length, last)
         at = at + length
-    token = lax.broadcasted_iota(jnp.int32, (TOK, 2 * LANES), 0)
+    token = lane_iota((wide, TOK))
     live = (token >= first) & (token < last)
-    out_cols = jnp.where(live, spread[:, : 2 * LANES], 0.0).astype(BF16)
-    in_cols = spread[:, 2 * LANES :].astype(BF16)
-    both = dot(out_cols, in_cols, TN)
-    lane = lane_iota((LANES, LANES))
-    scr[...] = jnp.where(lane < RANK, both[:LANES], both[LANES:])
+    both = dot(jnp.where(live, spread, 0.0).astype(BF16), feat)
+    left = lane_iota((LANES, LANES)) < RANK
+    scr[0:LANES, :] = jnp.where(left, both[:LANES], pltpu.roll(both[LANES:], RANK, 1))
     pairs = half // 2
     for p in range(pairs // 2):
         low = scr[pl.ds(p, DOCS, stride=pairs), :]
@@ -157,7 +159,7 @@
     sub = lax.broadcasted_iota(jnp.int32, (2 * DOCS, LANES), 0)
     note = jnp.zeros((2 * DOCS, LANES), jnp.int32)
     for i in range(DOCS):
-        note = jnp.where(sub == i, corpus_ref[i] // DOCS, note)
+        note = jnp.where(sub == i, slot_of(corpus_ref[i] // DOCS), note)
         note = jnp.where(sub == DOCS + i, corpus_ref[i] % DOCS + 1, note)
     docs_ref[:, pairs // 2 * LANES :] = note.astype(F32).astype(BF16)
 
@@ -173,7 +175,7 @@
             jax.ShapeDtypeStruct((TOK, 2 * RANK), BF16),
             jax.ShapeDtypeStruct((2 * DOCS, 9 * LANES), BF16),
         ],
-        scratch_shapes=[VMEM((LANES, LANES), F32)],
+        scratch_shapes=[VMEM((LANES + 16, LANES), F32)],
         compiler_params=params(),
         cost_estimate=pl.CostEstimate(flops=200_000_000, bytes_accessed=1_500_000, transcendentals=0),
     )(own, other, lengths, corpus)
@@ -204,11 +206,11 @@
 
 def place_kernel(feat_ref, plan_ref, out_ref, tokens):
     me = lax.axis_index("mp")
-    tokens[...] = feat_ref[...].astype(F32)
+    tokens[0:TOK, :] = feat_ref[...].astype(F32)
     lane = lane_iota((DP, LANES))
-    dest = plan_ref[:, 0:1]
+    dest = slot_of(plan_ref[:, 0:1])
     first = plan_ref[:, 1:2]
-    send = jnp.where((dest == DP - 1 - lane) & (first < CAP), 1.0, 0.0).astype(BF16)
+    send = jnp.where((dest == lane) & (first < CAP), 1.0, 0.0).astype(BF16)
     for r in range(HALF_BLOCK):
         rows = tokens[pl.ds(HALF_BLOCK * me + r, DP, stride=BLOCK), :].astype(BF16)
         out_ref[pl.ds(r, DP, stride=SLOT), :] = dot(send, rows, TN)
@@ -224,8 +226,8 @@
         place_kernel,
         in_specs=[vmem] * 2,
         out_specs=vmem,
-        out_shape=jax.ShapeDtypeStruct((DP * SLOT, LANES), F32),
-        scratch_shapes=[VMEM((TOK, LANES), F32)],
+        out_shape=jax.ShapeDtypeStruct((DP * SLOT + PAD, LANES), F32),
+        scratch_shapes=[VMEM((TOK + PAD, LANES), F32)],
         compiler_params=params(),
         cost_estimate=pl.CostEstimate(flops=20_000_000, bytes_accessed=900_000, transcendentals=0),
     )(features, plan)
@@ -248,13 +250,13 @@
     notes = [ref[:, 8 * LANES :].astype(F32) for ref in (d0, d1, d2, d3)]
     owner = jnp.concatenate([note[:DOCS] for note in notes], axis=0)
     row = jnp.concatenate([note[DOCS:] for note in notes], axis=0)
-    hit = jnp.where(owner == (DP - 1 - short).astype(F32), 1.0, 0.0).astype(BF16)
+    hit = jnp.where(owner == short.astype(F32), 1.0, 0.0).astype(BF16)
     marks = jnp.where(short // 32 == piece, row, 0.0).astype(BF16)
     two = 2 * DOCS
     stage[pl.ds(SCORE_ROW, DP, stride=SLOT), :] = dot(hit[:two], scores[:two], TN)
     stage[pl.ds(SCORE_ROW + 1, DP, stride=SLOT), :] = dot(hit[two:], scores[two:], TN)
     stage[pl.ds(OWNER_ROW, DP, stride=SLOT), :] = dot(hit, marks, TN)
-    out_ref[...] = stage[...].astype(BF16)
+    out_ref[...] = stage[0 : DP * SLOT, :].astype(BF16)
 
 
 def pack(base, own, other, pieces):
@@ -264,14 +266,14 @@
         in_specs=[vmem] * 7,
         out_specs=vmem,
         out_shape=jax.ShapeDtypeStruct((DP * SLOT, LANES), BF16),
-        scratch_shapes=[VMEM((DP * SLOT, LANES), F32)],
+        scratch_shapes=[VMEM((DP * SLOT + PAD, LANES), F32)],
         compiler_params=params(),
         cost_estimate=pl.CostEstimate(flops=4_000_000, bytes_accessed=900_000, transcendentals=0),
     )(base, own, other, *pieces)
 
 
 def split_kernel(got_ref, after_ref, rows_ref, notes_ref, stage):
-    stage[...] = got_ref[...].astype(F32)
+    stage[0 : DP * SLOT, :] = got_ref[...].astype(F32)
     for r in range(HALF_BLOCK):
         part = stage[pl.ds(r, DP, stride=SLOT), :]
         rows_ref[r * DP : (r + 1) * DP, :] = part.astype(BF16)
@@ -290,7 +292,7 @@
             jax.ShapeDtypeStruct((HALF_BLOCK * DP, LANES), BF16),
             jax.ShapeDtypeStruct((HALF_BLOCK * DP, LANES), F32),
         ],
-        scratch_shapes=[VMEM((DP * SLOT, LANES), F32)],
+        scratch_shapes=[VMEM((DP * SLOT + PAD, LANES), F32)],
         compiler_params=params(),
         cost_estimate=pl.CostEstimate(flops=0, bytes_accessed=600_000, transcendentals=0),
     )(got, after)
@@ -305,7 +307,7 @@
     for x in range(GROUP):
 
         def taken(row):
-            return notes_ref[pl.ds((row - HALF_BLOCK) * DP + x, count, stride=GROUP), :]
+            return notes_ref[pl.ds((row - HALF_BLOCK) * DP + x * count, count), :]
 
         hit = jnp.where(taken(OWNER_ROW) == want, 1.0, 0.0).astype(BF16)
         one = dot(hit, taken(SCORE_ROW).astype(BF16), TN)
@@ -343,7 +345,7 @@
         far = other_ref[r * DP : (r + 1) * DP, :]
         rows[pl.ds(HALF_BLOCK * me + r, blocks, stride=BLOCK), :] = dot(put, near, TN)[:blocks]
         rows[pl.ds(HALF_BLOCK * (1 - me) + r, blocks, stride=BLOCK), :] = dot(put, far, TN)[:blocks]
-    balanced_ref[...] = rows[...].astype(BF16)
+    balanced_ref[...] = rows[0:CAP, :].astype(BF16)
 
 
 def balance(own, other, notes):
@@ -353,7 +355,7 @@
         in_specs=[vmem, vmem, vmem],
         out_specs=vmem,
         out_shape=jax.ShapeDtypeStruct((CAP, 2 * RANK), BF16),
-        scratch_shapes=[VMEM((CAP, LANES), F32)],
+        scratch_shapes=[VMEM((CAP + PAD, LANES), F32)],
         compiler_params=params(),
         cost_estimate=pl.CostEstimate(flops=40_000_000, bytes_accessed=700_000, transcendentals=0),
     )(own, other, notes)
@@ -420,7 +422,7 @@
         0,
         0,
         tiled=True,
-        axis_index_groups=[list(range(DP - 1, -1, -1))],
+        axis_index_groups=[sorted(range(DP), key=slot_of)],
     )
     input_grad, token = input_gradient(cotangent, other_cot, value_weight)
     rows, notes = split(got.reshape(DP * SLOT, LANES), token)

time: 60.8 us -> 60.4 us (level)
  no operation moved by 1% of the time
where the time goes in v4:
time: 60.4 us; the launch traced here: 59.9 us
  starting transfers between devices  33.5 us (55%)
  Pallas kernels  18.8 us (31%)
  waiting for transfers between devices  6.75 us (11%)
  between operations  0.74 us (1%)
    all_to_all x1, starting transfers between devices, body(): lax.all_to_all(packed.reshape(DP, SLOT, LANES), 'dp', 0, 0, tiled=True, a...  12.6 us
    all_to_all x1, starting transfers between devices, body(): lax.all_to_all(copies(query_grads, members), 'dp', 0, 0, tiled=True, axis...  12 us
    pallas_call x1, Pallas kernels, input_gradient(): pl.pallas_call(grad_kernel, grid=(weight.shape[1] // columns,), in_specs=...  7.65 us
    pallas_call x1, Pallas kernels, partial_features(): pl.pallas_call(partial_kernel, in_specs=[hbm] * 4, out_specs=pl.BlockSpec...  4.4 us
    ppermute x3, waiting for transfers between devices, body(): pieces.append(lax.ppermute(docs, 'dp', [(s, s ^ i) for s in range(DP)]))  3.84 us
    ppermute x3, starting transfers between devices, body(): pieces.append(lax.ppermute(docs, 'dp', [(s, s ^ i) for s in range(DP)]))  3.34 us
    ppermute x1, starting transfers between devices, body(): lax.ppermute(mine, 'mp', swap)  2.41 us
    ppermute x1, starting transfers between devices, body(): balanced = balance(rows, lax.ppermute(rows, 'mp', swap), notes)  1.94 us
  transfers between devices with their start and end apart: 9, of which 6 were waited for; matrix products, arithmetic and copies ran while one was open for 0% of the time, Pallas kernels for 27%

profile of v4, /device:TPU:1, one launch (start us, length us, event | category | flops | bytes accessed | tf_op | source)
XLA Modules:
  0.0 59.9 jit_solution(15015259900164113009)
XLA Ops:
  0.6 0.0 copy-start.2
  0.6 0.0 copy-start.1
  0.7 1.5 %shard_map.116 = bf16[32,4,2048]{2,1,0:T(4,128)(2,1)} custom-call(bf16[4,2048]{1,0:T(4,128)(2,1)} %source_ref.1), custom_call_target="tpu_custom_call" | custom-call | tf_op jit(solution)/shard_map/pallas_call | solution.py:60
  2.2 12.0 %all-to-all-start = ((bf16[32,4,2048]{2,1,0:T(4,128)(2,1)}), bf16[32,4,2048]{2,1,0:T(4,128)(2,1)S(1)}, u32[]{:S(2)}, u32[]{:S(2)}) async-start(bf16[32,4,2048]{2,1,0:T(4,128)(2,1)} %shard_map.116), calls=%async_computation | async-start | bytes 1048576 | tf_op jit(solution)/shard_map/all_to_all | solution.py:404
  14.2 0.0 copy-start.3
  14.2 0.0 copy-start
  14.3 1.0 %collective-permute-start = (bf16[1024,512]{1,0:T(8,128)(2,1)}, bf16[1024,512]{1,0:T(8,128)(2,1)S(1)}, u32[]{:S(2)}, u32[]{:S(2)}) collective-permute-start(bf16[1024,512]{1,0:T(8,128)(2,1)} %cot_ref.1), channel_id=1, source_target_pairs={{0,1},{1,0},{2,3},{3,2},{4,5},{5,4},{6,7},{7,6},{8,9},{9,8},{10,11... | collective-permute-start | bytes 3145736 | tf_op jit(solution)/shard_map/ppermute | solution.py:403
  15.3 4.4 %shard_map.113.own_ref = f32[1024,128]{1,0:T(8,128)S(1)} custom-call(bf16[1024,2048]{1,0:T(8,128)(2,1)} %acts_ref.1, bf16[1024,512]{1,0:T(8,128)(2,1)} %cot_ref.1, bf16[64,2048]{1,0:T(8,128)(2,1)} %pin_ref.1, bf16[64,1024]{1,0:T(8,128)(2,1)} %pout_ref.1), custom_call_target="tpu_custom_call" | custom-call | flops 340000000 | bytes 6000000 | tf_op jit(solution)/shard_map/pallas_call | solution.py:113
  19.7 0.1 collective-permute-start.1
  19.8 1.9 %collective-permute-done.1.other_ref = f32[1024,128]{1,0:T(8,128)S(1)} collective-permute-done((f32[1024,128]{1,0:T(8,128)S(1)}, f32[1024,128]{1,0:T(8,128)S(1)}, u32[]{:S(2)}, u32[]{:S(2)}) %collective-permute-start.1) | collective-permute-done | bytes 524320 | tf_op jit(solution)/shard_map/ppermute | solution.py:413
  21.7 0.0 copy-done.2
  21.7 0.0 copy-done.1
  21.7 1.1 %shard_map.114 = (bf16[1024,128]{1,0:T(8,128)(2,1)S(1)}, bf16[16,1152]{1,0:T(8,128)(2,1)S(1)}) custom-call(f32[1024,128]{1,0:T(8,128)S(1)} %shard_map.113.own_ref, f32[1024,128]{1,0:T(8,128)S(1)} %collective-permute-done.1.other_ref, s32[8]{0:T(128)S(1)} %copy-done.1, s32[8]{0:T(128)S(1)} %copy-done.2), custom_call_target="tpu_custom_call" | custom-call | flops 200000000 | bytes 1500000 | tf_op jit(solution)/shard_map/pallas_call | solution.py:170
  22.8 2.6 %collective-permute-start.4 = (bf16[16,1152]{1,0:T(8,128)(2,1)S(1)}, bf16[16,1152]{1,0:T(8,128)(2,1)S(1)}, u32[]{:S(2)}, u32[]{:S(2)}) collective-permute-start(bf16[16,1152]{1,0:T(8,128)(2,1)S(1)} %get-tuple-element.11.d0), channel_id=1, source_target_pairs={{0,6},{2,4},{4,2},{6,0},{8,14},{10,12},{12,10},{14,8},{16,22},{18,... | collective-permute-start | bytes 110600 | tf_op jit(solution)/shard_map/ppermute | solution.py:416
  25.4 0.5 collective-permute-start.3
  25.9 0.3 collective-permute-start.2
  26.2 1.1 %collective-permute-done.4.d3 = bf16[16,1152]{1,0:T(8,128)(2,1)S(1)} collective-permute-done((bf16[16,1152]{1,0:T(8,128)(2,1)S(1)}, bf16[16,1152]{1,0:T(8,128)(2,1)S(1)}, u32[]{:S(2)}, u32[]{:S(2)}) %collective-permute-start.4) | collective-permute-done | bytes 36896 | tf_op jit(solution)/shard_map/ppermute | solution.py:416
  27.2 2.8 %collective-permute-done.3.d2 = bf16[16,1152]{1,0:T(8,128)(2,1)S(1)} collective-permute-done((bf16[16,1152]{1,0:T(8,128)(2,1)S(1)}, bf16[16,1152]{1,0:T(8,128)(2,1)S(1)}, u32[]{:S(2)}, u32[]{:S(2)}) %collective-permute-start.3) | collective-permute-done | bytes 36896 | tf_op jit(solution)/shard_map/ppermute | solution.py:416
  30.0 0.0 collective-permute-done.2.d1
  30.0 0.5 all-to-all-done.queries_ref
  30.5 0.6 %shard_map.117.own_ref = f32[32,128]{1,0:T(8,128)S(1)} custom-call(bf16[16,1152]{1,0:T(8,128)(2,1)S(1)} %get-tuple-element.11.d0, bf16[16,1152]{1,0:T(8,128)(2,1)S(1)} %collective-permute-done.2.d1, bf16[16,1152]{1,0:T(8,128)(2,1)S(1)} %collective-permute-done.3.d2, bf16[16,1152]{1,0:T(8,128)(2,1)S(1)} %collective-permute-done.4.d3, ...), custom_call_target="tpu_custom_call" | custom-call | flops 17000000 | bytes 700000 | tf_op jit(solution)/shard_map/pallas_call | solution.py:197
  31.1 2.4 %collective-permute-start.5 = (f32[32,128]{1,0:T(8,128)S(1)}, f32[32,128]{1,0:T(8,128)S(1)}, u32[]{:S(2)}, u32[]{:S(2)}) collective-permute-start(f32[32,128]{1,0:T(8,128)S(1)} %shard_map.117.own_ref), channel_id=1, source_target_pairs={{0,1},{1,0},{2,3},{3,2},{4,5},{5,4},{6,7},{7,6},{8,9},{9,8},{10,11... | collective-permute-start | bytes 49160 | tf_op jit(solution)/shard_map/ppermute | solution.py:418
  33.6 0.0 copy-done.3
  33.6 0.1 copy.12.plan_ref
  33.7 0.5 shard_map.115.base_ref
  34.2 0.2 collective-permute-done.5.other_ref
  34.4 0.9 %shard_map.118 = bf16[1024,128]{1,0:T(8,128)(2,1)} custom-call(f32[1032,128]{1,0:T(8,128)S(1)} %shard_map.115.base_ref, f32[32,128]{1,0:T(8,128)S(1)} %shard_map.117.own_ref, f32[32,128]{1,0:T(8,128)S(1)} %collective-permute-done.5.other_ref, bf16[16,1152]{1,0:T(8,128)(2,1)S(1)} %get-tuple-element.11.d0, bf16[16,1152]{1,0:T(8,128)(2,1)S(1)} %collective-permute-done.2.d1, ...), custom_call_target="tpu_custom_call" | custom-call | flops 4000000 | bytes 900000 | tf_op jit(solution)/shard_map/pallas_call | solution.py:264
  35.3 12.6 %all-to-all-start.1 = ((bf16[128,8,128]{2,1,0:T(8,128)(2,1)}), bf16[128,8,128]{2,1,0:T(8,128)(2,1)S(1)}, u32[]{:S(2)}, u32[]{:S(2)}) async-start(bf16[128,8,128]{2,1,0:T(8,128)(2,1)} %bitcast), calls=%async_computation.1 | async-start | bytes 524288 | tf_op jit(solution)/shard_map/all_to_all | solution.py:419
  48.0 0.0 collective-permute-done.other_ref
  48.0 0.0 copy-done
  48.0 7.7 %shard_map.112 = (bf16[1024,2048]{1,0:T(8,128)(2,1)}, f32[8,128]{1,0:T(8,128)S(1)}) custom-call(bf16[1024,512]{1,0:T(8,128)(2,1)S(1)} %copy-done, bf16[1024,512]{1,0:T(8,128)(2,1)S(1)} %collective-permute-done.other_ref, bf16[1024,2048]{1,0:T(8,128)(2,1)} %weight_ref.1), custom_call_target="tpu_custom_call" | custom-call | flops 4300000256 | bytes 10500000 | tf_op jit(solution)/shard_map/pallas_call | solution.py:376
  55.6 0.3 all-to-all-done.1
  55.9 0.1 shard_map.119
  56.0 1.9 %collective-permute-start.6 = (bf16[512,128]{1,0:T(8,128)(2,1)S(1)}, bf16[512,128]{1,0:T(8,128)(2,1)S(1)}, u32[]{:S(2)}, u32[]{:S(2)}) collective-permute-start(bf16[512,128]{1,0:T(8,128)(2,1)S(1)} %get-tuple-element.13.own_ref), channel_id=1, source_target_pairs={{0,1},{1,0},{2,3},{3,2},{4,5},{5,4},{6,7},{7,6},{8,9},{9,8},{10,11... | collective-permute-start | bytes 393224 | tf_op jit(solution)/shard_map/ppermute | solution.py:429
  58.0 1.0 %shard_map.121 = f32[8,256]{1,0:T(8,128)} custom-call(f32[512,128]{1,0:T(8,128)S(1)} %get-tuple-element.14.notes_ref), custom_call_target="tpu_custom_call" | custom-call | flops 2000000 | bytes 270000 | tf_op jit(solution)/shard_map/pallas_call | solution.py:327
  59.0 0.0 collective-permute-done.6.other_ref
  59.0 1.0 %shard_map.120 = bf16[640,128]{1,0:T(8,128)(2,1)} custom-call(bf16[512,128]{1,0:T(8,128)(2,1)S(1)} %get-tuple-element.13.own_ref, bf16[512,128]{1,0:T(8,128)(2,1)S(1)} %collective-permute-done.6.other_ref, f32[512,128]{1,0:T(8,128)S(1)} %get-tuple-element.14.notes_ref), custom_call_target="tpu_custom_call" | custom-call | flops 40000000 | bytes 700000 | tf_op jit(solution)/shard_map/pallas_call | solution.py:353
Async XLA Ops:
  0.6 21.1 %copy-start.2 = (s32[8]{0:T(128)S(1)}, s32[8]{0:T(128)}, u32[]{:S(2)}) copy-start(s32[8]{0:T(128)} %corpus_ref.1) | copy-start | bytes 100
  0.6 21.1 %copy-start.1 = (s32[8]{0:T(128)S(1)}, s32[8]{0:T(128)}, u32[]{:S(2)}) copy-start(s32[8]{0:T(128)} %lengths_ref.1) | copy-start | bytes 100
  2.2 28.3 %all-to-all-start = ((bf16[32,4,2048]{2,1,0:T(4,128)(2,1)}), bf16[32,4,2048]{2,1,0:T(4,128)(2,1)S(1)}, u32[]{:S(2)}, u32[]{:S(2)}) async-start(bf16[32,4,2048]{2,1,0:T(4,128)(2,1)} %shard_map.116), calls=%async_computation | async-start | bytes 1048576 | tf_op jit(solution)/shard_map/all_to_all | solution.py:404
  14.2 19.3 %copy-start.3 = (s32[128,2]{0,1:T(2,128)S(1)}, s32[128,2]{0,1:T(2,128)}, u32[]{:S(2)}) copy-start(s32[128,2]{0,1:T(2,128)} %param.17) | copy-start | bytes 3076
  14.2 33.7 %copy-start = (bf16[1024,512]{1,0:T(8,128)(2,1)S(1)}, bf16[1024,512]{1,0:T(8,128)(2,1)}, u32[]{:S(2)}) copy-start(bf16[1024,512]{1,0:T(8,128)(2,1)} %cot_ref.1) | copy-start | bytes 3145732
  14.3 33.7 %collective-permute-start = (bf16[1024,512]{1,0:T(8,128)(2,1)}, bf16[1024,512]{1,0:T(8,128)(2,1)S(1)}, u32[]{:S(2)}, u32[]{:S(2)}) collective-permute-start(bf16[1024,512]{1,0:T(8,128)(2,1)} %cot_ref.1), channel_id=1, source_target_pairs={{0,1},{1,0},{2,3},{3,2},{4,5},{5,4},{6,7},{7,6},{8,9},{9,8},{10,11... | collective-permute-start | bytes 3145736 | tf_op jit(solution)/shard_map/ppermute | solution.py:403
  19.7 2.0 %collective-permute-start.1 = (f32[1024,128]{1,0:T(8,128)S(1)}, f32[1024,128]{1,0:T(8,128)S(1)}, u32[]{:S(2)}, u32[]{:S(2)}) collective-permute-start(f32[1024,128]{1,0:T(8,128)S(1)} %shard_map.113.own_ref), channel_id=1, source_target_pairs={{0,1},{1,0},{2,3},{3,2},{4,5},{5,4},{6,7},{7,6},{8,9},{9,8},{10,11... | collective-permute-start | bytes 1572872 | tf_op jit(solution)/shard_map/ppermute | solution.py:413
  22.8 4.4 %collective-permute-start.4 = (bf16[16,1152]{1,0:T(8,128)(2,1)S(1)}, bf16[16,1152]{1,0:T(8,128)(2,1)S(1)}, u32[]{:S(2)}, u32[]{:S(2)}) collective-permute-start(bf16[16,1152]{1,0:T(8,128)(2,1)S(1)} %get-tuple-element.11.d0), channel_id=1, source_target_pairs={{0,6},{2,4},{4,2},{6,0},{8,14},{10,12},{12,10},{14,8},{16,22},{18,... | collective-permute-start | bytes 110600 | tf_op jit(solution)/shard_map/ppermute | solution.py:416
  25.4 4.6 %collective-permute-start.3 = (bf16[16,1152]{1,0:T(8,128)(2,1)S(1)}, bf16[16,1152]{1,0:T(8,128)(2,1)S(1)}, u32[]{:S(2)}, u32[]{:S(2)}) collective-permute-start(bf16[16,1152]{1,0:T(8,128)(2,1)S(1)} %get-tuple-element.11.d0), channel_id=1, source_target_pairs={{0,4},{2,6},{4,0},{6,2},{8,12},{10,14},{12,8},{14,10},{16,20},{18,... | collective-permute-start | bytes 110600 | tf_op jit(solution)/shard_map/ppermute | solution.py:416
  25.9 4.1 %collective-permute-start.2 = (bf16[16,1152]{1,0:T(8,128)(2,1)S(1)}, bf16[16,1152]{1,0:T(8,128)(2,1)S(1)}, u32[]{:S(2)}, u32[]{:S(2)}) collective-permute-start(bf16[16,1152]{1,0:T(8,128)(2,1)S(1)} %get-tuple-element.11.d0), channel_id=1, source_target_pairs={{0,2},{2,0},{4,6},{6,4},{8,10},{10,8},{12,14},{14,12},{16,18},{18,... | collective-permute-start | bytes 110600 | tf_op jit(solution)/shard_map/ppermute | solution.py:416
  31.1 3.3 %collective-permute-start.5 = (f32[32,128]{1,0:T(8,128)S(1)}, f32[32,128]{1,0:T(8,128)S(1)}, u32[]{:S(2)}, u32[]{:S(2)}) collective-permute-start(f32[32,128]{1,0:T(8,128)S(1)} %shard_map.117.own_ref), channel_id=1, source_target_pairs={{0,1},{1,0},{2,3},{3,2},{4,5},{5,4},{6,7},{7,6},{8,9},{9,8},{10,11... | collective-permute-start | bytes 49160 | tf_op jit(solution)/shard_map/ppermute | solution.py:418
  35.3 20.6 %all-to-all-start.1 = ((bf16[128,8,128]{2,1,0:T(8,128)(2,1)}), bf16[128,8,128]{2,1,0:T(8,128)(2,1)S(1)}, u32[]{:S(2)}, u32[]{:S(2)}) async-start(bf16[128,8,128]{2,1,0:T(8,128)(2,1)} %bitcast), calls=%async_computation.1 | async-start | bytes 524288 | tf_op jit(solution)/shard_map/all_to_all | solution.py:419
  56.0 2.9 %collective-permute-start.6 = (bf16[512,128]{1,0:T(8,128)(2,1)S(1)}, bf16[512,128]{1,0:T(8,128)(2,1)S(1)}, u32[]{:S(2)}, u32[]{:S(2)}) collective-permute-start(bf16[512,128]{1,0:T(8,128)(2,1)S(1)} %get-tuple-element.13.own_ref), channel_id=1, source_target_pairs={{0,1},{1,0},{2,3},{3,2},{4,5},{5,4},{6,7},{7,6},{8,9},{9,8},{10,11... | collective-permute-start | bytes 393224 | tf_op jit(solution)/shard_map/ppermute | solution.py:429

commit v5 on v4

--- a/solution.py
+++ b/solution.py
@@ -33,7 +33,7 @@
 
 def slot_of(device):
     z, y, x = device // 16, device // GROUP % GROUP, device % GROUP
-    return DP - 1 - (x * 32 + y * 8 + z)
+    return DP - 1 - (x * 32 + (y + x) % 4 * 8 + (z + 2 * y + 3 * x) % 8)
 
 
 def lane_iota(shape):
@@ -104,7 +104,7 @@
                 copy.start()
         low = dot(acts[span, :], pin[...], NT)
         high = dot(cot[span, :], pout[...], NT)
-        out_ref[span, :] = jnp.concatenate([low, high], axis=1)
+        out_ref[span, :] = jnp.concatenate([low, high], axis=1).astype(BF16)
 
 
 def partial_features(acts, cotangent, proj_in, proj_out):
@@ -114,7 +114,7 @@
         partial_kernel,
         in_specs=[hbm] * 4,
         out_specs=pl.BlockSpec(memory_space=VMEM),
-        out_shape=VMEM((TOK, 2 * RANK), F32),
+        out_shape=VMEM((TOK, 2 * RANK), BF16),
         scratch_shapes=[
             VMEM(acts.shape, BF16),
             VMEM(cotangent.shape, BF16),
@@ -236,7 +236,11 @@
 def pack_kernel(base_ref, own_ref, other_ref, d0, d1, d2, d3, out_ref, stage):
     me = lax.axis_index("mp")
     stage[...] = base_ref[...]
-    total = (own_ref[...] + other_ref[...]).astype(BF16).astype(F32)
+    sums = (own_ref[...] + other_ref[...]).astype(BF16)
+    source = lax.broadcasted_iota(jnp.int32, (LANES, LANES), 0)
+    z, y = 7 - source // 4 % 8, GROUP - 1 - source // 32
+    order = lane_iota(source.shape) == (z * GROUP + y) * 4 + source % 4
+    total = dot(sums, jnp.where(order, 1.0, 0.0).astype(BF16))
     swapped = pltpu.roll(total, 64, 1)
     short = lane_iota(total.shape)
     piece = lax.broadcasted_iota(jnp.int32, total.shape, 0) // DOCS
@@ -399,7 +403,10 @@
 ):
     swap = [(0, 1), (1, 0)]
     members = DP // GROUP
-    columns = [[k + GROUP * i for i in range(members)] for k in range(GROUP)]
+    columns = [
+        [k + GROUP * y + GROUP * GROUP * z for y in reversed(range(GROUP)) for z in reversed(range(8))]
+        for k in range(GROUP)
+    ]
     other_cot = lax.ppermute(cotangent, "mp", swap)
     queries = lax.all_to_all(
         copies(query_grads, members),

time: 60.4 us -> 59.4 us (0.983)
    all_to_all x1, starting transfers between devices: 12.6 us -> 11.7 us  [body(): lax.all_to_all(packed.reshape(DP, SLOT, LANES), 'dp', 0, 0, tiled=True, a...]
    ppermute x1, starting transfers between devices: 2.41 us -> 1.59 us  [body(): lax.ppermute(mine, 'mp', swap)]
    all_to_all x1, waiting for transfers between devices: 0.29 us -> 1.02 us  [body(): lax.all_to_all(packed.reshape(DP, SLOT, LANES), 'dp', 0, 0, tiled=True, a...]
    all_to_all x1, starting transfers between devices: 12 us -> 12.7 us  [body(): lax.all_to_all(copies(query_grads, members), 'dp', 0, 0, tiled=True, axis...]
    ppermute x1, waiting for transfers between devices: 1.89 us -> 1.28 us  [body(): lax.ppermute(own, 'mp', swap)]
  transfers between devices with their start and end apart: 9 -> 9, of which waited for: 6 -> 5; matrix products, arithmetic and copies ran while one was open for 0% -> 0% of each run, Pallas kernels for 27% -> 28%
where the time goes in v5:
time: 59.4 us; the launch traced here: 59 us
  starting transfers between devices  33.1 us (56%)
  Pallas kernels  18.9 us (32%)
  waiting for transfers between devices  6.16 us (10%)
  between operations  0.74 us (1%)
    all_to_all x1, starting transfers between devices, body(): lax.all_to_all(copies(query_grads, members), 'dp', 0, 0, tiled=True, axis...  12.7 us
    all_to_all x1, starting transfers between devices, body(): lax.all_to_all(packed.reshape(DP, SLOT, LANES), 'dp', 0, 0, tiled=True, a...  11.7 us
    pallas_call x1, Pallas kernels, input_gradient(): pl.pallas_call(grad_kernel, grid=(weight.shape[1] // columns,), in_specs=...  7.65 us
    pallas_call x1, Pallas kernels, partial_features(): pl.pallas_call(partial_kernel, in_specs=[hbm] * 4, out_specs=pl.BlockSpec...  4.18 us
    ppermute x3, waiting for transfers between devices, body(): pieces.append(lax.ppermute(docs, 'dp', [(s, s ^ i) for s in range(DP)]))  3.65 us
    ppermute x3, starting transfers between devices, body(): pieces.append(lax.ppermute(docs, 'dp', [(s, s ^ i) for s in range(DP)]))  3.34 us
    ppermute x1, starting transfers between devices, body(): balanced = balance(rows, lax.ppermute(rows, 'mp', swap), notes)  2.14 us
    ppermute x1, starting transfers between devices, body(): lax.ppermute(mine, 'mp', swap)  1.59 us
  transfers between devices with their start and end apart: 9, of which 5 were waited for; matrix products, arithmetic and copies ran while one was open for 0% of the time, Pallas kernels for 28%

profile of v5, /device:TPU:1, one launch (start us, length us, event | category | flops | bytes accessed | tf_op | source)
XLA Modules:
  0.0 59.0 jit_solution(6623949311124822836)
XLA Ops:
  0.6 0.0 copy-start.2
  0.6 0.0 copy-start.1
  0.7 1.5 %shard_map.116 = bf16[32,4,2048]{2,1,0:T(4,128)(2,1)} custom-call(bf16[4,2048]{1,0:T(4,128)(2,1)} %source_ref.1), custom_call_target="tpu_custom_call" | custom-call | tf_op jit(solution)/shard_map/pallas_call | solution.py:60
  2.2 0.0 copy-start.3
  2.2 12.7 %all-to-all-start = ((bf16[32,4,2048]{2,1,0:T(4,128)(2,1)}), bf16[32,4,2048]{2,1,0:T(4,128)(2,1)S(1)}, u32[]{:S(2)}, u32[]{:S(2)}) async-start(bf16[32,4,2048]{2,1,0:T(4,128)(2,1)} %shard_map.116), calls=%async_computation | async-start | bytes 1048576 | tf_op jit(solution)/shard_map/all_to_all | solution.py:411
  14.9 0.0 copy-start
  14.9 1.3 %collective-permute-start = (bf16[1024,512]{1,0:T(8,128)(2,1)}, bf16[1024,512]{1,0:T(8,128)(2,1)S(1)}, u32[]{:S(2)}, u32[]{:S(2)}) collective-permute-start(bf16[1024,512]{1,0:T(8,128)(2,1)} %cot_ref.1), channel_id=1, source_target_pairs={{0,1},{1,0},{2,3},{3,2},{4,5},{5,4},{6,7},{7,6},{8,9},{9,8},{10,11... | collective-permute-start | bytes 3145736 | tf_op jit(solution)/shard_map/ppermute | solution.py:410
  16.2 4.2 %shard_map.113.own_ref = bf16[1024,128]{1,0:T(8,128)(2,1)S(1)} custom-call(bf16[1024,2048]{1,0:T(8,128)(2,1)} %acts_ref.1, bf16[1024,512]{1,0:T(8,128)(2,1)} %cot_ref.1, bf16[64,2048]{1,0:T(8,128)(2,1)} %pin_ref.1, bf16[64,1024]{1,0:T(8,128)(2,1)} %pout_ref.1), custom_call_target="tpu_custom_call" | custom-call | flops 340000000 | bytes 6000000 | tf_op jit(solution)/shard_map/pallas_call | solution.py:113
  20.4 0.3 collective-permute-start.1
  20.7 1.3 %collective-permute-done.1.other_ref = bf16[1024,128]{1,0:T(8,128)(2,1)S(1)} collective-permute-done((bf16[1024,128]{1,0:T(8,128)(2,1)S(1)}, bf16[1024,128]{1,0:T(8,128)(2,1)S(1)}, u32[]{:S(2)}, u32[]{:S(2)}) %collective-permute-start.1) | collective-permute-done | bytes 262176 | tf_op jit(solution)/shard_map/ppermute | solution.py:420
  22.0 0.0 copy-done.2
  22.0 0.0 copy-done.1
  22.0 1.2 %shard_map.114 = (bf16[1024,128]{1,0:T(8,128)(2,1)S(1)}, bf16[16,1152]{1,0:T(8,128)(2,1)S(1)}) custom-call(bf16[1024,128]{1,0:T(8,128)(2,1)S(1)} %shard_map.113.own_ref, bf16[1024,128]{1,0:T(8,128)(2,1)S(1)} %collective-permute-done.1.other_ref, s32[8]{0:T(128)S(1)} %copy-done.1, s32[8]{0:T(128)S(1)} %copy-done.2), custom_call_target="tpu_custom_call" | custom-call | flops 200000000 | bytes 1500000 | tf_op jit(solution)/shard_map/pallas_call | solution.py:170
  23.2 2.6 %collective-permute-start.4 = (bf16[16,1152]{1,0:T(8,128)(2,1)S(1)}, bf16[16,1152]{1,0:T(8,128)(2,1)S(1)}, u32[]{:S(2)}, u32[]{:S(2)}) collective-permute-start(bf16[16,1152]{1,0:T(8,128)(2,1)S(1)} %get-tuple-element.11.d0), channel_id=1, source_target_pairs={{0,6},{2,4},{4,2},{6,0},{8,14},{10,12},{12,10},{14,8},{16,22},{18,... | collective-permute-start | bytes 110600 | tf_op jit(solution)/shard_map/ppermute | solution.py:423
  25.8 0.5 collective-permute-start.3
  26.3 0.3 collective-permute-start.2
  26.6 1.1 %collective-permute-done.4.d3 = bf16[16,1152]{1,0:T(8,128)(2,1)S(1)} collective-permute-done((bf16[16,1152]{1,0:T(8,128)(2,1)S(1)}, bf16[16,1152]{1,0:T(8,128)(2,1)S(1)}, u32[]{:S(2)}, u32[]{:S(2)}) %collective-permute-start.4) | collective-permute-done | bytes 36896 | tf_op jit(solution)/shard_map/ppermute | solution.py:423
  27.6 2.6 %collective-permute-done.3.d2 = bf16[16,1152]{1,0:T(8,128)(2,1)S(1)} collective-permute-done((bf16[16,1152]{1,0:T(8,128)(2,1)S(1)}, bf16[16,1152]{1,0:T(8,128)(2,1)S(1)}, u32[]{:S(2)}, u32[]{:S(2)}) %collective-permute-start.3) | collective-permute-done | bytes 36896 | tf_op jit(solution)/shard_map/ppermute | solution.py:423
  30.2 0.0 collective-permute-done.2.d1
  30.2 0.0 all-to-all-done.queries_ref
  30.2 0.6 %shard_map.117.own_ref = f32[32,128]{1,0:T(8,128)S(1)} custom-call(bf16[16,1152]{1,0:T(8,128)(2,1)S(1)} %get-tuple-element.11.d0, bf16[16,1152]{1,0:T(8,128)(2,1)S(1)} %collective-permute-done.2.d1, bf16[16,1152]{1,0:T(8,128)(2,1)S(1)} %collective-permute-done.3.d2, bf16[16,1152]{1,0:T(8,128)(2,1)S(1)} %collective-permute-done.4.d3, ...), custom_call_target="tpu_custom_call" | custom-call | flops 17000000 | bytes 700000 | tf_op jit(solution)/shard_map/pallas_call | solution.py:197
  30.9 1.6 %collective-permute-start.5 = (f32[32,128]{1,0:T(8,128)S(1)}, f32[32,128]{1,0:T(8,128)S(1)}, u32[]{:S(2)}, u32[]{:S(2)}) collective-permute-start(f32[32,128]{1,0:T(8,128)S(1)} %shard_map.117.own_ref), channel_id=1, source_target_pairs={{0,1},{1,0},{2,3},{3,2},{4,5},{5,4},{6,7},{7,6},{8,9},{9,8},{10,11... | collective-permute-start | bytes 49160 | tf_op jit(solution)/shard_map/ppermute | solution.py:425
  32.5 0.0 copy-done.3
  32.5 0.1 copy.12.plan_ref
  32.6 0.5 shard_map.115.base_ref
  33.1 0.2 collective-permute-done.5.other_ref
  33.3 1.1 %shard_map.118 = bf16[1024,128]{1,0:T(8,128)(2,1)} custom-call(f32[1032,128]{1,0:T(8,128)S(1)} %shard_map.115.base_ref, f32[32,128]{1,0:T(8,128)S(1)} %shard_map.117.own_ref, f32[32,128]{1,0:T(8,128)S(1)} %collective-permute-done.5.other_ref, bf16[16,1152]{1,0:T(8,128)(2,1)S(1)} %get-tuple-element.11.d0, bf16[16,1152]{1,0:T(8,128)(2,1)S(1)} %collective-permute-done.2.d1, ...), custom_call_target="tpu_custom_call" | custom-call | flops 4000000 | bytes 900000 | tf_op jit(solution)/shard_map/pallas_call | solution.py:268
  34.4 11.7 %all-to-all-start.1 = ((bf16[128,8,128]{2,1,0:T(8,128)(2,1)}), bf16[128,8,128]{2,1,0:T(8,128)(2,1)S(1)}, u32[]{:S(2)}, u32[]{:S(2)}) async-start(bf16[128,8,128]{2,1,0:T(8,128)(2,1)} %bitcast), calls=%async_computation.1 | async-start | bytes 524288 | tf_op jit(solution)/shard_map/all_to_all | solution.py:426
  46.1 0.0 collective-permute-done.other_ref
  46.1 0.0 copy-done
  46.1 7.7 %shard_map.112 = (bf16[1024,2048]{1,0:T(8,128)(2,1)}, f32[8,128]{1,0:T(8,128)S(1)}) custom-call(bf16[1024,512]{1,0:T(8,128)(2,1)S(1)} %copy-done, bf16[1024,512]{1,0:T(8,128)(2,1)S(1)} %collective-permute-done.other_ref, bf16[1024,2048]{1,0:T(8,128)(2,1)} %weight_ref.1), custom_call_target="tpu_custom_call" | custom-call | flops 4300000256 | bytes 10500000 | tf_op jit(solution)/shard_map/pallas_call | solution.py:380
  53.7 1.0 %all-to-all-done.1 = bf16[128,8,128]{2,1,0:T(8,128)(2,1)S(1)} async-done(((bf16[128,8,128]{2,1,0:T(8,128)(2,1)}), bf16[128,8,128]{2,1,0:T(8,128)(2,1)S(1)}, u32[]{:S(2)}, u32[]{:S(2)}) %all-to-all-start.1) | async-done | bytes 262176 | tf_op jit(solution)/shard_map/all_to_all | solution.py:426
  54.7 0.1 shard_map.119
  54.9 2.1 %collective-permute-start.6 = (bf16[512,128]{1,0:T(8,128)(2,1)S(1)}, bf16[512,128]{1,0:T(8,128)(2,1)S(1)}, u32[]{:S(2)}, u32[]{:S(2)}) collective-permute-start(bf16[512,128]{1,0:T(8,128)(2,1)S(1)} %get-tuple-element.13.own_ref), channel_id=1, source_target_pairs={{0,1},{1,0},{2,3},{3,2},{4,5},{5,4},{6,7},{7,6},{8,9},{9,8},{10,11... | collective-permute-start | bytes 393224 | tf_op jit(solution)/shard_map/ppermute | solution.py:436
  57.0 1.0 %shard_map.121 = f32[8,256]{1,0:T(8,128)} custom-call(f32[512,128]{1,0:T(8,128)S(1)} %get-tuple-element.14.notes_ref), custom_call_target="tpu_custom_call" | custom-call | flops 2000000 | bytes 270000 | tf_op jit(solution)/shard_map/pallas_call | solution.py:331
  58.0 0.0 collective-permute-done.6.other_ref
  58.0 1.0 %shard_map.120 = bf16[640,128]{1,0:T(8,128)(2,1)} custom-call(bf16[512,128]{1,0:T(8,128)(2,1)S(1)} %get-tuple-element.13.own_ref, bf16[512,128]{1,0:T(8,128)(2,1)S(1)} %collective-permute-done.6.other_ref, f32[512,128]{1,0:T(8,128)S(1)} %get-tuple-element.14.notes_ref), custom_call_target="tpu_custom_call" | custom-call | flops 40000000 | bytes 700000 | tf_op jit(solution)/shard_map/pallas_call | solution.py:357
Async XLA Ops:
  0.6 21.4 %copy-start.2 = (s32[8]{0:T(128)S(1)}, s32[8]{0:T(128)}, u32[]{:S(2)}) copy-start(s32[8]{0:T(128)} %corpus_ref.1) | copy-start | bytes 100
  0.6 21.4 %copy-start.1 = (s32[8]{0:T(128)S(1)}, s32[8]{0:T(128)}, u32[]{:S(2)}) copy-start(s32[8]{0:T(128)} %lengths_ref.1) | copy-start | bytes 100
  2.2 30.3 %copy-start.3 = (s32[128,2]{0,1:T(2,128)S(1)}, s32[128,2]{0,1:T(2,128)}, u32[]{:S(2)}) copy-start(s32[128,2]{0,1:T(2,128)} %param.17) | copy-start | bytes 3076
  2.2 28.0 %all-to-all-start = ((bf16[32,4,2048]{2,1,0:T(4,128)(2,1)}), bf16[32,4,2048]{2,1,0:T(4,128)(2,1)S(1)}, u32[]{:S(2)}, u32[]{:S(2)}) async-start(bf16[32,4,2048]{2,1,0:T(4,128)(2,1)} %shard_map.116), calls=%async_computation | async-start | bytes 1048576 | tf_op jit(solution)/shard_map/all_to_all | solution.py:411
  14.9 31.2 %copy-start = (bf16[1024,512]{1,0:T(8,128)(2,1)S(1)}, bf16[1024,512]{1,0:T(8,128)(2,1)}, u32[]{:S(2)}) copy-start(bf16[1024,512]{1,0:T(8,128)(2,1)} %cot_ref.1) | copy-start | bytes 3145732
  14.9 31.2 %collective-permute-start = (bf16[1024,512]{1,0:T(8,128)(2,1)}, bf16[1024,512]{1,0:T(8,128)(2,1)S(1)}, u32[]{:S(2)}, u32[]{:S(2)}) collective-permute-start(bf16[1024,512]{1,0:T(8,128)(2,1)} %cot_ref.1), channel_id=1, source_target_pairs={{0,1},{1,0},{2,3},{3,2},{4,5},{5,4},{6,7},{7,6},{8,9},{9,8},{10,11... | collective-permute-start | bytes 3145736 | tf_op jit(solution)/shard_map/ppermute | solution.py:410
  20.4 1.6 %collective-permute-start.1 = (bf16[1024,128]{1,0:T(8,128)(2,1)S(1)}, bf16[1024,128]{1,0:T(8,128)(2,1)S(1)}, u32[]{:S(2)}, u32[]{:S(2)}) collective-permute-start(bf16[1024,128]{1,0:T(8,128)(2,1)S(1)} %shard_map.113.own_ref), channel_id=1, source_target_pairs={{0,1},{1,0},{2,3},{3,2},{4,5},{5,4},{6,7},{7,6},{8,9},{9,8},{10,11... | collective-permute-start | bytes 786440 | tf_op jit(solution)/shard_map/ppermute | solution.py:420
  23.2 4.4 %collective-permute-start.4 = (bf16[16,1152]{1,0:T(8,128)(2,1)S(1)}, bf16[16,1152]{1,0:T(8,128)(2,1)S(1)}, u32[]{:S(2)}, u32[]{:S(2)}) collective-permute-start(bf16[16,1152]{1,0:T(8,128)(2,1)S(1)} %get-tuple-element.11.d0), channel_id=1, source_target_pairs={{0,6},{2,4},{4,2},{6,0},{8,14},{10,12},{12,10},{14,8},{16,22},{18,... | collective-permute-start | bytes 110600 | tf_op jit(solution)/shard_map/ppermute | solution.py:423
  25.8 4.4 %collective-permute-start.3 = (bf16[16,1152]{1,0:T(8,128)(2,1)S(1)}, bf16[16,1152]{1,0:T(8,128)(2,1)S(1)}, u32[]{:S(2)}, u32[]{:S(2)}) collective-permute-start(bf16[16,1152]{1,0:T(8,128)(2,1)S(1)} %get-tuple-element.11.d0), channel_id=1, source_target_pairs={{0,4},{2,6},{4,0},{6,2},{8,12},{10,14},{12,8},{14,10},{16,20},{18,... | collective-permute-start | bytes 110600 | tf_op jit(solution)/shard_map/ppermute | solution.py:423
  26.3 3.9 %collective-permute-start.2 = (bf16[16,1152]{1,0:T(8,128)(2,1)S(1)}, bf16[16,1152]{1,0:T(8,128)(2,1)S(1)}, u32[]{:S(2)}, u32[]{:S(2)}) collective-permute-start(bf16[16,1152]{1,0:T(8,128)(2,1)S(1)} %get-tuple-element.11.d0), channel_id=1, source_target_pairs={{0,2},{2,0},{4,6},{6,4},{8,10},{10,8},{12,14},{14,12},{16,18},{18,... | collective-permute-start | bytes 110600 | tf_op jit(solution)/shard_map/ppermute | solution.py:423
  30.9 2.4 %collective-permute-start.5 = (f32[32,128]{1,0:T(8,128)S(1)}, f32[32,128]{1,0:T(8,128)S(1)}, u32[]{:S(2)}, u32[]{:S(2)}) collective-permute-start(f32[32,128]{1,0:T(8,128)S(1)} %shard_map.117.own_ref), channel_id=1, source_target_pairs={{0,1},{1,0},{2,3},{3,2},{4,5},{5,4},{6,7},{7,6},{8,9},{9,8},{10,11... | collective-permute-start | bytes 49160 | tf_op jit(solution)/shard_map/ppermute | solution.py:425
  34.4 20.4 %all-to-all-start.1 = ((bf16[128,8,128]{2,1,0:T(8,128)(2,1)}), bf16[128,8,128]{2,1,0:T(8,128)(2,1)S(1)}, u32[]{:S(2)}, u32[]{:S(2)}) async-start(bf16[128,8,128]{2,1,0:T(8,128)(2,1)} %bitcast), calls=%async_computation.1 | async-start | bytes 524288 | tf_op jit(solution)/shard_map/all_to_all | solution.py:426
  54.9 3.1 %collective-permute-start.6 = (bf16[512,128]{1,0:T(8,128)(2,1)S(1)}, bf16[512,128]{1,0:T(8,128)(2,1)S(1)}, u32[]{:S(2)}, u32[]{:S(2)}) collective-permute-start(bf16[512,128]{1,0:T(8,128)(2,1)S(1)} %get-tuple-element.13.own_ref), channel_id=1, source_target_pairs={{0,1},{1,0},{2,3},{3,2},{4,5},{5,4},{6,7},{7,6},{8,9},{9,8},{10,11... | collective-permute-start | bytes 393224 | tf_op jit(solution)/shard_map/ppermute | solution.py:436

commit v6 on v5

--- a/solution.py
+++ b/solution.py
@@ -104,7 +104,7 @@
                 copy.start()
         low = dot(acts[span, :], pin[...], NT)
         high = dot(cot[span, :], pout[...], NT)
-        out_ref[span, :] = jnp.concatenate([low, high], axis=1).astype(BF16)
+        out_ref[span, :] = jnp.concatenate([low, high], axis=1)
 
 
 def partial_features(acts, cotangent, proj_in, proj_out):
@@ -114,7 +114,7 @@
         partial_kernel,
         in_specs=[hbm] * 4,
         out_specs=pl.BlockSpec(memory_space=VMEM),
-        out_shape=VMEM((TOK, 2 * RANK), BF16),
+        out_shape=VMEM((TOK, 2 * RANK), F32),
         scratch_shapes=[
             VMEM(acts.shape, BF16),
             VMEM(cotangent.shape, BF16),

time: 59.4 us -> 59.8 us (level)
  transfers between devices with their start and end apart: 9 -> 9, of which waited for: 5 -> 5; matrix products, arithmetic and copies ran while one was open for 0% -> 0% of each run, Pallas kernels for 28% -> 27%
where the time goes in v6:
time: 59.8 us; the launch traced here: 59.3 us
  starting transfers between devices  33.2 us (56%)
  Pallas kernels  18.9 us (32%)
  waiting for transfers between devices  6.42 us (11%)
  between operations  0.74 us (1%)
    all_to_all x1, starting transfers between devices, body(): lax.all_to_all(copies(query_grads, members), 'dp', 0, 0, tiled=True, axis...  12.7 us
    all_to_all x1, starting transfers between devices, body(): lax.all_to_all(packed.reshape(DP, SLOT, LANES), 'dp', 0, 0, tiled=True, a...  11.7 us
    pallas_call x1, Pallas kernels, input_gradient(): pl.pallas_call(grad_kernel, grid=(weight.shape[1] // columns,), in_specs=...  7.66 us
    pallas_call x1, Pallas kernels, partial_features(): pl.pallas_call(partial_kernel, in_specs=[hbm] * 4, out_specs=pl.BlockSpec...  4.17 us
    ppermute x3, waiting for transfers between devices, body(): pieces.append(lax.ppermute(docs, 'dp', [(s, s ^ i) for s in range(DP)]))  3.54 us
    ppermute x3, starting transfers between devices, body(): pieces.append(lax.ppermute(docs, 'dp', [(s, s ^ i) for s in range(DP)]))  3.34 us
    ppermute x1, starting transfers between devices, body(): balanced = balance(rows, lax.ppermute(rows, 'mp', swap), notes)  2.14 us
    ppermute x1, starting transfers between devices, body(): lax.ppermute(mine, 'mp', swap)  1.7 us
  transfers between devices with their start and end apart: 9, of which 5 were waited for; matrix products, arithmetic and copies ran while one was open for 0% of the time, Pallas kernels for 27%

profile of v6, /device:TPU:1, one launch (start us, length us, event | category | flops | bytes accessed | tf_op | source)
XLA Modules:
  0.0 59.3 jit_solution(3662863205767743749)
XLA Ops:
  0.6 0.0 copy-start.2
  0.6 0.0 copy-start.1
  0.7 1.5 %shard_map.116 = bf16[32,4,2048]{2,1,0:T(4,128)(2,1)} custom-call(bf16[4,2048]{1,0:T(4,128)(2,1)} %source_ref.1), custom_call_target="tpu_custom_call" | custom-call | tf_op jit(solution)/shard_map/pallas_call | solution.py:60
  2.2 12.7 %all-to-all-start = ((bf16[32,4,2048]{2,1,0:T(4,128)(2,1)}), bf16[32,4,2048]{2,1,0:T(4,128)(2,1)S(1)}, u32[]{:S(2)}, u32[]{:S(2)}) async-start(bf16[32,4,2048]{2,1,0:T(4,128)(2,1)} %shard_map.116), calls=%async_computation | async-start | bytes 1048576 | tf_op jit(solution)/shard_map/all_to_all | solution.py:411
  14.9 0.0 copy-start.3
  14.9 0.0 copy-start
  14.9 1.3 %collective-permute-start = (bf16[1024,512]{1,0:T(8,128)(2,1)}, bf16[1024,512]{1,0:T(8,128)(2,1)S(1)}, u32[]{:S(2)}, u32[]{:S(2)}) collective-permute-start(bf16[1024,512]{1,0:T(8,128)(2,1)} %cot_ref.1), channel_id=1, source_target_pairs={{0,1},{1,0},{2,3},{3,2},{4,5},{5,4},{6,7},{7,6},{8,9},{9,8},{10,11... | collective-permute-start | bytes 3145736 | tf_op jit(solution)/shard_map/ppermute | solution.py:410
  16.2 4.2 %shard_map.113.own_ref = f32[1024,128]{1,0:T(8,128)S(1)} custom-call(bf16[1024,2048]{1,0:T(8,128)(2,1)} %acts_ref.1, bf16[1024,512]{1,0:T(8,128)(2,1)} %cot_ref.1, bf16[64,2048]{1,0:T(8,128)(2,1)} %pin_ref.1, bf16[64,1024]{1,0:T(8,128)(2,1)} %pout_ref.1), custom_call_target="tpu_custom_call" | custom-call | flops 340000000 | bytes 6000000 | tf_op jit(solution)/shard_map/pallas_call | solution.py:113
  20.4 0.3 collective-permute-start.1
  20.7 1.7 %collective-permute-done.1.other_ref = f32[1024,128]{1,0:T(8,128)S(1)} collective-permute-done((f32[1024,128]{1,0:T(8,128)S(1)}, f32[1024,128]{1,0:T(8,128)S(1)}, u32[]{:S(2)}, u32[]{:S(2)}) %collective-permute-start.1) | collective-permute-done | bytes 524320 | tf_op jit(solution)/shard_map/ppermute | solution.py:420
  22.4 0.0 copy-done.2
  22.4 0.0 copy-done.1
  22.4 1.2 %shard_map.114 = (bf16[1024,128]{1,0:T(8,128)(2,1)S(1)}, bf16[16,1152]{1,0:T(8,128)(2,1)S(1)}) custom-call(f32[1024,128]{1,0:T(8,128)S(1)} %shard_map.113.own_ref, f32[1024,128]{1,0:T(8,128)S(1)} %collective-permute-done.1.other_ref, s32[8]{0:T(128)S(1)} %copy-done.1, s32[8]{0:T(128)S(1)} %copy-done.2), custom_call_target="tpu_custom_call" | custom-call | flops 200000000 | bytes 1500000 | tf_op jit(solution)/shard_map/pallas_call | solution.py:170
  23.6 2.6 %collective-permute-start.4 = (bf16[16,1152]{1,0:T(8,128)(2,1)S(1)}, bf16[16,1152]{1,0:T(8,128)(2,1)S(1)}, u32[]{:S(2)}, u32[]{:S(2)}) collective-permute-start(bf16[16,1152]{1,0:T(8,128)(2,1)S(1)} %get-tuple-element.11.d0), channel_id=1, source_target_pairs={{0,6},{2,4},{4,2},{6,0},{8,14},{10,12},{12,10},{14,8},{16,22},{18,... | collective-permute-start | bytes 110600 | tf_op jit(solution)/shard_map/ppermute | solution.py:423
  26.2 0.5 collective-permute-start.3
  26.7 0.3 collective-permute-start.2
  26.9 1.1 %collective-permute-done.4.d3 = bf16[16,1152]{1,0:T(8,128)(2,1)S(1)} collective-permute-done((bf16[16,1152]{1,0:T(8,128)(2,1)S(1)}, bf16[16,1152]{1,0:T(8,128)(2,1)S(1)}, u32[]{:S(2)}, u32[]{:S(2)}) %collective-permute-start.4) | collective-permute-done | bytes 36896 | tf_op jit(solution)/shard_map/ppermute | solution.py:423
  28.0 2.5 %collective-permute-done.3.d2 = bf16[16,1152]{1,0:T(8,128)(2,1)S(1)} collective-permute-done((bf16[16,1152]{1,0:T(8,128)(2,1)S(1)}, bf16[16,1152]{1,0:T(8,128)(2,1)S(1)}, u32[]{:S(2)}, u32[]{:S(2)}) %collective-permute-start.3) | collective-permute-done | bytes 36896 | tf_op jit(solution)/shard_map/ppermute | solution.py:423
  30.5 0.0 collective-permute-done.2.d1
  30.5 0.0 all-to-all-done.queries_ref
  30.5 0.6 %shard_map.117.own_ref = f32[32,128]{1,0:T(8,128)S(1)} custom-call(bf16[16,1152]{1,0:T(8,128)(2,1)S(1)} %get-tuple-element.11.d0, bf16[16,1152]{1,0:T(8,128)(2,1)S(1)} %collective-permute-done.2.d1, bf16[16,1152]{1,0:T(8,128)(2,1)S(1)} %collective-permute-done.3.d2, bf16[16,1152]{1,0:T(8,128)(2,1)S(1)} %collective-permute-done.4.d3, ...), custom_call_target="tpu_custom_call" | custom-call | flops 17000000 | bytes 700000 | tf_op jit(solution)/shard_map/pallas_call | solution.py:197
  31.1 1.7 %collective-permute-start.5 = (f32[32,128]{1,0:T(8,128)S(1)}, f32[32,128]{1,0:T(8,128)S(1)}, u32[]{:S(2)}, u32[]{:S(2)}) collective-permute-start(f32[32,128]{1,0:T(8,128)S(1)} %shard_map.117.own_ref), channel_id=1, source_target_pairs={{0,1},{1,0},{2,3},{3,2},{4,5},{5,4},{6,7},{7,6},{8,9},{9,8},{10,11... | collective-permute-start | bytes 49160 | tf_op jit(solution)/shard_map/ppermute | solution.py:425
  32.8 0.0 copy-done.3
  32.8 0.1 copy.12.plan_ref
  32.9 0.5 shard_map.115.base_ref
  33.5 0.2 collective-permute-done.5.other_ref
  33.7 1.1 %shard_map.118 = bf16[1024,128]{1,0:T(8,128)(2,1)} custom-call(f32[1032,128]{1,0:T(8,128)S(1)} %shard_map.115.base_ref, f32[32,128]{1,0:T(8,128)S(1)} %shard_map.117.own_ref, f32[32,128]{1,0:T(8,128)S(1)} %collective-permute-done.5.other_ref, bf16[16,1152]{1,0:T(8,128)(2,1)S(1)} %get-tuple-element.11.d0, bf16[16,1152]{1,0:T(8,128)(2,1)S(1)} %collective-permute-done.2.d1, ...), custom_call_target="tpu_custom_call" | custom-call | flops 4000000 | bytes 900000 | tf_op jit(solution)/shard_map/pallas_call | solution.py:268
  34.8 11.7 %all-to-all-start.1 = ((bf16[128,8,128]{2,1,0:T(8,128)(2,1)}), bf16[128,8,128]{2,1,0:T(8,128)(2,1)S(1)}, u32[]{:S(2)}, u32[]{:S(2)}) async-start(bf16[128,8,128]{2,1,0:T(8,128)(2,1)} %bitcast), calls=%async_computation.1 | async-start | bytes 524288 | tf_op jit(solution)/shard_map/all_to_all | solution.py:426
  46.4 0.0 collective-permute-done.other_ref
  46.4 0.0 copy-done
  46.5 7.7 %shard_map.112 = (bf16[1024,2048]{1,0:T(8,128)(2,1)}, f32[8,128]{1,0:T(8,128)S(1)}) custom-call(bf16[1024,512]{1,0:T(8,128)(2,1)S(1)} %copy-done, bf16[1024,512]{1,0:T(8,128)(2,1)S(1)} %collective-permute-done.other_ref, bf16[1024,2048]{1,0:T(8,128)(2,1)} %weight_ref.1), custom_call_target="tpu_custom_call" | custom-call | flops 4300000256 | bytes 10500000 | tf_op jit(solution)/shard_map/pallas_call | solution.py:380
  54.1 1.0 %all-to-all-done.1 = bf16[128,8,128]{2,1,0:T(8,128)(2,1)S(1)} async-done(((bf16[128,8,128]{2,1,0:T(8,128)(2,1)}), bf16[128,8,128]{2,1,0:T(8,128)(2,1)S(1)}, u32[]{:S(2)}, u32[]{:S(2)}) %all-to-all-start.1) | async-done | bytes 262176 | tf_op jit(solution)/shard_map/all_to_all | solution.py:426
  55.1 0.1 shard_map.119
  55.3 2.1 %collective-permute-start.6 = (bf16[512,128]{1,0:T(8,128)(2,1)S(1)}, bf16[512,128]{1,0:T(8,128)(2,1)S(1)}, u32[]{:S(2)}, u32[]{:S(2)}) collective-permute-start(bf16[512,128]{1,0:T(8,128)(2,1)S(1)} %get-tuple-element.13.own_ref), channel_id=1, source_target_pairs={{0,1},{1,0},{2,3},{3,2},{4,5},{5,4},{6,7},{7,6},{8,9},{9,8},{10,11... | collective-permute-start | bytes 393224 | tf_op jit(solution)/shard_map/ppermute | solution.py:436
  57.4 1.0 %shard_map.121 = f32[8,256]{1,0:T(8,128)} custom-call(f32[512,128]{1,0:T(8,128)S(1)} %get-tuple-element.14.notes_ref), custom_call_target="tpu_custom_call" | custom-call | flops 2000000 | bytes 270000 | tf_op jit(solution)/shard_map/pallas_call | solution.py:331
  58.4 0.0 collective-permute-done.6.other_ref
  58.4 1.0 %shard_map.120 = bf16[640,128]{1,0:T(8,128)(2,1)} custom-call(bf16[512,128]{1,0:T(8,128)(2,1)S(1)} %get-tuple-element.13.own_ref, bf16[512,128]{1,0:T(8,128)(2,1)S(1)} %collective-permute-done.6.other_ref, f32[512,128]{1,0:T(8,128)S(1)} %get-tuple-element.14.notes_ref), custom_call_target="tpu_custom_call" | custom-call | flops 40000000 | bytes 700000 | tf_op jit(solution)/shard_map/pallas_call | solution.py:357
Async XLA Ops:
  0.6 21.8 %copy-start.2 = (s32[8]{0:T(128)S(1)}, s32[8]{0:T(128)}, u32[]{:S(2)}) copy-start(s32[8]{0:T(128)} %corpus_ref.1) | copy-start | bytes 100
  0.6 21.8 %copy-start.1 = (s32[8]{0:T(128)S(1)}, s32[8]{0:T(128)}, u32[]{:S(2)}) copy-start(s32[8]{0:T(128)} %lengths_ref.1) | copy-start | bytes 100
  2.2 28.3 %all-to-all-start = ((bf16[32,4,2048]{2,1,0:T(4,128)(2,1)}), bf16[32,4,2048]{2,1,0:T(4,128)(2,1)S(1)}, u32[]{:S(2)}, u32[]{:S(2)}) async-start(bf16[32,4,2048]{2,1,0:T(4,128)(2,1)} %shard_map.116), calls=%async_computation | async-start | bytes 1048576 | tf_op jit(solution)/shard_map/all_to_all | solution.py:411
  14.9 18.0 %copy-start.3 = (s32[128,2]{0,1:T(2,128)S(1)}, s32[128,2]{0,1:T(2,128)}, u32[]{:S(2)}) copy-start(s32[128,2]{0,1:T(2,128)} %param.17) | copy-start | bytes 3076
  14.9 31.6 %copy-start = (bf16[1024,512]{1,0:T(8,128)(2,1)S(1)}, bf16[1024,512]{1,0:T(8,128)(2,1)}, u32[]{:S(2)}) copy-start(bf16[1024,512]{1,0:T(8,128)(2,1)} %cot_ref.1) | copy-start | bytes 3145732
  14.9 31.6 %collective-permute-start = (bf16[1024,512]{1,0:T(8,128)(2,1)}, bf16[1024,512]{1,0:T(8,128)(2,1)S(1)}, u32[]{:S(2)}, u32[]{:S(2)}) collective-permute-start(bf16[1024,512]{1,0:T(8,128)(2,1)} %cot_ref.1), channel_id=1, source_target_pairs={{0,1},{1,0},{2,3},{3,2},{4,5},{5,4},{6,7},{7,6},{8,9},{9,8},{10,11... | collective-permute-start | bytes 3145736 | tf_op jit(solution)/shard_map/ppermute | solution.py:410
  20.4 2.0 %collective-permute-start.1 = (f32[1024,128]{1,0:T(8,128)S(1)}, f32[1024,128]{1,0:T(8,128)S(1)}, u32[]{:S(2)}, u32[]{:S(2)}) collective-permute-start(f32[1024,128]{1,0:T(8,128)S(1)} %shard_map.113.own_ref), channel_id=1, source_target_pairs={{0,1},{1,0},{2,3},{3,2},{4,5},{5,4},{6,7},{7,6},{8,9},{9,8},{10,11... | collective-permute-start | bytes 1572872 | tf_op jit(solution)/shard_map/ppermute | solution.py:420
  23.6 4.4 %collective-permute-start.4 = (bf16[16,1152]{1,0:T(8,128)(2,1)S(1)}, bf16[16,1152]{1,0:T(8,128)(2,1)S(1)}, u32[]{:S(2)}, u32[]{:S(2)}) collective-permute-start(bf16[16,1152]{1,0:T(8,128)(2,1)S(1)} %get-tuple-element.11.d0), channel_id=1, source_target_pairs={{0,6},{2,4},{4,2},{6,0},{8,14},{10,12},{12,10},{14,8},{16,22},{18,... | collective-permute-start | bytes 110600 | tf_op jit(solution)/shard_map/ppermute | solution.py:423
  26.2 4.3 %collective-permute-start.3 = (bf16[16,1152]{1,0:T(8,128)(2,1)S(1)}, bf16[16,1152]{1,0:T(8,128)(2,1)S(1)}, u32[]{:S(2)}, u32[]{:S(2)}) collective-permute-start(bf16[16,1152]{1,0:T(8,128)(2,1)S(1)} %get-tuple-element.11.d0), channel_id=1, source_target_pairs={{0,4},{2,6},{4,0},{6,2},{8,12},{10,14},{12,8},{14,10},{16,20},{18,... | collective-permute-start | bytes 110600 | tf_op jit(solution)/shard_map/ppermute | solution.py:423
  26.7 3.8 %collective-permute-start.2 = (bf16[16,1152]{1,0:T(8,128)(2,1)S(1)}, bf16[16,1152]{1,0:T(8,128)(2,1)S(1)}, u32[]{:S(2)}, u32[]{:S(2)}) collective-permute-start(bf16[16,1152]{1,0:T(8,128)(2,1)S(1)} %get-tuple-element.11.d0), channel_id=1, source_target_pairs={{0,2},{2,0},{4,6},{6,4},{8,10},{10,8},{12,14},{14,12},{16,18},{18,... | collective-permute-start | bytes 110600 | tf_op jit(solution)/shard_map/ppermute | solution.py:423
  31.1 2.5 %collective-permute-start.5 = (f32[32,128]{1,0:T(8,128)S(1)}, f32[32,128]{1,0:T(8,128)S(1)}, u32[]{:S(2)}, u32[]{:S(2)}) collective-permute-start(f32[32,128]{1,0:T(8,128)S(1)} %shard_map.117.own_ref), channel_id=1, source_target_pairs={{0,1},{1,0},{2,3},{3,2},{4,5},{5,4},{6,7},{7,6},{8,9},{9,8},{10,11... | collective-permute-start | bytes 49160 | tf_op jit(solution)/shard_map/ppermute | solution.py:425
  34.8 20.4 %all-to-all-start.1 = ((bf16[128,8,128]{2,1,0:T(8,128)(2,1)}), bf16[128,8,128]{2,1,0:T(8,128)(2,1)S(1)}, u32[]{:S(2)}, u32[]{:S(2)}) async-start(bf16[128,8,128]{2,1,0:T(8,128)(2,1)} %bitcast), calls=%async_computation.1 | async-start | bytes 524288 | tf_op jit(solution)/shard_map/all_to_all | solution.py:426
  55.3 3.1 %collective-permute-start.6 = (bf16[512,128]{1,0:T(8,128)(2,1)S(1)}, bf16[512,128]{1,0:T(8,128)(2,1)S(1)}, u32[]{:S(2)}, u32[]{:S(2)}) collective-permute-start(bf16[512,128]{1,0:T(8,128)(2,1)S(1)} %get-tuple-element.13.own_ref), channel_id=1, source_target_pairs={{0,1},{1,0},{2,3},{3,2},{4,5},{5,4},{6,7},{7,6},{8,9},{9,8},{10,11... | collective-permute-start | bytes 393224 | tf_op jit(solution)/shard_map/ppermute | solution.py:436
